TPU v7x, 32 devices: a whole 2x2x4 slice. The times are simulated.
32 devices in a mesh: dp: 4 (over x, core), expert: 8 (over z, y).
Axes of the slice: x: 2, y: 2, z: 4, core: 2. Of those that a mesh axis runs over, the one named last changes fastest.
Arguments:
- tokens: bfloat16 [4096, 2048], P(('dp', 'expert')), may hold values from -6 to 6
- routes: int32 [4096, 2], P(('dp', 'expert')), may hold values from 0 to 7, all different within a row; in each aligned block of 128 rows (0 to 127, 128 to 255, ...) at most 48 rows name the same one
- gates: float32 [4096, 2], P(('dp', 'expert')), may hold values from 0.25 to 1
- keep: int32 [4096], P(('dp', 'expert')), may hold values 0 or 1
- cotangent: bfloat16 [4096, 2048], P(('dp', 'expert')), may hold values from -6 to 6
- w_gate: bfloat16 [8, 2048, 768], P('expert'), may hold values from -0.125 to 0.125
- w_up: bfloat16 [8, 2048, 768], P('expert'), may hold values from -0.125 to 0.125
- w_down: bfloat16 [8, 768, 2048], P('expert'), may hold values from -0.21875 to 0.21875
Outputs:
- token_grads: bfloat16 [4096, 2048], P(('dp', 'expert'))
- expert_grads: float32 [8, 2048, 2304], P('expert', 'dp')
Inputs may be any that keep to these rules, and one draw needn't show every extreme that they name: `routes`: the 2 experts of a token differ. Among the 128 tokens of one device, no expert is named more than 48 times, a bound that some block reaches.
All inputs are finite; a program needn't handle non-finite values. No bound on the sum of `keep` on one device may be relied on, other than what follows from the above.
Results may differ from a plain program's by a relative error of at most 0.0061.
Values may be sent and summed in bfloat16 or wider, within the bound.
No kernel may reach another device: no remote copies, remote signals or barrier semaphores. Data moves between devices by JAX's collectives and lax.ppermute only.
A program may use at most 128 MiB of HBM per device.

v0:
```python
import jax
import jax.numpy as jnp
from jax import lax
from jax.sharding import PartitionSpec as P


def logistic_parts(act):
    sigma = jax.nn.sigmoid(act)
    return (act * sigma, sigma * (1.0 + act * (1.0 - sigma)))


def dot_rows(left, right):
    return lax.dot_general(
        left, right, (((0,), (0,)), ((), ())), preferred_element_type=jnp.float32
    )


def dot_back(left, weight):
    return lax.dot_general(
        left, weight, (((1,), (1,)), ((), ())), preferred_element_type=jnp.float32
    )


def on_device(tokens, routes, gates, keep, cotangent, w_gate, w_up, w_down):
    groups = lax.axis_size("expert")
    replicas = lax.axis_size("dp")
    tok_count, width = tokens.shape
    choose = routes.shape[1]
    capacity = 3 * tok_count * choose // (2 * groups)
    slots = groups * capacity
    weight_gate = w_gate[0]
    weight_up = w_up[0]
    weight_down = w_down[0]
    flat = routes.reshape(-1)
    expert_ids = lax.broadcasted_iota(jnp.int32, (tok_count * choose, groups), 1)
    onehot = (flat[:, None] == expert_ids).astype(jnp.int32)
    before = jnp.cumsum(onehot, axis=0) - onehot
    place = flat * capacity + jnp.sum(before * onehot, axis=1)
    repeated = jnp.repeat(tokens, choose, axis=0)
    outgoing = (
        jnp.zeros((slots, width), jnp.bfloat16)
        .at[place]
        .set(repeated)
        .reshape(groups, capacity, width)
    )
    received = lax.all_to_all(outgoing, "expert", split_axis=0, concat_axis=0, tiled=True)
    items = received.shape[1]
    rows = received.reshape(-1, width)
    gate_act = jnp.dot(rows, weight_gate, preferred_element_type=jnp.float32)
    up_act = jnp.dot(rows, weight_up, preferred_element_type=jnp.float32)
    silu_val, slope = logistic_parts(gate_act)
    hidden = (silu_val * up_act).astype(jnp.bfloat16)
    result = jnp.dot(hidden, weight_down, preferred_element_type=jnp.float32).astype(jnp.bfloat16)
    back = lax.all_to_all(
        result.reshape(groups, items, width), "expert", split_axis=0, concat_axis=0, tiled=True
    )
    returned, arrived, gate_act, up_act, hidden = (
        back,
        received,
        gate_act.reshape(groups, items, -1),
        up_act.reshape(groups, items, -1),
        hidden.reshape(groups, items, -1),
    )
    local_gate = jnp.dot(tokens, weight_gate, preferred_element_type=jnp.float32)
    local_up = jnp.dot(tokens, weight_up, preferred_element_type=jnp.float32)
    local_silu, local_slope = logistic_parts(local_gate)
    local_hidden = (local_silu * local_up).astype(jnp.bfloat16)
    keep_f = keep.astype(jnp.float32)[:, None]
    local_out = keep_f * jnp.dot(local_hidden, weight_down, preferred_element_type=jnp.float32)
    picked = (
        jnp.take(returned.reshape(slots, width), place, axis=0)
        .reshape(tok_count, choose, width)
        .astype(jnp.float32)
    )
    mixed = jnp.sum(gates[:, :, None] * picked, axis=1)
    difference = mixed - local_out
    upstream = cotangent.astype(jnp.float32) + difference
    routed_rows = (gates[:, :, None] * upstream[:, None, :]).astype(jnp.bfloat16).reshape(-1, width)
    local_cot = (-(keep_f * difference)).astype(jnp.bfloat16)
    routed_cot = (
        jnp.zeros((slots, width), jnp.bfloat16)
        .at[place]
        .set(routed_rows)
        .reshape(groups, capacity, width)
    )
    received = lax.all_to_all(routed_cot, "expert", split_axis=0, concat_axis=0, tiled=True)
    items = received.shape[1]
    grad_hidden = dot_back(received.reshape(-1, width), weight_down)
    arrived_cot, grad_hidden = (received, grad_hidden.reshape(groups, items, -1))
    rows_x = jnp.concatenate([arrived.reshape(slots, width), tokens], axis=0)
    rows_c = jnp.concatenate([arrived_cot.reshape(slots, width), local_cot], axis=0)
    gate_all = jnp.concatenate([gate_act.reshape(slots, -1), local_gate], axis=0)
    up_all = jnp.concatenate([up_act.reshape(slots, -1), local_up], axis=0)
    hidden_all = jnp.concatenate([hidden.reshape(slots, -1), local_hidden], axis=0)
    grad_all = jnp.concatenate(
        [grad_hidden.reshape(slots, -1), dot_back(local_cot, weight_down)], axis=0
    )
    silu_all, slope_all = logistic_parts(gate_all)
    gate_back = (grad_all * up_all * slope_all).astype(jnp.bfloat16)
    up_back = (grad_all * silu_all).astype(jnp.bfloat16)
    back_all = dot_back(gate_back, weight_gate) + dot_back(up_back, weight_up)
    routed_back = back_all[:slots].astype(jnp.bfloat16).reshape(groups, capacity, width)
    returned_back = lax.all_to_all(routed_back, "expert", split_axis=0, concat_axis=0, tiled=True)
    picked_back = (
        jnp.take(returned_back.reshape(slots, width), place, axis=0)
        .reshape(tok_count, choose, width)
        .astype(jnp.float32)
    )
    token_grads = (jnp.sum(picked_back, axis=1) + back_all[slots:]).astype(jnp.bfloat16)
    columns = (
        lax.all_to_all(rows_x, "dp", split_axis=1, concat_axis=0, tiled=True),
        lax.all_to_all(rows_c, "dp", split_axis=1, concat_axis=0, tiled=True),
    )
    input_rows = columns[0]
    cot_rows = columns[1]
    summed = jnp.concatenate(
        [
            dot_rows(input_rows, lax.all_gather(gate_back, "dp", axis=0, tiled=True)),
            dot_rows(input_rows, lax.all_gather(up_back, "dp", axis=0, tiled=True)),
            dot_rows(cot_rows, lax.all_gather(hidden_all, "dp", axis=0, tiled=True)),
        ],
        axis=1,
    )
    expert_grads = (summed * (1.0 / replicas))[None]
    return (token_grads, expert_grads)


def solution(mesh):
    return jax.shard_map(
        on_device,
        mesh=mesh,
        in_specs=(
            P(("dp", "expert"), None),
            P(("dp", "expert"), None),
            P(("dp", "expert"), None),
            P(("dp", "expert")),
            P(("dp", "expert"), None),
            P("expert", None, None),
            P("expert", None, None),
            P("expert", None, None),
        ),
        out_specs=(P(("dp", "expert"), None), P("expert", "dp", None)),
        check_vma=False,
    )
```

profile of v0, /device:TPU:0, one launch (start us, length us, event | category | flops | bytes accessed | tf_op | source)
XLA Modules:
  0.0 329.9 jit_solution(2170369642488602719)
XLA Ops:
  15.2 4.1 %scatter_custom_fusion = bf16[384,2048]{1,0:T(8,128)(2,1)} fusion(s32[256]{0:T(256)S(1)} %bitcast.92, bf16[256,2048]{1,0:T(8,128)(2,1)} %reshape.181, bf16[]{:T(256)} %constant.15.clone.1), kind=kCustom, calls=%fused_computation.55 | custom fusion | bytes 1573376 | tf_op jit(solution)/shard_map/scatter | solution.py:43
  19.3 44.5 %all_to_all.52 = bf16[8,48,2048]{2,1,0:T(8,128)(2,1)S(1)} all-to-all(bf16[8,48,2048]{2,1,0:T(8,128)(2,1)} %bitcast.88), channel_id=1, replica_groups=mesh['dp'=4,'expert'=8] {'expert'}, dimensions={0} | all-to-all | bytes 3145728 | tf_op jit(solution)/shard_map/all_to_all | solution.py:46
  70.3 4.4 %all-to-all-start.1 = ((bf16[8,48,2048]{2,1,0:T(8,128)(2,1)}), bf16[8,48,2048]{2,1,0:T(8,128)(2,1)}, u32[]{:S(2)}, u32[]{:S(2)}) async-start(bf16[8,48,2048]{2,1,0:T(8,128)(2,1)} %bitcast.90), calls=%async_computation.1 | async-start | bytes 3145728 | tf_op jit(solution)/shard_map/all_to_all | solution.py:54
  81.6 29.4 %all-to-all-done.1 = bf16[8,48,2048]{2,1,0:T(8,128)(2,1)} async-done(((bf16[8,48,2048]{2,1,0:T(8,128)(2,1)}), bf16[8,48,2048]{2,1,0:T(8,128)(2,1)}, u32[]{:S(2)}, u32[]{:S(2)}) %all-to-all-start.1) | async-done | bytes 1572896 | tf_op jit(solution)/shard_map/all_to_all | solution.py:54
  111.0 4.9 %gather_fusion = bf16[256,2048]{1,0:T(8,128)(2,1)} fusion(bf16[384,2048]{1,0:T(8,128)(2,1)} %bitcast.10, s32[1024]{0:T(1024)S(1)} %pad_clamp_fusion), kind=kCustom, calls=%fused_computation.clone | custom fusion | bytes 2098176 | tf_op jit(solution)/shard_map/jit(_take)/gather | solution.py:71
  122.1 5.0 %multiply_reduce_fusion = f32[128,2048]{1,0:T(8,128)S(1)} fusion(f32[128,2,2048]{2,1,0:T(2,128)} %reshape.159, f32[128,2]{1,0:T(8,128)} %copy-done.18), kind=kLoop, calls=%fused_computation.33 | loop fusion | flops 786432 | bytes 3146752 | tf_op jit(solution)/shard_map/reduce_sum | solution.py:75
  136.1 4.7 %scatter_custom_fusion.1 = bf16[384,2048]{1,0:T(8,128)(2,1)} fusion(s32[256]{0:T(256)S(1)} %bitcast.93, f32[256,2048]{1,0:T(8,128)} %mul.123, f32[256]{0:T(256)S(1)} %mul.110, bf16[]{:T(256)} %constant.15.clone.1), kind=kCustom, calls=%fused_computation.45 | custom fusion | flops 1048576 | bytes 3671042 | tf_op jit(solution)/shard_map/scatter | solution.py:83
  140.8 4.3 %all-to-all-start.2 = ((bf16[8,48,2048]{2,1,0:T(8,128)(2,1)}), bf16[8,48,2048]{2,1,0:T(8,128)(2,1)}, u32[]{:S(2)}, u32[]{:S(2)}) async-start(bf16[8,48,2048]{2,1,0:T(8,128)(2,1)} %bitcast.87), calls=%async_computation.2 | async-start | bytes 3145728 | tf_op jit(solution)/shard_map/all_to_all | solution.py:86
  145.2 4.0 %fusion = f32[128,768]{1,0:T(8,128)} fusion(bf16[128,2048]{1,0:T(8,128)(2,1)} %get-tuple-element.8, bf16[1,768,2048]{2,1,0:T(8,128)(2,1)} %param.17), kind=kOutput, calls=%fused_computation.6 | convolution fusion | flops 402653184 | bytes 4063232 | tf_op jit(solution)/shard_map/dot_general | solution.py:19
  149.2 32.5 %all-to-all-done.2 = bf16[8,48,2048]{2,1,0:T(8,128)(2,1)} async-done(((bf16[8,48,2048]{2,1,0:T(8,128)(2,1)}), bf16[8,48,2048]{2,1,0:T(8,128)(2,1)}, u32[]{:S(2)}, u32[]{:S(2)}) %all-to-all-start.2) | async-done | bytes 1572896 | tf_op jit(solution)/shard_map/all_to_all | solution.py:86
  181.7 3.9 %fusion.2 = f32[384,768]{1,0:T(8,128)S(1)} fusion(bf16[384,2048]{1,0:T(8,128)(2,1)} %bitcast.12, bf16[1,768,2048]{2,1,0:T(8,128)(2,1)} %param.17), kind=kOutput, calls=%fused_computation.8 | convolution fusion | flops 1207959552 | bytes 5898240 | tf_op jit(solution)/shard_map/dot_general | solution.py:19
  189.9 3.9 %concatenate.52 = bf16[384,4,512]{2,1,0:T(4,128)(2,1)} reshape(bf16[8,48,2048]{2,1,0:T(8,128)(2,1)} %all-to-all-done.2) | data formatting | bytes 3145728 | tf_op jit(solution)/shard_map/concatenate | solution.py:91
  198.6 4.4 %all-to-all-start.5 = ((bf16[512,4,512]{2,0,1:T(8,128)(2,1)}), bf16[512,4,512]{2,0,1:T(8,128)(2,1)}, u32[]{:S(2)}, u32[]{:S(2)}) async-start(bf16[512,4,512]{2,0,1:T(8,128)(2,1)} %copy.34), calls=%async_computation.5 | async-start | bytes 4194304 | tf_op jit(solution)/shard_map/all_to_all | solution.py:112
  203.0 5.0 %fusion.8 = f32[512,2048]{1,0:T(8,128)} fusion(bf16[512,768]{1,0:T(8,128)(2,1)} %get-tuple-element.6, bf16[1,2048,768]{2,1,0:T(8,128)(2,1)S(1)} %copy-done), kind=kOutput, calls=%fused_computation.14 | convolution fusion | flops 1610612736 | bytes 8126464 | tf_op jit(solution)/shard_map/dot_general | solution.py:19
  208.0 5.2 %fusion.20 = f32[512,2048]{1,0:T(8,128)S(1)} fusion(f32[512,2048]{1,0:T(8,128)} %fusion.8, bf16[512,768]{1,0:T(8,128)(2,1)} %get-tuple-element.5, bf16[1,2048,768]{2,1,0:T(8,128)(2,1)} %param.15), kind=kOutput, calls=%fused_computation.26 | convolution fusion | flops 1611661312 | bytes 12320768 | tf_op jit(solution)/shard_map/dot_general | solution.py:19
  216.7 19.7 %all-to-all-done.5 = bf16[512,4,512]{2,0,1:T(8,128)(2,1)} async-done(((bf16[512,4,512]{2,0,1:T(8,128)(2,1)}), bf16[512,4,512]{2,0,1:T(8,128)(2,1)}, u32[]{:S(2)}, u32[]{:S(2)}) %all-to-all-start.5) | async-done | bytes 2097184 | tf_op jit(solution)/shard_map/all_to_all | solution.py:112
  236.4 5.5 %all-to-all-start.3 = ((bf16[8,48,2048]{2,1,0:T(8,128)(2,1)}), bf16[8,48,2048]{2,1,0:T(8,128)(2,1)S(1)}, u32[]{:S(2)}, u32[]{:S(2)}) async-start(bf16[8,48,2048]{2,1,0:T(8,128)(2,1)} %bitcast.13), calls=%async_computation.3 | async-start | bytes 3145728 | tf_op jit(solution)/shard_map/all_to_all | solution.py:103
  254.1 24.9 %all-to-all-done.3 = bf16[8,48,2048]{2,1,0:T(8,128)(2,1)S(1)} async-done(((bf16[8,48,2048]{2,1,0:T(8,128)(2,1)}), bf16[8,48,2048]{2,1,0:T(8,128)(2,1)S(1)}, u32[]{:S(2)}, u32[]{:S(2)}) %all-to-all-start.3) | async-done | bytes 1572896 | tf_op jit(solution)/shard_map/all_to_all | solution.py:103
  279.0 4.7 %all-to-all-start.4 = ((bf16[512,4,512]{2,0,1:T(8,128)(2,1)}), bf16[512,4,512]{2,0,1:T(8,128)(2,1)}, u32[]{:S(2)}, u32[]{:S(2)}) async-start(bf16[512,4,512]{2,0,1:T(8,128)(2,1)} %copy.33), calls=%async_computation.4 | async-start | bytes 4194304 | tf_op jit(solution)/shard_map/all_to_all | solution.py:111
  283.7 5.5 %convolution_bitcast_fusion = f32[1,512,768]{2,1,0:T(8,128)} fusion(bf16[2048,512]{1,0:T(8,128)(2,1)} %bitcast.22, bf16[2048,768]{1,0:T(8,128)(2,1)} %all-gather.8.cloned.1.call-done), kind=kOutput, calls=%fused_computation.41 | convolution fusion | flops 1610612736 | bytes 6815744 | tf_op jit(solution)/shard_map/dot_general | solution.py:13
  293.1 4.1 %reduce_sum.32 = f32[128,2048]{1,0:T(8,128)S(1)} reduce(f32[128,2,2048]{2,1,0:T(2,128)} %reshape.160, f32[]{:T(128)} %constant.6.clone.1), dimensions={1}, to_apply=%region_6.8 | reduce | flops 262144 | bytes 3145732 | tf_op jit(solution)/shard_map/reduce_sum | solution.py:109
  299.4 10.1 %all-to-all-done.4 = bf16[512,4,512]{2,0,1:T(8,128)(2,1)} async-done(((bf16[512,4,512]{2,0,1:T(8,128)(2,1)}), bf16[512,4,512]{2,0,1:T(8,128)(2,1)}, u32[]{:S(2)}, u32[]{:S(2)}) %all-to-all-start.4) | async-done | bytes 2097184 | tf_op jit(solution)/shard_map/all_to_all | solution.py:111
  309.5 5.5 %convolution_bitcast_fusion.1 = f32[1,512,768]{2,1,0:T(8,128)} fusion(bf16[2048,512]{1,0:T(8,128)(2,1)} %bitcast.17, bf16[2048,768]{1,0:T(8,128)(2,1)} %all-gather.6.cloned.1.call-done), kind=kOutput, calls=%fused_computation.42 | convolution fusion | flops 1610612736 | bytes 6815744 | tf_op jit(solution)/shard_map/dot_general | solution.py:13
  315.0 4.5 %convolution_bitcast_fusion.2 = f32[1,512,768]{2,1,0:T(8,128)S(1)} fusion(bf16[2048,512]{1,0:T(8,128)(2,1)} %bitcast.17, bf16[2048,768]{1,0:T(8,128)(2,1)} %all-gather.4.cloned.1.call-done), kind=kOutput, calls=%fused_computation.43 | convolution fusion | flops 1610612736 | bytes 6815744 | tf_op jit(solution)/shard_map/dot_general | solution.py:13
  (101 shorter events, 70.5 us)
Async XLA Ops:
  7.2 58.1 %copy-start = (bf16[1,2048,768]{2,1,0:T(8,128)(2,1)S(1)}, bf16[1,2048,768]{2,1,0:T(8,128)(2,1)}, u32[]{:S(2)}) copy-start(bf16[1,2048,768]{2,1,0:T(8,128)(2,1)} %param.16) | copy-start | bytes 9437188
  19.3 44.6 %copy-start.7 = (bf16[1,2048,768]{2,1,0:T(8,128)(2,1)S(1)}, bf16[1,2048,768]{2,1,0:T(8,128)(2,1)}, u32[]{:S(2)}) copy-start(bf16[1,2048,768]{2,1,0:T(8,128)(2,1)} %param.15) | copy-start | bytes 9437188
  65.2 2.5 copy-start.12
  70.3 4.7 %copy-start.20 = (f32[128,2]{0,1:T(2,128)S(1)}, f32[128,2]{0,1:T(2,128)}, u32[]{:S(2)}) copy-start(f32[128,2]{0,1:T(2,128)} %param.12) | copy-start | bytes 3076
  70.3 4.8 %copy-start.22 = (s32[128]{0:T(128)S(1)}, s32[128]{0:T(128)}, u32[]{:S(2)}) copy-start(s32[128]{0:T(128)} %param.13) | copy-start | bytes 1540
  70.3 40.6 %all-to-all-start.1 = ((bf16[8,48,2048]{2,1,0:T(8,128)(2,1)}), bf16[8,48,2048]{2,1,0:T(8,128)(2,1)}, u32[]{:S(2)}, u32[]{:S(2)}) async-start(bf16[8,48,2048]{2,1,0:T(8,128)(2,1)} %bitcast.90), calls=%async_computation.1 | async-start | bytes 3145728 | tf_op jit(solution)/shard_map/all_to_all | solution.py:54
  74.8 209.0 %all-gather.8.cloned.1.call-start = ((), (), s32[]{:S(2)}) async-start(), calls=%async_computation.8 | async-start | bytes 3932160 | tf_op jit(solution)/shard_map/all_gather | solution.py:120
  75.8 2.7 copy-start.6
  122.1 5.0 %copy-start.3 = (bf16[1,768,2048]{2,1,0:T(8,128)(2,1)S(1)}, bf16[1,768,2048]{2,1,0:T(8,128)(2,1)}, u32[]{:S(2)}) copy-start(bf16[1,768,2048]{2,1,0:T(8,128)(2,1)} %param.17) | copy-start | bytes 9437188
  122.1 5.0 %copy-start.21 = (f32[128]{0:T(128)S(1)}, f32[128]{0:T(128)}, u32[]{:S(2)}) copy-start(f32[128]{0:T(128)} %convert_element_type.58) | copy-start | bytes 1540
  140.8 40.8 %all-to-all-start.2 = ((bf16[8,48,2048]{2,1,0:T(8,128)(2,1)}), bf16[8,48,2048]{2,1,0:T(8,128)(2,1)}, u32[]{:S(2)}, u32[]{:S(2)}) async-start(bf16[8,48,2048]{2,1,0:T(8,128)(2,1)} %bitcast.87), calls=%async_computation.2 | async-start | bytes 3145728 | tf_op jit(solution)/shard_map/all_to_all | solution.py:86
  145.1 164.3 %all-gather.6.cloned.1.call-start = ((), (), s32[]{:S(2)}) async-start(), calls=%async_computation.7 | async-start | bytes 3932160 | tf_op jit(solution)/shard_map/all_gather | solution.py:119
  181.7 4.0 %copy-start.11 = (f32[128,768]{1,0:T(8,128)S(1)}, f32[128,768]{1,0:T(8,128)}, u32[]{:S(2)}) copy-start(f32[128,768]{1,0:T(8,128)} %fusion) | copy-start | bytes 1179652
  181.7 4.0 %copy-start.13 = (f32[384,768]{1,0:T(8,128)S(1)}, f32[384,768]{1,0:T(8,128)}, u32[]{:S(2)}) copy-start(f32[384,768]{1,0:T(8,128)} %copy-done.12) | copy-start | bytes 3538948
  181.7 4.0 %copy-start.14 = (f32[384,768]{1,0:T(8,128)S(1)}, f32[384,768]{1,0:T(8,128)}, u32[]{:S(2)}) copy-start(f32[384,768]{1,0:T(8,128)} %get-tuple-element.10) | copy-start | bytes 3538948
  181.7 4.0 %copy-start.19 = (f32[128,768]{1,0:T(8,128)S(1)}, f32[128,768]{1,0:T(8,128)}, u32[]{:S(2)}) copy-start(f32[128,768]{1,0:T(8,128)} %get-tuple-element.12) | copy-start | bytes 1179652
  198.6 37.8 %all-to-all-start.5 = ((bf16[512,4,512]{2,0,1:T(8,128)(2,1)}), bf16[512,4,512]{2,0,1:T(8,128)(2,1)}, u32[]{:S(2)}, u32[]{:S(2)}) async-start(bf16[512,4,512]{2,0,1:T(8,128)(2,1)} %copy.34), calls=%async_computation.5 | async-start | bytes 4194304 | tf_op jit(solution)/shard_map/all_to_all | solution.py:112
  236.4 42.6 %all-to-all-start.3 = ((bf16[8,48,2048]{2,1,0:T(8,128)(2,1)}), bf16[8,48,2048]{2,1,0:T(8,128)(2,1)S(1)}, u32[]{:S(2)}, u32[]{:S(2)}) async-start(bf16[8,48,2048]{2,1,0:T(8,128)(2,1)} %bitcast.13), calls=%async_computation.3 | async-start | bytes 3145728 | tf_op jit(solution)/shard_map/all_to_all | solution.py:103
  241.9 5.0 %copy-start.5 = (bf16[8,48,2048]{2,1,0:T(8,128)(2,1)S(1)}, bf16[8,48,2048]{2,1,0:T(8,128)(2,1)}, u32[]{:S(2)}) copy-start(bf16[8,48,2048]{2,1,0:T(8,128)(2,1)} %copy-done.4) | copy-start | bytes 4718596
  241.9 73.0 %all-gather.4.cloned.1.call-start = ((), (), s32[]{:S(2)}) async-start(), calls=%async_computation.6 | async-start | bytes 3932160 | tf_op jit(solution)/shard_map/all_gather | solution.py:118
  279.0 30.4 %all-to-all-start.4 = ((bf16[512,4,512]{2,0,1:T(8,128)(2,1)}), bf16[512,4,512]{2,0,1:T(8,128)(2,1)}, u32[]{:S(2)}, u32[]{:S(2)}) async-start(bf16[512,4,512]{2,0,1:T(8,128)(2,1)} %copy.33), calls=%async_computation.4 | async-start | bytes 4194304 | tf_op jit(solution)/shard_map/all_to_all | solution.py:111
  315.0 4.5 %copy-start.9 = (f32[1,512,768]{2,1,0:T(8,128)S(1)}, f32[1,512,768]{2,1,0:T(8,128)}, u32[]{:S(2)}) copy-start(f32[1,512,768]{2,1,0:T(8,128)} %convolution_bitcast_fusion) | copy-start | bytes 4718596
  315.0 4.5 %copy-start.10 = (f32[1,512,768]{2,1,0:T(8,128)S(1)}, f32[1,512,768]{2,1,0:T(8,128)}, u32[]{:S(2)}) copy-start(f32[1,512,768]{2,1,0:T(8,128)} %convolution_bitcast_fusion.1) | copy-start | bytes 4718596
  319.5 3.4 %copy-start.1 = (bf16[1,2048,768]{2,1,0:T(8,128)(2,1)S(1)}, bf16[1,2048,768]{2,1,0:T(8,128)(2,1)}, u32[]{:S(2)}) copy-start(bf16[1,2048,768]{2,1,0:T(8,128)(2,1)} %param.16) | copy-start | bytes 9437188
  (7 other events, 11.9 us)
Sparse Core Ops, SparseCore 0:
  81.7 29.7 all-gather.7
  187.7 35.2 all-gather.5
  244.3 28.9 all-gather.3
where the time goes:
time: 337 us; the launch traced here: 330 us
  waiting for transfers between devices  117 us (35%)
  local copies, waits for them, and re-layouts  50.4 us (15%)
  matrix products  46.9 us (14%)
  blocking collectives  44.5 us (13%)
  other arithmetic  32.5 us (10%)
  starting transfers between devices  23.7 us (7%)
  between operations  14.5 us (4%)
    all_to_all x1, blocking collectives, on_device(): lax.all_to_all(outgoing, 'expert', split_axis=0, concat_axis=0, tiled=True)  44.5 us
    all_to_all x1, waiting for transfers between devices, on_device(): lax.all_to_all(routed_cot, 'expert', split_axis=0, concat_axis=0, tiled=T...  32.5 us
    all_to_all x1, waiting for transfers between devices, on_device(): lax.all_to_all(result.reshape(groups, items, width), 'expert', split_axis...  29.4 us
    all_to_all x1, waiting for transfers between devices, on_device(): lax.all_to_all(routed_back, 'expert', split_axis=0, concat_axis=0, tiled=...  24.9 us
    all_to_all x1, waiting for transfers between devices, on_device(): lax.all_to_all(rows_c, 'dp', split_axis=1, concat_axis=0, tiled=True)  19.7 us
    dot_general x4, matrix products, dot_back(): lax.dot_general(left, weight, (((1,), (1,)), ((), ())), preferred_element...  18.1 us
    dot_general x3, matrix products, dot_rows(): lax.dot_general(left, right, (((0,), (0,)), ((), ())), preferred_element_...  15.5 us
    all_to_all x1, waiting for transfers between devices, on_device(): lax.all_to_all(rows_x, 'dp', split_axis=1, concat_axis=0, tiled=True)  10.1 us
  transfers between devices with their start and end apart: 8, of which 5 were waited for; matrix products, arithmetic and copies ran while one was open for 30% of the time, Pallas kernels for 0%

commit v1 on v0

v1 whole, which is shorter than its diff:
```python
import jax
import jax.numpy as jnp
from jax import lax
from jax.sharding import PartitionSpec as P

F32 = jnp.float32
BF16 = jnp.bfloat16


def logistic_parts(act):
    sigma = jax.nn.sigmoid(act)
    return (act * sigma, sigma * (1.0 + act * (1.0 - sigma)))


def dot(left, right):
    return jnp.dot(left, right, preferred_element_type=F32)


def dot_rows(left, right):
    return lax.dot_general(left, right, (((0,), (0,)), ((), ())), preferred_element_type=F32)


def dot_back(left, weight):
    return lax.dot_general(left, weight, (((1,), (1,)), ((), ())), preferred_element_type=F32)


def halves(value):
    high = value.astype(BF16)
    return high, (value - high.astype(F32)).astype(BF16)


def on_device(tokens, routes, gates, keep, cotangent, w_gate, w_up, w_down):
    groups = lax.axis_size("expert")
    replicas = lax.axis_size("dp")
    tok_count, width = tokens.shape
    choose = routes.shape[1]
    capacity = 3 * tok_count * choose // (2 * groups)
    slots = groups * capacity
    cores = 2 if replicas % 2 == 0 else 1
    chips = replicas // cores
    part = width // replicas
    weight_gate, weight_up, weight_down = w_gate[0], w_up[0], w_down[0]

    def exchange(block):
        block = block.reshape(groups, capacity, -1)
        moved = lax.all_to_all(block, "expert", split_axis=0, concat_axis=0, tiled=True)
        return moved.reshape(slots, -1)

    expert_ids = lax.broadcasted_iota(jnp.int32, (tok_count, groups), 1)
    member = sum((routes[:, k : k + 1] == expert_ids).astype(BF16) for k in range(choose))
    lower = lax.broadcasted_iota(jnp.int32, (tok_count, tok_count), 0) > lax.broadcasted_iota(
        jnp.int32, (tok_count, tok_count), 1
    )
    before = dot(lower.astype(BF16), member).astype(jnp.int32)
    slot_ids = lax.broadcasted_iota(jnp.int32, (tok_count, slots), 1)
    hits = []
    for k in range(choose):
        chosen = routes[:, k : k + 1]
        slot = jnp.sum(jnp.where(chosen == expert_ids, before, 0), axis=1, keepdims=True)
        hits.append(slot_ids == chosen * capacity + slot)
    spread = sum(hit.astype(BF16) for hit in hits)
    gated = sum(jnp.where(hit, gates[:, k : k + 1], 0.0) for k, hit in enumerate(hits))
    slot_gate = jnp.sum(gated, axis=0)[:, None]
    gated_high, gated_low = halves(gated)

    rows = exchange(dot_rows(spread, tokens).astype(BF16))

    keep_f = keep.astype(F32)[:, None]
    local_gate = dot(tokens, weight_gate)
    local_up = dot(tokens, weight_up)
    local_silu, local_slope = logistic_parts(local_gate)
    local_hidden = (local_silu * local_up).astype(BF16)
    local_out = keep_f * dot(local_hidden, weight_down)

    gate_act = dot(rows, weight_gate)
    up_act = dot(rows, weight_up)
    silu, slope = logistic_parts(gate_act)
    hidden = (silu * up_act).astype(BF16)
    returned = exchange(dot(hidden, weight_down).astype(BF16))

    mixed = dot(gated_high, returned) + dot(gated_low, returned)
    difference = mixed - local_out
    upstream = cotangent.astype(F32) + difference
    local_cot = (-(keep_f * difference)).astype(BF16)
    up_high, up_low = halves(upstream)
    routed_cot = (slot_gate * (dot_rows(spread, up_high) + dot_rows(spread, up_low))).astype(BF16)
    cots = exchange(routed_cot)

    grad_hidden = dot_back(cots, weight_down)
    gate_back = (grad_hidden * (up_act * slope)).astype(BF16)
    up_back = (grad_hidden * silu).astype(BF16)
    back = dot_back(gate_back, weight_gate) + dot_back(up_back, weight_up)
    returned_back = exchange(back.astype(BF16))

    local_grad = dot_back(local_cot, weight_down)
    local_gate_back = (local_grad * (local_up * local_slope)).astype(BF16)
    local_up_back = (local_grad * local_silu).astype(BF16)
    local_back = dot_back(local_gate_back, weight_gate) + dot_back(local_up_back, weight_up)
    token_grads = (dot(spread, returned_back) + local_back).astype(BF16)

    core = lax.axis_index("dp") % cores
    chip = lax.axis_index("dp") // cores

    def with_sibling(*arrays):
        if cores == 1:
            return [arrays]
        pairs = [(i, i ^ 1) for i in range(replicas)]
        return [arrays, tuple(lax.ppermute(a, "dp", pairs) for a in arrays)]

    x_all = with_sibling(jnp.concatenate([rows, tokens], axis=0))
    h_all = with_sibling(jnp.concatenate([hidden, local_hidden], axis=0))
    c_all = with_sibling(jnp.concatenate([cots, local_cot], axis=0))
    g_all = with_sibling(
        jnp.concatenate([gate_back, local_gate_back], axis=0),
        jnp.concatenate([up_back, local_up_back], axis=0),
    )

    def columns(array, target):
        return lax.dynamic_slice_in_dim(array, (target * cores + core) * part, part, axis=1)

    def sums(target):
        total_gate = total_up = total_down = 0.0
        for (x,), (h,), (c,), (gate, up) in zip(x_all, h_all, c_all, g_all):
            x_part, c_part = columns(x, target), columns(c, target)
            total_gate += dot_rows(x_part, gate)
            total_up += dot_rows(x_part, up)
            total_down += dot_rows(c_part, h)
        return total_gate, total_up, total_down

    received = []
    for shift in range(1, chips):
        moves = [
            (chip_from * cores + i, (chip_from + shift) % chips * cores + i)
            for chip_from in range(chips)
            for i in range(cores)
        ]
        sent = [value.astype(BF16) for value in sums((chip + shift) % chips)]
        received.append([lax.ppermute(value, "dp", moves) for value in sent])
    totals = list(sums(chip))
    for arrays in received:
        totals = [total + value.astype(F32) for total, value in zip(totals, arrays)]
    expert_grads = (jnp.concatenate(totals, axis=1) * (1.0 / replicas))[None]
    return (token_grads, expert_grads)


def solution(mesh):
    return jax.shard_map(
        on_device,
        mesh=mesh,
        in_specs=(
            P(("dp", "expert"), None),
            P(("dp", "expert"), None),
            P(("dp", "expert"), None),
            P(("dp", "expert")),
            P(("dp", "expert"), None),
            P("expert", None, None),
            P("expert", None, None),
            P("expert", None, None),
        ),
        out_specs=(P(("dp", "expert"), None), P("expert", "dp", None)),
        check_vma=False,
    )
```

time: 337 us -> 237 us (0.70); the launches traced: 330 us -> 236 us
  local copies, waits for them, and re-layouts: 50.4 us -> 6.72 us
  waiting for transfers between devices: 117 us -> 95.7 us
  other arithmetic: 32.5 us -> 14.6 us
  between operations: 14.5 us -> 1.19 us
  matrix products: 46.9 us -> 54.9 us
  starting transfers between devices: 23.7 us -> 18.3 us
    all_to_all x5 -> x3, waiting for transfers between devices: 117 us -> 58.1 us  [exchange(): lax.all_to_all(block, 'expert', split_axis=0, concat_axis=0, tiled=True)]
    ppermute x0 -> x8, waiting for transfers between devices: none -> 37.6 us  [the longest x3 37.6 us: on_device(): received.append([lax.ppermute(value, 'dp', moves) for value in sent])]
    concatenate x6 -> x0, local copies, waits for them, and re-layouts: 14.3 us -> none  [the longest x3 7.92 us: on_device(): jnp.concatenate([arrived_cot.reshape(slots, width), local_cot], axis=0)]
    all_to_all x5 -> x3, starting transfers between devices: 23.4 us -> 13.6 us  [exchange(): lax.all_to_all(block, 'expert', split_axis=0, concat_axis=0, tiled=True)]
    reduce_sum x3 -> x1, other arithmetic: 9.19 us -> 0.15 us  [on_device(): slot_gate = jnp.sum(gated, axis=0)[:, None]]
    dot_general x3 -> x15, matrix products: 15.5 us -> 23.4 us  [dot_rows(): lax.dot_general(left, right, (((0,), (0,)), ((), ())), preferred_element_...]
    convert_element_type x6 -> x1, other arithmetic: 7.58 us -> 0.01 us  [on_device(): keep_f = keep.astype(F32)[:, None]]
    mul x5 -> x0, local copies, waits for them, and re-layouts: 6.59 us -> none  [the longest x3 6.33 us: on_device(): gates[:, :, None] * upstream[:, None, :]]
  transfers between devices with their start and end apart: 8 -> 11, of which waited for: 5 -> 5; matrix products, arithmetic and copies ran while one was open for 30% -> 21% of each run, Pallas kernels for 0% -> 0%
where the time goes in v1:
time: 237 us; the launch traced here: 236 us
  waiting for transfers between devices  95.7 us (40%)
  matrix products  54.9 us (23%)
  blocking collectives  44.3 us (19%)
  starting transfers between devices  18.3 us (8%)
  other arithmetic  14.6 us (6%)
  local copies, waits for them, and re-layouts  6.72 us (3%)
    all_to_all x3, waiting for transfers between devices, exchange(): lax.all_to_all(block, 'expert', split_axis=0, concat_axis=0, tiled=True)  58.1 us
    all_to_all x1, blocking collectives, exchange(): lax.all_to_all(block, 'expert', split_axis=0, concat_axis=0, tiled=True)  44.3 us
    ppermute x3, waiting for transfers between devices, on_device(): received.append([lax.ppermute(value, 'dp', moves) for value in sent])  37.6 us
    dot_general x15, matrix products, dot_rows(): lax.dot_general(left, right, (((0,), (0,)), ((), ())), preferred_element_...  23.4 us
    dot_general x10, matrix products, dot(): return jnp.dot(left, right, preferred_element_type=F32)  18.1 us
    all_to_all x3, starting transfers between devices, exchange(): lax.all_to_all(block, 'expert', split_axis=0, concat_axis=0, tiled=True)  13.6 us
    dot_general x6, matrix products, dot_back(): lax.dot_general(left, weight, (((1,), (1,)), ((), ())), preferred_element...  13.4 us
    unnamed x72, local copies, waits for them, and re-layouts  5.87 us
  transfers between devices with their start and end apart: 11, of which 5 were waited for; matrix products, arithmetic and copies ran while one was open for 21% of the time, Pallas kernels for 0%

profile of v1, /device:TPU:0, one launch (start us, length us, event | category | flops | bytes accessed | tf_op | source)
XLA Modules:
  0.0 235.8 jit_solution(17491507072558712153)
XLA Ops:
  4.2 44.3 %all_to_all.20 = bf16[8,48,2048]{2,1,0:T(8,128)(2,1)S(1)} all-to-all(bf16[8,48,2048]{2,1,0:T(8,128)(2,1)S(1)} %bitcast.115), channel_id=1, replica_groups=mesh['dp'=4,'expert'=8] {'expert'}, dimensions={0} | all-to-all | bytes 3145728 | tf_op jit(solution)/shard_map/all_to_all | solution.py:46
  51.0 2.5 %multiply_convert_fusion.3 = (bf16[384,768]{1,0:T(8,128)(2,1)S(1)}, f32[384,768]{1,0:T(8,128)}) fusion(f32[384,768]{1,0:T(8,128)S(1)} %fusion.22, bf16[384,2048]{1,0:T(8,128)(2,1)S(1)} %bitcast.108, bf16[1,2048,768]{2,1,0:T(8,128)(2,1)S(1)} %copy-done.25), kind=kOutput, calls=%fused_computation.53 | convolution fusion | flops 1209729024 | bytes 7667712 | tf_op jit(solution)/shard_map/dot_general | solution.py:16
  53.5 2.6 %fusion.26 = bf16[384,2048]{1,0:T(8,128)(2,1)} fusion(bf16[384,768]{1,0:T(8,128)(2,1)S(1)} %get-tuple-element.14, bf16[1,768,2048]{2,1,0:T(8,128)(2,1)S(1)} %copy-done), kind=kOutput, calls=%fused_computation.33 | convolution fusion | flops 1208745984 | bytes 5308416 | tf_op jit(solution)/shard_map/dot_general | solution.py:16
  56.1 4.5 %all-to-all-start.1 = ((bf16[8,48,2048]{2,1,0:T(8,128)(2,1)}), bf16[8,48,2048]{2,1,0:T(8,128)(2,1)}, u32[]{:S(2)}, u32[]{:S(2)}) async-start(bf16[8,48,2048]{2,1,0:T(8,128)(2,1)} %bitcast.117), calls=%async_computation.1 | async-start | bytes 3145728 | tf_op jit(solution)/shard_map/all_to_all | solution.py:46
  60.7 2.8 %fusion.20 = f32[128,768]{1,0:T(8,128)S(1)} fusion(bf16[128,2048]{1,0:T(8,128)(2,1)} %param.8, bf16[1,2048,768]{2,1,0:T(8,128)(2,1)} %param.13), kind=kOutput, calls=%fused_computation.27 | convolution fusion | flops 402653184 | bytes 4063232 | tf_op jit(solution)/shard_map/dot_general | solution.py:16
  65.7 31.1 %all-to-all-done.1 = bf16[8,48,2048]{2,1,0:T(8,128)(2,1)} async-done(((bf16[8,48,2048]{2,1,0:T(8,128)(2,1)}), bf16[8,48,2048]{2,1,0:T(8,128)(2,1)}, u32[]{:S(2)}, u32[]{:S(2)}) %all-to-all-start.1) | async-done | bytes 1572896 | tf_op jit(solution)/shard_map/all_to_all | solution.py:46
  98.7 1.9 convolution_add_fusion
  104.6 4.5 %all-to-all-start.2 = ((bf16[8,48,2048]{2,1,0:T(8,128)(2,1)}), bf16[8,48,2048]{2,1,0:T(8,128)(2,1)}, u32[]{:S(2)}, u32[]{:S(2)}) async-start(bf16[8,48,2048]{2,1,0:T(8,128)(2,1)} %bitcast.114), calls=%async_computation.2 | async-start | bytes 3145728 | tf_op jit(solution)/shard_map/all_to_all | solution.py:46
  109.2 2.1 pad_maximum_fusion.4
  111.3 2.7 %pad_maximum_fusion = bf16[512,2048]{1,0:T(8,128)(2,1)} fusion(bf16[128,2048]{1,0:T(8,128)(2,1)} %param.8, bf16[384,2048]{1,0:T(8,128)(2,1)S(1)} %bitcast.109), kind=kLoop, calls=%fused_computation.3 | loop fusion | flops 4194304 | bytes 4194304 | tf_op jit(solution)/shard_map/concatenate | solution.py:110
  116.4 2.2 fusion.8
  118.6 27.0 %all-to-all-done.2 = bf16[8,48,2048]{2,1,0:T(8,128)(2,1)} async-done(((bf16[8,48,2048]{2,1,0:T(8,128)(2,1)}), bf16[8,48,2048]{2,1,0:T(8,128)(2,1)}, u32[]{:S(2)}, u32[]{:S(2)}) %all-to-all-start.2) | async-done | bytes 1572896 | tf_op jit(solution)/shard_map/all_to_all | solution.py:46
  145.6 4.0 %multiply_convert_fusion.2 = (bf16[384,768]{1,0:T(8,128)(2,1)S(1)}, bf16[384,768]{1,0:T(8,128)(2,1)S(1)}) fusion(f32[384,768]{1,0:T(8,128)} %get-tuple-element.15, f32[384,768]{1,0:T(8,128)} %copy-done.35, bf16[384,2048]{1,0:T(8,128)(2,1)} %bitcast.16, bf16[1,768,2048]{2,1,0:T(8,128)(2,1)S(1)} %copy-done), kind=kOutput, calls=%fused_computation.52 | convolution fusion | flops 1211793408 | bytes 8257536 | tf_op jit(solution)/shard_map/dot_general | solution.py:24
  151.9 2.6 %add_convert_fusion = bf16[384,2048]{1,0:T(8,128)(2,1)} fusion(f32[384,2048]{1,0:T(8,128)S(1)} %fusion.10, bf16[384,768]{1,0:T(8,128)(2,1)S(1)} %get-tuple-element.4, bf16[1,2048,768]{2,1,0:T(8,128)(2,1)S(1)} %copy-done.8), kind=kOutput, calls=%fused_computation.31 | convolution fusion | flops 1209532416 | bytes 8454144 | tf_op jit(solution)/shard_map/dot_general | solution.py:24
  154.5 4.7 %all-to-all-start.3 = ((bf16[8,48,2048]{2,1,0:T(8,128)(2,1)}), bf16[8,48,2048]{2,1,0:T(8,128)(2,1)}, u32[]{:S(2)}, u32[]{:S(2)}) async-start(bf16[8,48,2048]{2,1,0:T(8,128)(2,1)} %bitcast.116), calls=%async_computation.3 | async-start | bytes 3145728 | tf_op jit(solution)/shard_map/all_to_all | solution.py:46
  165.7 2.8 %fusion.49 = f32[512,768]{1,0:T(8,128)} fusion(s32[]{:T(128)S(6)} %select_n.47, bf16[384,2048]{1,0:T(8,128)(2,1)} %bitcast.16, bf16[128,2048]{1,0:T(8,128)(2,1)S(1)} %copy-done.11, bf16[128,768]{1,0:T(8,128)(2,1)S(1)} %get-tuple-element.16, bf16[384,768]{1,0:T(8,128)(2,1)S(1)} %copy-done.17), kind=kOutput, calls=%fused_computation.66 | convolution fusion | flops 405274624 | bytes 4456452 | tf_op jit(solution)/shard_map/dot_general | solution.py:20
  179.1 13.4 %collective-permute-done.4 = bf16[512,768]{1,0:T(8,128)(2,1)S(1)} collective-permute-done((bf16[512,768]{1,0:T(8,128)(2,1)S(1)}, bf16[512,768]{1,0:T(8,128)(2,1)S(1)}, u32[]{:S(2)}, u32[]{:S(2)}) %collective-permute-start.4) | collective-permute-done | bytes 786464 | tf_op jit(solution)/shard_map/ppermute | solution.py:138
  194.0 14.1 %collective-permute-done.2 = bf16[512,768]{1,0:T(8,128)(2,1)S(1)} collective-permute-done((bf16[512,768]{1,0:T(8,128)(2,1)S(1)}, bf16[512,768]{1,0:T(8,128)(2,1)S(1)}, u32[]{:S(2)}, u32[]{:S(2)}) %collective-permute-start.2) | collective-permute-done | bytes 786464 | tf_op jit(solution)/shard_map/ppermute | solution.py:138
  209.6 2.6 %add_convert_fusion.1 = bf16[512,768]{1,0:T(8,128)(2,1)} fusion(f32[512,768]{1,0:T(8,128)S(1)} %fusion.52, bf16[512,768]{1,0:T(8,128)(2,1)} %collective-permute-done.6, bf16[512,2048]{1,0:T(8,128)(2,1)S(1)} %collective-permute-done.5, s32[]{:T(128)S(6)} %select_n.49), kind=kOutput, calls=%fused_computation.46 | convolution fusion | flops 403439616 | bytes 3670020 | tf_op jit(solution)/shard_map/dot_general | solution.py:20
  213.8 3.1 %fusion.57 = f32[512,768]{1,0:T(8,128)} fusion(bf16[512,768]{1,0:T(8,128)(2,1)} %collective-permute-done.6, bf16[512,2048]{1,0:T(8,128)(2,1)S(1)} %collective-permute-done.5, s32[]{:T(128)S(6)} %select_n.47), kind=kOutput, calls=%fused_computation.72 | convolution fusion | flops 402653184 | bytes 2883588 | tf_op jit(solution)/shard_map/dot_general | solution.py:20
  216.8 2.0 fusion.71
  218.9 2.0 fusion.41
  220.8 10.1 %collective-permute-done.7 = bf16[512,768]{1,0:T(8,128)(2,1)} collective-permute-done((bf16[512,768]{1,0:T(8,128)(2,1)}, bf16[512,768]{1,0:T(8,128)(2,1)}, u32[]{:S(2)}, u32[]{:S(2)}) %collective-permute-start.7) | collective-permute-done | bytes 786464 | tf_op jit(solution)/shard_map/ppermute | solution.py:138
  232.3 2.6 %maximum_multiply_fusion = f32[1,512,2304]{2,1,0:T(8,128)} fusion(f32[1,512,768]{2,1,0:T(8,128)S(1)} %add_bitcast_fusion, f32[1,512,768]{2,1,0:T(8,128)S(1)} %copy-done.12, f32[1,512,768]{2,1,0:T(8,128)S(1)} %copy-done.13), kind=kLoop, calls=%fused_computation | loop fusion | flops 3538944 | bytes 9437184 | tf_op jit(solution)/shard_map/mul | solution.py:142
  (116 shorter events, 42.5 us)
Async XLA Ops:
  0.6 52.9 %copy-start = (bf16[1,768,2048]{2,1,0:T(8,128)(2,1)S(1)}, bf16[1,768,2048]{2,1,0:T(8,128)(2,1)}, u32[]{:S(2)}) copy-start(bf16[1,768,2048]{2,1,0:T(8,128)(2,1)} %param.15) | copy-start | bytes 9437188
  4.2 44.4 %copy-start.7 = (bf16[1,2048,768]{2,1,0:T(8,128)(2,1)S(1)}, bf16[1,2048,768]{2,1,0:T(8,128)(2,1)}, u32[]{:S(2)}) copy-start(bf16[1,2048,768]{2,1,0:T(8,128)(2,1)} %param.13) | copy-start | bytes 9437188
  56.1 4.5 %copy-start.33 = (s32[128]{0:T(128)S(1)}, s32[128]{0:T(128)}, u32[]{:S(2)}) copy-start(s32[128]{0:T(128)} %param.11) | copy-start | bytes 1540
  56.1 4.5 %copy-start.32 = (f32[128,2]{0,1:T(2,128)S(1)}, f32[128,2]{0,1:T(2,128)}, u32[]{:S(2)}) copy-start(f32[128,2]{0,1:T(2,128)} %param.10) | copy-start | bytes 3076
  56.1 40.7 %all-to-all-start.1 = ((bf16[8,48,2048]{2,1,0:T(8,128)(2,1)}), bf16[8,48,2048]{2,1,0:T(8,128)(2,1)}, u32[]{:S(2)}, u32[]{:S(2)}) async-start(bf16[8,48,2048]{2,1,0:T(8,128)(2,1)} %bitcast.117), calls=%async_computation.1 | async-start | bytes 3145728 | tf_op jit(solution)/shard_map/all_to_all | solution.py:46
  60.7 3.6 %copy-start.5 = (bf16[128,2048]{1,0:T(8,128)(2,1)S(1)}, bf16[128,2048]{1,0:T(8,128)(2,1)}, u32[]{:S(2)}) copy-start(bf16[128,2048]{1,0:T(8,128)(2,1)} %param.8) | copy-start | bytes 1572868
  60.7 3.6 %copy-start.26 = (bf16[1,2048,768]{2,1,0:T(8,128)(2,1)S(1)}, bf16[1,2048,768]{2,1,0:T(8,128)(2,1)}, u32[]{:S(2)}) copy-start(bf16[1,2048,768]{2,1,0:T(8,128)(2,1)} %param.14) | copy-start | bytes 9437188
  104.6 40.9 %all-to-all-start.2 = ((bf16[8,48,2048]{2,1,0:T(8,128)(2,1)}), bf16[8,48,2048]{2,1,0:T(8,128)(2,1)}, u32[]{:S(2)}, u32[]{:S(2)}) async-start(bf16[8,48,2048]{2,1,0:T(8,128)(2,1)} %bitcast.114), calls=%async_computation.2 | async-start | bytes 3145728 | tf_op jit(solution)/shard_map/all_to_all | solution.py:46
  111.3 98.3 %collective-permute-start.6 = (bf16[512,768]{1,0:T(8,128)(2,1)}, bf16[512,768]{1,0:T(8,128)(2,1)}, u32[]{:S(2)}, u32[]{:S(2)}) collective-permute-start(bf16[512,768]{1,0:T(8,128)(2,1)} %pad_maximum_fusion.4), channel_id=1, source_target_pairs={{0,8},{8,0},{16,24},{24,16},{1,9},{9,1},{17,25},{25,17},{2,10},{10... | collective-permute-start | bytes 2359304 | tf_op jit(solution)/shard_map/ppermute | solution.py:108
  114.0 56.3 %collective-permute-start = (bf16[512,2048]{1,0:T(8,128)(2,1)}, bf16[512,2048]{1,0:T(8,128)(2,1)}, u32[]{:S(2)}, u32[]{:S(2)}) collective-permute-start(bf16[512,2048]{1,0:T(8,128)(2,1)} %pad_maximum_fusion), channel_id=1, source_target_pairs={{0,8},{8,0},{16,24},{24,16},{1,9},{9,1},{17,25},{25,17},{2,10},{10... | collective-permute-start | bytes 6291464 | tf_op jit(solution)/shard_map/ppermute | solution.py:108
  145.6 4.0 %copy-start.28 = (bf16[1,2048,768]{2,1,0:T(8,128)(2,1)S(1)}, bf16[1,2048,768]{2,1,0:T(8,128)(2,1)}, u32[]{:S(2)}) copy-start(bf16[1,2048,768]{2,1,0:T(8,128)(2,1)} %param.14) | copy-start | bytes 9437188
  154.5 4.7 %copy-start.11 = (bf16[128,2048]{1,0:T(8,128)(2,1)S(1)}, bf16[128,2048]{1,0:T(8,128)(2,1)}, u32[]{:S(2)}) copy-start(bf16[128,2048]{1,0:T(8,128)(2,1)} %get-tuple-element.18) | copy-start | bytes 1572868
  154.5 62.3 %all-to-all-start.3 = ((bf16[8,48,2048]{2,1,0:T(8,128)(2,1)}), bf16[8,48,2048]{2,1,0:T(8,128)(2,1)}, u32[]{:S(2)}, u32[]{:S(2)}) async-start(bf16[8,48,2048]{2,1,0:T(8,128)(2,1)} %bitcast.116), calls=%async_computation.3 | async-start | bytes 3145728 | tf_op jit(solution)/shard_map/all_to_all | solution.py:46
  161.0 48.7 %collective-permute-start.5 = (bf16[512,2048]{1,0:T(8,128)(2,1)S(1)}, bf16[512,2048]{1,0:T(8,128)(2,1)S(1)}, u32[]{:S(2)}, u32[]{:S(2)}) collective-permute-start(bf16[512,2048]{1,0:T(8,128)(2,1)S(1)} %pad_maximum_fusion.1), channel_id=1, source_target_pairs={{0,8},{8,0},{16,24},{24,16},{1,9},{9,1},{17,25},{25,17},{2,10},{10... | collective-permute-start | bytes 6291464 | tf_op jit(solution)/shard_map/ppermute | solution.py:108
  161.1 9.2 %collective-permute-start.3 = (bf16[512,768]{1,0:T(8,128)(2,1)S(1)}, bf16[512,768]{1,0:T(8,128)(2,1)S(1)}, u32[]{:S(2)}, u32[]{:S(2)}) collective-permute-start(bf16[512,768]{1,0:T(8,128)(2,1)S(1)} %pad_maximum_fusion.3), channel_id=1, source_target_pairs={{0,8},{8,0},{16,24},{24,16},{1,9},{9,1},{17,25},{25,17},{2,10},{10... | collective-permute-start | bytes 2359304 | tf_op jit(solution)/shard_map/ppermute | solution.py:108
  163.8 9.8 %collective-permute-start.1 = (bf16[512,768]{1,0:T(8,128)(2,1)S(1)}, bf16[512,768]{1,0:T(8,128)(2,1)S(1)}, u32[]{:S(2)}, u32[]{:S(2)}) collective-permute-start(bf16[512,768]{1,0:T(8,128)(2,1)S(1)} %pad_maximum_fusion.2), channel_id=1, source_target_pairs={{0,8},{8,0},{16,24},{24,16},{1,9},{9,1},{17,25},{25,17},{2,10},{10... | collective-permute-start | bytes 2359304 | tf_op jit(solution)/shard_map/ppermute | solution.py:108
  172.0 20.5 %collective-permute-start.4 = (bf16[512,768]{1,0:T(8,128)(2,1)S(1)}, bf16[512,768]{1,0:T(8,128)(2,1)S(1)}, u32[]{:S(2)}, u32[]{:S(2)}) collective-permute-start(bf16[512,768]{1,0:T(8,128)(2,1)S(1)} %add_convert_fusion.2), channel_id=1, source_target_pairs={{0,16},{8,24},{16,0},{24,8},{1,17},{9,25},{17,1},{25,9},{2,18},{10... | collective-permute-start | bytes 2359304 | tf_op jit(solution)/shard_map/ppermute | solution.py:138
  175.2 32.9 %collective-permute-start.2 = (bf16[512,768]{1,0:T(8,128)(2,1)S(1)}, bf16[512,768]{1,0:T(8,128)(2,1)S(1)}, u32[]{:S(2)}, u32[]{:S(2)}) collective-permute-start(bf16[512,768]{1,0:T(8,128)(2,1)S(1)} %add_convert_fusion.3), channel_id=1, source_target_pairs={{0,16},{8,24},{16,0},{24,8},{1,17},{9,25},{17,1},{25,9},{2,18},{10... | collective-permute-start | bytes 2359304 | tf_op jit(solution)/shard_map/ppermute | solution.py:138
  212.3 18.6 %collective-permute-start.7 = (bf16[512,768]{1,0:T(8,128)(2,1)}, bf16[512,768]{1,0:T(8,128)(2,1)}, u32[]{:S(2)}, u32[]{:S(2)}) collective-permute-start(bf16[512,768]{1,0:T(8,128)(2,1)} %add_convert_fusion.1), channel_id=1, source_target_pairs={{0,16},{8,24},{16,0},{24,8},{1,17},{9,25},{17,1},{25,9},{2,18},{10... | collective-permute-start | bytes 2359304 | tf_op jit(solution)/shard_map/ppermute | solution.py:138
  213.8 5.1 %copy-start.9 = (bf16[1,2048,768]{2,1,0:T(8,128)(2,1)S(1)}, bf16[1,2048,768]{2,1,0:T(8,128)(2,1)}, u32[]{:S(2)}) copy-start(bf16[1,2048,768]{2,1,0:T(8,128)(2,1)} %param.13) | copy-start | bytes 9437188
  218.8 12.0 %copy-start.14 = (f32[512,768]{1,0:T(8,128)S(1)}, f32[512,768]{1,0:T(8,128)}, u32[]{:S(2)}) copy-start(f32[512,768]{1,0:T(8,128)} %fusion.49) | copy-start | bytes 4718596
  218.9 12.0 %copy-start.15 = (f32[512,768]{1,0:T(8,128)S(1)}, f32[512,768]{1,0:T(8,128)}, u32[]{:S(2)}) copy-start(f32[512,768]{1,0:T(8,128)} %fusion.57) | copy-start | bytes 4718596
  220.8 11.5 %copy-start.12 = (f32[1,512,768]{2,1,0:T(8,128)S(1)}, f32[1,512,768]{2,1,0:T(8,128)}, u32[]{:S(2)}) copy-start(f32[1,512,768]{2,1,0:T(8,128)} %add_bitcast_fusion.1) | copy-start | bytes 4718596
  220.8 11.5 %copy-start.13 = (f32[1,512,768]{2,1,0:T(8,128)S(1)}, f32[1,512,768]{2,1,0:T(8,128)}, u32[]{:S(2)}) copy-start(f32[1,512,768]{2,1,0:T(8,128)} %add_bitcast_fusion.2) | copy-start | bytes 4718596
  (23 other events, 46.6 us)

commit v2 on v1

v2 whole, which is shorter than its diff:
```python
import math

import jax
import jax.numpy as jnp
from jax import lax
from jax.experimental import pallas as pl
from jax.experimental.pallas import tpu as pltpu
from jax.sharding import PartitionSpec as P

F32 = jnp.float32
BF16 = jnp.bfloat16
MIB = 1 << 20
VMEM = pl.BlockSpec(memory_space=pltpu.VMEM)
SMEM = pl.BlockSpec(memory_space=pltpu.SMEM)
HBM = pl.BlockSpec(memory_space=pltpu.HBM)


def logistic_parts(act):
    sigma = jax.nn.sigmoid(act)
    return (act * sigma, sigma * (1.0 + act * (1.0 - sigma)))


def dot(left, right):
    return jnp.dot(left, right, preferred_element_type=F32)


def dot_rows(left, right):
    return lax.dot_general(left, right, (((0,), (0,)), ((), ())), preferred_element_type=F32)


def dot_back(left, weight):
    return lax.dot_general(left, weight, (((1,), (1,)), ((), ())), preferred_element_type=F32)


def tile_of(size, most):
    tile = most
    while size % tile:
        tile //= 2
    return tile


def held(array):
    return pltpu.with_memory_space_constraint(array, pltpu.HBM)


def pinned(array):
    return pltpu.with_memory_space_constraint(array, pltpu.VMEM)


def room(array):
    return pltpu.VMEM(array.shape, array.dtype)


def on_chip(dims, kind):
    return pltpu.VMEM(tuple(dims), kind)


def in_hbm(dims, kind):
    return pltpu.HBM(tuple(dims), kind)


def call(kernel, outs, operands, specs, flops, limit, scratch=(), name=None, aliases=None):
    total = sum(math.prod(o.shape) * o.dtype.itemsize for o in (*outs, *operands))
    return pl.pallas_call(
        kernel,
        out_shape=tuple(outs),
        in_specs=specs,
        out_specs=tuple(HBM if out.memory_space == pltpu.HBM else VMEM for out in outs),
        scratch_shapes=list(scratch),
        input_output_aliases=aliases or {},
        compiler_params=pltpu.CompilerParams(vmem_limit_bytes=limit * MIB),
        cost_estimate=pl.CostEstimate(flops=int(flops), bytes_accessed=int(total), transcendentals=0),
        name=name,
    )(*operands)


class Copies:
    def __init__(self, sems):
        self.sems, self.count, self.waiting = sems, 0, []

    def start(self, source, target, keep=False):
        copy = pltpu.make_async_copy(source, target, self.sems.at[self.count])
        self.count += 1
        copy.start()
        if keep:
            self.waiting.append(copy)
        return copy

    def finish(self):
        for copy in self.waiting:
            copy.wait()


def split(array, refs, cols):
    size = refs[0].shape[0]
    for i, ref in enumerate(refs):
        ref[:, cols] = array[i * size : (i + 1) * size]


def joined_rows(refs, cols):
    return jnp.concatenate([ref[:, cols] for ref in refs], axis=0) if len(refs) > 1 else refs[0][:, cols]


def place_of(ids_ref, cores, part):
    device = ids_ref[1]
    chip = device // cores
    return device * part, (device - chip * cores) * part, chip


def aligned(begin):
    return pl.multiple_of(begin, 128)


def chip_columns(ids_ref, shift, chips, cores, part):
    _, _, chip = place_of(ids_ref, cores, part)
    other = chip + shift
    return pl.ds(aligned(jnp.where(other >= chips, other - chips, other) * (cores * part)), cores * part)


def home_of(ids_ref, k, n_blocks):
    place = ids_ref[0] - k
    return jnp.where(place < 0, place + n_blocks, place) if n_blocks > 1 else 0


def column_of(row):
    count = row.shape[1]
    same = lax.broadcasted_iota(jnp.int32, (count, count), 0) == lax.broadcasted_iota(
        jnp.int32, (count, count), 1
    )
    return jnp.sum(jnp.where(same, row, 0.0), axis=1, keepdims=True)


def dispatch(ids, tokens, routes_t, groups, capacity, n_blocks):
    tok, width = tokens.shape
    choose = routes_t.shape[0]
    slots = groups * capacity
    pairs = choose * tok
    step = tile_of(width, 512)

    def kernel(ids_ref, tokens_hbm, routes_hbm, *refs):
        blocks, (place_ref, pick_ref, tokens_ref, routes_ref, sems) = refs[:n_blocks], refs[n_blocks:]
        copies = Copies(sems)
        routes_in = copies.start(routes_hbm, routes_ref)
        tokens_in = copies.start(tokens_hbm, tokens_ref)
        routes_in.wait()
        chosen = routes_ref[...]
        near = chosen - ids_ref[0]
        near = jnp.where(near < 0, near + groups, near)
        expert_ids = lax.broadcasted_iota(jnp.int32, (groups, tok), 0)
        member = jnp.zeros((groups, tok), F32)
        for k in range(choose):
            member += (chosen[k : k + 1, :] == expert_ids).astype(F32)
        upper = lax.broadcasted_iota(jnp.int32, (tok, tok), 0) < lax.broadcasted_iota(
            jnp.int32, (tok, tok), 1
        )
        before = dot(member.astype(BF16), upper.astype(F32).astype(BF16))
        slot_ids = lax.broadcasted_iota(jnp.int32, (slots, tok), 0)
        both = jnp.zeros((slots, tok), F32)
        for k in range(choose):
            mine = chosen[k : k + 1, :]
            slot = jnp.sum(jnp.where(mine == expert_ids, before, 0.0), axis=0, keepdims=True).astype(jnp.int32)
            hit = (slot_ids == near[k : k + 1, :] * capacity + slot).astype(F32)
            place_ref[:, k * tok : (k + 1) * tok] = hit.astype(BF16)
            both += hit
            hit = (slot_ids == mine * capacity + slot).astype(F32)
            pick_ref[k * tok : (k + 1) * tok, :] = hit.T.astype(BF16)
        both = both.astype(BF16)
        tokens_in.wait()
        for n in range(0, width, step):
            cols = pl.ds(n, step)
            split(dot(both, tokens_ref[:, cols]).astype(BF16), blocks, cols)

    outs = call(
        kernel,
        [on_chip((slots // n_blocks, width), BF16)] * n_blocks
        + [on_chip((slots, pairs), BF16), on_chip((pairs, slots), BF16)],
        [ids, held(tokens), held(routes_t)],
        [SMEM, HBM, HBM],
        2 * slots * tok * width,
        8,
        [room(tokens), room(routes_t), pltpu.SemaphoreType.DMA((2,))],
        name="dispatch",
    )
    return list(outs[:n_blocks]), *outs[n_blocks:]


def hidden_units(rows, gate_ref, up_ref, hidden_ref, silu_ref, factor_ref, f_tile):
    for j in range(0, gate_ref.shape[1], f_tile):
        cols = pl.ds(j, f_tile)
        gate = dot(rows, gate_ref[:, cols])
        up = dot(rows, up_ref[:, cols])
        silu, slope = logistic_parts(gate)
        silu_ref[:, cols] = silu
        factor_ref[:, cols] = up * slope
        hidden_ref[:, cols] = (silu * up).astype(BF16)


def forward_local(tokens, w_gate, w_up, w_down, keep_row):
    count, width = tokens.shape
    units = w_gate.shape[1]
    f_tile, d_tile = tile_of(units, 256), tile_of(width, 512)

    def kernel(tokens_hbm, gate_hbm, up_hbm, down_hbm, keep_hbm, *refs):
        out_hbm, silu_hbm, factor_hbm, hidden_ref, tokens_ref, gate_ref, up_ref, down_ref = refs[:8]
        keep_ref, out_ref, silu_ref, factor_ref, sems = refs[8:]
        copies = Copies(sems)
        arriving = [
            copies.start(source, target)
            for source, target in (
                (tokens_hbm, tokens_ref),
                (keep_hbm, keep_ref),
                (gate_hbm, gate_ref),
                (up_hbm, up_ref),
                (down_hbm, down_ref),
            )
        ]
        for copy in arriving[:4]:
            copy.wait()
        hidden_units(tokens_ref[...], gate_ref, up_ref, hidden_ref, silu_ref, factor_ref, f_tile)
        copies.start(silu_ref, silu_hbm, True)
        copies.start(factor_ref, factor_hbm, True)
        keep = column_of(keep_ref[...].astype(F32))
        arriving[4].wait()
        for n in range(0, width, d_tile):
            cols = pl.ds(n, d_tile)
            out_ref[:, cols] = keep * dot(hidden_ref[...], down_ref[:, cols])
        copies.start(out_ref, out_hbm, True)
        copies.finish()

    return call(
        kernel,
        [
            in_hbm((count, width), F32),
            in_hbm((count, units), F32),
            in_hbm((count, units), F32),
            on_chip((count, units), BF16),
            on_chip((count, width), BF16),
            on_chip(w_gate.shape, BF16),
            on_chip(w_up.shape, BF16),
            on_chip(w_down.shape, BF16),
        ],
        [held(array) for array in (tokens, w_gate, w_up, w_down, keep_row)],
        [HBM] * 5,
        6 * count * width * units,
        8,
        [
            room(keep_row),
            pltpu.VMEM((count, width), F32),
            pltpu.VMEM((count, units), F32),
            pltpu.VMEM((count, units), F32),
            pltpu.SemaphoreType.DMA((8,)),
        ],
        name="forward_local",
    )


def forward(ids, blocks, tokens, local_hidden, w_gate, w_up, w_down, chips, cores, part):
    n_blocks = len(blocks)
    size, width = blocks[0].shape
    count = n_blocks * size
    total = count + tokens.shape[0]
    units = w_gate.shape[1]
    f_tile, d_tile = tile_of(units, 256), tile_of(width, 512)

    def kernel(ids_ref, *refs):
        ins, refs = refs[:n_blocks], refs[n_blocks:]
        (tokens_ref, local_ref, gate_ref, up_ref, down_ref), refs = refs[:5], refs[5:]
        (out_hbm, rows_hbm, hidden_hbm, silu_hbm, factor_hbm), refs = refs[:5], refs[5:]
        sent, (out_ref, rows_ref, hidden_ref, silu_ref, factor_ref, sems) = refs[: chips - 1], refs[chips - 1 :]
        copies = Copies(sems)
        for i, ref in enumerate(ins):
            rows_ref[i * size : (i + 1) * size, :] = ref[...]
        rows_ref[count:, :] = tokens_ref[...]
        hidden_ref[count:, :] = local_ref[...]
        copies.start(rows_ref, rows_hbm, True)
        routed = pl.ds(0, count)
        hidden_units(
            rows_ref[:count, :], gate_ref, up_ref, hidden_ref.at[routed], silu_ref, factor_ref, f_tile
        )
        copies.start(hidden_ref, hidden_hbm, True)
        copies.start(silu_ref, silu_hbm, True)
        copies.start(factor_ref, factor_hbm, True)
        for n in range(0, width, d_tile):
            cols = pl.ds(n, d_tile)
            out_ref[:, cols] = dot(hidden_ref[:count, :], down_ref[:, cols]).astype(BF16)
            for k in range(n_blocks):
                target = out_hbm.at[pl.ds(home_of(ids_ref, k, n_blocks) * size, size), cols]
                copies.start(out_ref.at[pl.ds(k * size, size), cols], target, True)
        for shift, target in enumerate(sent, 1):
            target[...] = rows_ref[:, chip_columns(ids_ref, shift, chips, cores, part)]
        copies.finish()

    outs = call(
        kernel,
        [
            in_hbm((count, width), BF16),
            in_hbm((total, width), BF16),
            in_hbm((total, units), BF16),
            in_hbm((count, units), F32),
            in_hbm((count, units), F32),
        ]
        + [on_chip((total, cores * part), BF16)] * (chips - 1),
        [ids] + [pinned(array) for array in (*blocks, tokens, local_hidden, w_gate, w_up, w_down)],
        [SMEM] + [VMEM] * (n_blocks + 5),
        6 * count * width * units,
        16,
        [
            pltpu.VMEM((count, width), BF16),
            pltpu.VMEM((total, width), BF16),
            pltpu.VMEM((total, units), BF16),
            pltpu.VMEM((count, units), F32),
            pltpu.VMEM((count, units), F32),
            pltpu.SemaphoreType.DMA((4 + n_blocks * (width // d_tile),)),
        ],
        name="forward",
    )
    return *outs[:5], list(outs[5:])


def mix(returned, place, pick, gates_t, keep_row, cotangent, local_out, n_blocks):
    slots, width = returned.shape
    choose, tok = gates_t.shape
    step = tile_of(width, 512)

    def kernel(returned_ref, *refs):
        sources, refs = refs[:6], refs[6:]
        outs, local_ref, refs = refs[:n_blocks], refs[n_blocks], refs[n_blocks + 1 :]
        targets, sems = refs[:6], refs[6]
        pick_ref, gates_ref, keep_ref, out_ref, cot_ref, place_ref = targets
        copies = Copies(sems)
        arriving = [copies.start(source, target) for source, target in zip(sources, targets)]
        for copy in arriving:
            copy.wait()
        gates = [column_of(gates_ref[k : k + 1, :]) for k in range(choose)]
        keep = column_of(keep_ref[...].astype(F32))
        for n in range(0, width, step):
            cols = pl.ds(n, step)
            picked = dot(pick_ref[...], returned_ref[:, cols])
            mixed = sum(gates[k] * picked[k * tok : (k + 1) * tok] for k in range(choose))
            difference = mixed - out_ref[:, cols]
            upstream = cot_ref[:, cols].astype(F32) + difference
            local_ref[:, cols] = (-(keep * difference)).astype(BF16)
            routed = jnp.concatenate([(gate * upstream).astype(BF16) for gate in gates], axis=0)
            split(dot(place_ref[...], routed).astype(BF16), outs, cols)

    brought = [pick, gates_t, keep_row, local_out, cotangent, place]
    outs = call(
        kernel,
        [on_chip((slots // n_blocks, width), BF16)] * n_blocks + [on_chip((tok, width), BF16)],
        [returned] + [held(array) for array in brought],
        [VMEM] + [HBM] * 6,
        4 * slots * choose * tok * width,
        10,
        [room(array) for array in brought] + [pltpu.SemaphoreType.DMA((6,))],
        name="mix",
    )
    return list(outs[:n_blocks]), outs[n_blocks]


def gradients(cots, silu_ref, factor_ref, down_ref, gate_back, up_back, f_tile):
    for j in range(0, gate_back.shape[1], f_tile):
        cols = pl.ds(j, f_tile)
        grad = dot_back(cots, down_ref[cols, :])
        gate_back[:, cols] = (grad * factor_ref[:, cols]).astype(BF16)
        up_back[:, cols] = (grad * silu_ref[:, cols]).astype(BF16)


def backward_local(ids, cots, silu, factor, w_gate, w_up, w_down, kept, chips, cores, part):
    count, width = cots.shape
    units = w_gate.shape[1]
    f_tile, d_tile = tile_of(units, 256), tile_of(width, 512)
    span = cores * part
    n_kept = len(kept)

    def kernel(ids_ref, cots_ref, silu_hbm, factor_hbm, gate_hbm, up_hbm, down_hbm, *refs):
        kept_hbm, (back_hbm, gate_ref, up_ref, down_ref), refs = refs[:n_kept], refs[n_kept : n_kept + 4], refs[n_kept + 4 :]
        kept_refs, sent, refs = refs[:n_kept], refs[n_kept : n_kept + chips], refs[n_kept + chips :]
        back_ref, silu_ref, factor_ref, gate_back, up_back, sems = refs
        copies = Copies(sems)
        first = [copies.start(s, t) for s, t in ((silu_hbm, silu_ref), (factor_hbm, factor_ref), (down_hbm, down_ref))]
        second = [copies.start(s, t) for s, t in ((gate_hbm, gate_ref), (up_hbm, up_ref))]
        for source, target in zip(kept_hbm, kept_refs):
            copies.start(source, target, True)
        for copy in first:
            copy.wait()
        gradients(cots_ref[...], silu_ref, factor_ref, down_ref, gate_back, up_back, f_tile)
        for shift, target in enumerate(sent):
            target[:, :span] = cots_ref[:, chip_columns(ids_ref, shift, chips, cores, part)]
            target[:, span : span + units] = gate_back[...]
            target[:, span + units :] = up_back[...]
        for copy in second:
            copy.wait()
        for n in range(0, width, d_tile):
            cols = pl.ds(n, d_tile)
            back = dot_back(gate_back[...], gate_ref[cols, :])
            back += dot_back(up_back[...], up_ref[cols, :])
            back_ref[:, cols] = back
        copies.start(back_ref, back_hbm, True)
        copies.finish()

    outs = call(
        kernel,
        [in_hbm((count, width), F32)]
        + [on_chip(array.shape, array.dtype) for array in (w_gate, w_up, w_down, *kept)]
        + [on_chip((count, span + 2 * units), BF16)] * chips,
        [ids, pinned(cots)] + [held(array) for array in (silu, factor, w_gate, w_up, w_down, *kept)],
        [SMEM, VMEM] + [HBM] * (5 + n_kept),
        6 * count * width * units,
        10,
        [
            pltpu.VMEM((count, width), F32),
            room(silu),
            room(factor),
            pltpu.VMEM((count, units), BF16),
            pltpu.VMEM((count, units), BF16),
            pltpu.SemaphoreType.DMA((6 + n_kept,)),
        ],
        name="backward_local",
    )
    return outs[0], outs[1:4], outs[4 : 4 + n_kept], list(outs[4 + n_kept :])


def collect(ids, blocks, chips, cores, part):
    n_blocks = len(blocks)
    size, width = blocks[0].shape
    count, span = n_blocks * size, cores * part

    def kernel(ids_ref, *refs):
        ins, (rows_ref, *sent) = refs[:n_blocks], refs[n_blocks:]
        for i, ref in enumerate(ins):
            rows = pl.ds(i * size, size)
            rows_ref[rows, :] = ref[...]
            for shift, target in enumerate(sent, 1):
                target[rows, :] = ref[:, chip_columns(ids_ref, shift, chips, cores, part)]

    outs = call(
        kernel,
        [on_chip((count, width), BF16)] + [on_chip((count, span), BF16)] * (chips - 1),
        [ids] + [pinned(block) for block in blocks],
        [SMEM] + [VMEM] * n_blocks,
        0,
        8,
        name="collect",
    )
    return outs[0], list(outs[1:])


def backward(ids, cots, silu, factor, w_gate, w_up, w_down, n_blocks):
    count, width = cots.shape
    units = w_gate.shape[1]
    size = count // n_blocks
    f_tile, d_tile = tile_of(units, 256), tile_of(width, 512)

    def kernel(ids_ref, cots_ref, silu_ref, factor_ref, gate_ref, up_ref, down_ref, *refs):
        back_hbm, gate_hbm, up_hbm, back_ref, gate_back, up_back, sems = refs
        copies = Copies(sems)
        gradients(cots_ref[...], silu_ref, factor_ref, down_ref, gate_back, up_back, f_tile)
        copies.start(gate_back, gate_hbm, True)
        copies.start(up_back, up_hbm, True)
        for n in range(0, width, d_tile):
            cols = pl.ds(n, d_tile)
            back = dot_back(gate_back[...], gate_ref[cols, :])
            back += dot_back(up_back[...], up_ref[cols, :])
            back_ref[:, cols] = back.astype(BF16)
            for k in range(n_blocks):
                target = back_hbm.at[pl.ds(home_of(ids_ref, k, n_blocks) * size, size), cols]
                copies.start(back_ref.at[pl.ds(k * size, size), cols], target, True)
        copies.finish()

    return call(
        kernel,
        [in_hbm((count, width), BF16), in_hbm((count, units), BF16), in_hbm((count, units), BF16)],
        [ids] + [pinned(array) for array in (cots, silu, factor, w_gate, w_up, w_down)],
        [SMEM] + [VMEM] * 6,
        6 * count * width * units,
        10,
        [
            pltpu.VMEM((count, width), BF16),
            pltpu.VMEM((count, units), BF16),
            pltpu.VMEM((count, units), BF16),
            pltpu.SemaphoreType.DMA((2 + n_blocks * (width // d_tile),)),
        ],
        name="backward",
    )


WHOLE, CHIP = -1, -2


def weight_sums(ids, cores, part, terms, previous, units, sections, scale):
    step = tile_of(units, 256)
    begun = [] if previous is None else [previous]
    arrays = []
    for left, right, *_ in terms:
        for array, _ in left + right:
            arrays += [] if any(array is other for other in arrays) else [array]
    where = lambda array: next(i for i, other in enumerate(arrays) if other is array)
    rows_of = [sum(array.shape[0] for array, _ in left) for left, *_ in terms]
    n_copies = sum(len(left) + len(right) for left, right, *_ in terms)

    def kernel(ids_ref, *refs):
        sources, refs = refs[: len(arrays)], refs[len(arrays) :]
        begun_hbm, out_hbm, refs = refs[: len(begun)], refs[len(begun)], refs[len(begun) + 1 :]
        lefts, rights, out_ref, sems = refs[: len(terms)], refs[len(terms) : 2 * len(terms)], refs[-2], refs[-1]
        copies = Copies(sems)
        at_whole, at_chip, _ = place_of(ids_ref, cores, part)

        def bring(pieces, target, columns):
            row, started = 0, []
            for array, first in pieces:
                first = aligned(at_whole if first == WHOLE else at_chip) if first < 0 else first
                count = array.shape[0]
                source = sources[where(array)].at[:, pl.ds(first, columns)]
                started.append(copies.start(source, target.at[pl.ds(row, count), :]))
                row += count
            return started

        arriving = []
        for (left, right, _, wide), left_ref, right_ref in zip(terms, lefts, rights):
            arriving += bring(left, left_ref, part) + bring(right, right_ref, wide * units)
        for source in begun_hbm:
            for section in sections:
                cols = pl.ds(section * units, units)
                arriving.append(copies.start(source.at[:, cols], out_ref.at[:, cols]))
        for copy in arriving:
            copy.wait()
        for section in sections:
            for at in range(0, units, step):
                cols = pl.ds(section * units + at, step)
                total = out_ref[:, cols] if begun else None
                for i, (_, _, first, wide) in enumerate(terms):
                    if first <= section < first + wide:
                        begin = (section - first) * units + at
                        term = dot_rows(lefts[i][...], rights[i][:, begin : begin + step])
                        total = term if total is None else total + term
                out_ref[:, cols] = total if scale is None else total * scale
                copies.start(out_ref.at[:, cols], out_hbm.at[:, cols], True)
        copies.finish()

    operands = [ids] + [held(array) for array in (*arrays, *begun)]
    (out,) = call(
        kernel,
        [in_hbm((part, 3 * units), F32)],
        operands,
        [SMEM] + [HBM] * (len(operands) - 1),
        sum(2 * rows * part * wide * units for rows, (*_, wide) in zip(rows_of, terms)),
        20,
        [pltpu.VMEM((rows, part), BF16) for rows in rows_of]
        + [pltpu.VMEM((rows, wide * units), BF16) for rows, (*_, wide) in zip(rows_of, terms)]
        + [
            pltpu.VMEM((part, 3 * units), F32),
            pltpu.SemaphoreType.DMA((n_copies + len(begun) * len(sections) + len(sections) * (units // step),)),
        ],
        name="weight_sums",
        aliases={len(operands) - 1: 0} if begun else None,
    )
    return out


def combine(returned, pick, local_back, choose):
    slots, width = returned.shape
    tok = local_back.shape[0]
    step = tile_of(width, 512)

    def kernel(returned_ref, pick_hbm, local_hbm, out_hbm, pick_ref, local_ref, out_ref, sems):
        copies = Copies(sems)
        pick_in = copies.start(pick_hbm, pick_ref)
        local_in = copies.start(local_hbm, local_ref)
        pick_in.wait()
        local_in.wait()
        both = sum(pick_ref[k * tok : (k + 1) * tok, :].astype(F32) for k in range(choose)).astype(BF16)
        for n in range(0, width, step):
            cols = pl.ds(n, step)
            out_ref[:, cols] = (dot(both, returned_ref[:, cols]) + local_ref[:, cols]).astype(BF16)
            copies.start(out_ref.at[:, cols], out_hbm.at[:, cols], True)
        copies.finish()

    (out,) = call(
        kernel,
        [in_hbm((tok, width), BF16)],
        [returned, held(pick), held(local_back)],
        [VMEM, HBM, HBM],
        2 * slots * tok * width,
        8,
        [
            room(pick),
            room(local_back),
            pltpu.VMEM((tok, width), BF16),
            pltpu.SemaphoreType.DMA((2 + width // step,)),
        ],
        name="combine",
    )
    return out


def on_device(tokens, routes, gates, keep, cotangent, w_gate, w_up, w_down):
    groups = lax.axis_size("expert")
    replicas = lax.axis_size("dp")
    tok_count, width = tokens.shape
    choose = routes.shape[1]
    capacity = 3 * tok_count * choose // (2 * groups)
    slots = groups * capacity
    apart = capacity % 16 == 0 and groups <= 8
    n_blocks = groups if apart else 1
    cores = 2 if replicas % 2 == 0 else 1
    chips = replicas // cores
    part = width // replicas
    span = cores * part
    units = w_gate.shape[2]
    weights = (w_gate[0], w_up[0], w_down[0])
    siblings = [(i, i ^ 1) for i in range(replicas)]
    first = lax.axis_index("expert") if apart else 0
    ids = jnp.stack([jnp.asarray(first, jnp.int32), lax.axis_index("dp").astype(jnp.int32)])
    keep_row = keep[None]
    together = lax.optimization_barrier
    far_first = sorted(range(1, groups), key=lambda k: abs(k - groups / 2))

    def at_once(block):
        block = block.reshape(groups, capacity, -1)
        moved = lax.all_to_all(block, "expert", split_axis=0, concat_axis=0, tiled=True)
        return moved.reshape(slots, -1)

    def step_by_step(blocks):
        if not apart:
            return [at_once(blocks[0])]
        moved = [blocks[0]] + [None] * (groups - 1)
        for k in far_first:
            moved[k] = lax.ppermute(blocks[k], "expert", [(i, (i + k) % groups) for i in range(groups)])
        return moved

    def to_chips(arrays):
        return [
            lax.ppermute(
                array,
                "dp",
                [
                    (start * cores + i, (start + shift) % chips * cores + i)
                    for start in range(chips)
                    for i in range(cores)
                ],
            )
            for shift, array in enumerate(arrays, 1)
        ]

    def from_sibling(arrays):
        return [lax.ppermute(array, "dp", siblings) for array in arrays] if cores == 2 else []

    def to_others(array):
        return to_chips([array] * (chips - 1))

    blocks, place, pick = dispatch(ids, tokens, routes.T, groups, capacity, n_blocks)
    blocks = step_by_step(blocks)
    local_out, local_silu, local_factor, local_hidden, tokens_on, *on = forward_local(tokens, *weights, keep_row)
    out, rows, hidden, silu, factor, x_send = forward(
        ids, blocks, tokens_on, local_hidden, *on, chips, cores, part
    )
    returned = at_once(out)
    x_far = to_chips(x_send)
    h_far = to_others(hidden)
    returned, x_far, h_far = together((returned, x_far, h_far))
    blocks, local_cot = mix(returned, place, pick, gates.T, keep_row, cotangent, local_out, n_blocks)
    blocks = step_by_step(blocks)
    local_back, on, kept, l_send = backward_local(
        ids, local_cot, local_silu, local_factor, *weights, (silu, factor), chips, cores, part
    )
    l_own, l_far = l_send[0], to_chips(l_send[1:])
    blocks, l_far = together((blocks, l_far))
    cots, c_send = collect(ids, blocks, chips, cores, part)
    back, gate_back, up_back = backward(ids, cots, *kept, *on, n_blocks)
    returned = at_once(back)
    c_far = to_chips(c_send)
    g_far = to_others(gate_back)
    u_far = to_others(up_back)

    def terms_x(xs, at, gs, us, ls):
        return [
            ([(x, at)], [(right, 0), (l, span + section * units)], section, 1)
            for x, g, u, l in zip(xs, gs, us, ls)
            for section, right in enumerate((g, u))
        ]

    def terms_c(cs, at, ls, hs):
        return [([(c, at), (l, CHIP)], [(h, 0)], 2, 1) for c, l, h in zip(cs, ls, hs)]

    def both_cores(arrays):
        return arrays + from_sibling(arrays)

    x_near, h_near, l_near = both_cores([rows]), both_cores([hidden]), both_cores([l_own])
    g_near, u_near, c_near = both_cores([gate_back]), both_cores([up_back]), both_cores([cots])
    x_far, h_far, l_far = both_cores(x_far), both_cores(h_far), both_cores(l_far)
    c_far, g_far = both_cores(c_far), both_cores(g_far)
    scale = 1.0 / replicas
    totals = weight_sums(
        ids,
        cores,
        part,
        terms_x(x_near, WHOLE, g_near, u_near, l_near) + terms_c(c_near, WHOLE, l_near, h_near),
        None,
        units,
        (0, 1, 2),
        None,
    )
    if chips > 1:
        totals = weight_sums(
            ids, cores, part, terms_c(c_far, CHIP, l_far, h_far), totals, units, (2,), scale
        )
        u_far, totals = together((u_far, totals))
    u_far = both_cores(u_far)
    totals = weight_sums(
        ids,
        cores,
        part,
        terms_x(x_far, CHIP, g_far, u_far, l_far),
        totals,
        units,
        (0, 1) if chips > 1 else (0, 1, 2),
        scale,
    )
    token_grads = combine(returned, pick, local_back, choose)
    return (token_grads, totals[None])


def solution(mesh):
    return jax.shard_map(
        on_device,
        mesh=mesh,
        in_specs=(
            P(("dp", "expert"), None),
            P(("dp", "expert"), None),
            P(("dp", "expert"), None),
            P(("dp", "expert")),
            P(("dp", "expert"), None),
            P("expert", None, None),
            P("expert", None, None),
            P("expert", None, None),
        ),
        out_specs=(P(("dp", "expert"), None), P("expert", "dp", None)),
        check_vma=False,
    )
```

time: 237 us -> 225 us (0.949)
  matrix products: 54.9 us -> 0 us
  starting transfers between devices: 18.3 us -> 72.5 us
  Pallas kernels: 0 us -> 54 us
  blocking collectives: 44.3 us -> 0 us
  other arithmetic: 14.6 us -> 0.08 us
  waiting for transfers between devices: 95.7 us -> 90.5 us
    all_to_all x3 -> x2, waiting for transfers between devices: 58.1 us -> 0.01 us  [at_once(): lax.all_to_all(block, 'expert', split_axis=0, concat_axis=0, tiled=True)]
    dot_general x31 -> x0, matrix products: 54.9 us -> none  [the longest x15 23.4 us: dot_rows(): lax.dot_general(left, right, (((0,), (0,)), ((), ())), preferred_element_...]
    pallas_call x0 -> x11, Pallas kernels: none -> 54 us  [call(): pl.pallas_call(kernel, out_shape=tuple(outs), in_specs=specs, out_specs=t...]
    ppermute x8 -> x32, waiting for transfers between devices: 37.6 us -> 90.4 us  [the longest x6 67.4 us: to_chips(): lax.ppermute(array, 'dp', [(start * cores + i, (start + shift) % chips *...]
    ppermute x8 -> x32, starting transfers between devices: 4.72 us -> 54 us  [the longest x14 45.8 us: step_by_step(): lax.ppermute(blocks[k], 'expert', [(i, (i + k) % groups) for i in range(g...]
    all_to_all x1 -> x0, blocking collectives: 44.3 us -> none  [exchange(): lax.all_to_all(block, 'expert', split_axis=0, concat_axis=0, tiled=True)]
    concatenate x8 -> x0, other arithmetic: 11.1 us -> none  [the longest x3 4.43 us: on_device(): expert_grads = (jnp.concatenate(totals, axis=1) * (1.0 / replicas))[None]]
    all_to_all x3 -> x2, starting transfers between devices: 13.6 us -> 18.6 us  [at_once(): lax.all_to_all(block, 'expert', split_axis=0, concat_axis=0, tiled=True)]
  transfers between devices with their start and end apart: 11 -> 34, of which waited for: 5 -> 14; matrix products, arithmetic and copies ran while one was open for 21% -> 0% of each run, Pallas kernels for 0% -> 19%
where the time goes in v2:
time: 225 us
  waiting for transfers between devices  90.5 us (40%)
  starting transfers between devices  72.5 us (32%)
  Pallas kernels  54 us (24%)
  local copies, waits for them, and re-layouts  6.73 us (3%)
    ppermute x6, waiting for transfers between devices, to_chips(): lax.ppermute(array, 'dp', [(start * cores + i, (start + shift) % chips *...  67.4 us
    pallas_call x11, Pallas kernels, call(): pl.pallas_call(kernel, out_shape=tuple(outs), in_specs=specs, out_specs=t...  54 us
    ppermute x14, starting transfers between devices, step_by_step(): lax.ppermute(blocks[k], 'expert', [(i, (i + k) % groups) for i in range(g...  45.8 us
    ppermute x14, waiting for transfers between devices, step_by_step(): lax.ppermute(blocks[k], 'expert', [(i, (i + k) % groups) for i in range(g...  20.1 us
    all_to_all x2, starting transfers between devices, at_once(): lax.all_to_all(block, 'expert', split_axis=0, concat_axis=0, tiled=True)  18.6 us
    unnamed x38, local copies, waits for them, and re-layouts  6.73 us
    ppermute x6, starting transfers between devices, to_chips(): lax.ppermute(array, 'dp', [(start * cores + i, (start + shift) % chips *...  6.21 us
  transfers between devices with their start and end apart: 34, of which 14 were waited for; matrix products, arithmetic and copies ran while one was open for 0% of the time, Pallas kernels for 19%

profile of v2, /device:TPU:0, one launch (start us, length us, event | category | flops | bytes accessed | tf_op | source)
XLA Modules:
  0.0 224.8 jit_solution(9237982308691360213)
XLA Ops:
  4.3 3.0 %collective-permute-start = (bf16[48,2048]{1,0:T(8,128)(2,1)S(1)}, bf16[48,2048]{1,0:T(8,128)(2,1)S(1)}, u32[]{:S(2)}, u32[]{:S(2)}) collective-permute-start(bf16[48,2048]{1,0:T(8,128)(2,1)S(1)} %get-tuple-element.63), channel_id=1, source_target_pairs={{0,1},{1,2},{2,3},{3,4},{4,5},{5,6},{6,7},{7,0},{8,9},{9,10},{10,1... | collective-permute-start | bytes 589832 | tf_op jit(solution)/shard_map/ppermute | solution.py:628
  8.8 2.5 %collective-permute-start.2 = (bf16[48,2048]{1,0:T(8,128)(2,1)S(1)}, bf16[48,2048]{1,0:T(8,128)(2,1)S(1)}, u32[]{:S(2)}, u32[]{:S(2)}) collective-permute-start(bf16[48,2048]{1,0:T(8,128)(2,1)S(1)} %get-tuple-element.65), channel_id=1, source_target_pairs={{0,3},{1,4},{2,5},{3,6},{4,7},{5,0},{6,1},{7,2},{8,11},{9,12},{10,... | collective-permute-start | bytes 589832 | tf_op jit(solution)/shard_map/ppermute | solution.py:628
  12.6 2.6 %collective-permute-start.4 = (bf16[48,2048]{1,0:T(8,128)(2,1)S(1)}, bf16[48,2048]{1,0:T(8,128)(2,1)S(1)}, u32[]{:S(2)}, u32[]{:S(2)}) collective-permute-start(bf16[48,2048]{1,0:T(8,128)(2,1)S(1)} %get-tuple-element.67), channel_id=1, source_target_pairs={{0,5},{1,6},{2,7},{3,0},{4,1},{5,2},{6,3},{7,4},{8,13},{9,14},{10,... | collective-permute-start | bytes 589832 | tf_op jit(solution)/shard_map/ppermute | solution.py:628
  18.0 3.4 %collective-permute-start.6 = (bf16[48,2048]{1,0:T(8,128)(2,1)S(1)}, bf16[48,2048]{1,0:T(8,128)(2,1)S(1)}, u32[]{:S(2)}, u32[]{:S(2)}) collective-permute-start(bf16[48,2048]{1,0:T(8,128)(2,1)S(1)} %get-tuple-element.69), channel_id=1, source_target_pairs={{0,7},{1,0},{2,1},{3,2},{4,3},{5,4},{6,5},{7,6},{8,15},{9,8},{10,9... | collective-permute-start | bytes 589832 | tf_op jit(solution)/shard_map/ppermute | solution.py:628
  21.4 5.7 %forward_local.1 = (f32[128,2048]{1,0:T(8,128)}, f32[128,768]{1,0:T(8,128)}, f32[128,768]{1,0:T(8,128)}, bf16[128,768]{1,0:T(8,128)(2,1)S(1)}, bf16[128,2048]{1,...) custom-call(bf16[128,2048]{1,0:T(8,128)(2,1)} %tokens_hbm.3, ...), custom_call_target="tpu_custom_call" | custom-call | flops 1207959552 | bytes 21955072 | tf_op jit(solution)/shard_map/forward_local/pallas_call | solution.py:64
  27.2 5.0 %collective-permute-done.2.refs_3_ = bf16[48,2048]{1,0:T(8,128)(2,1)S(1)} collective-permute-done((bf16[48,2048]{1,0:T(8,128)(2,1)S(1)}, bf16[48,2048]{1,0:T(8,128)(2,1)S(1)}, u32[]{:S(2)}, u32[]{:S(2)}) %collective-permute-start.2) | collective-permute-done | bytes 196640 | tf_op jit(solution)/shard_map/ppermute | solution.py:628
  33.8 6.1 %forward.1 = (bf16[384,2048]{1,0:T(8,128)(2,1)}, bf16[512,2048]{1,0:T(8,128)(2,1)}, bf16[512,768]{1,0:T(8,128)(2,1)}, f32[384,768]{1,0:T(8,128)}, f32[384,768]{1,0:T(8,128)}, /*index=5*/bf16[512,1024]{1,0:T(8,128)(2,1)S(1)}) custom-call(s32[2]{0:T(128)S(1)} %pad_add_fusion.ids_ref, bf16[48,2048]{1,0:T(8,128)(2,1)S(1)} %get-tuple-element.62.refs_0_, ...), custom_call_target="tpu_custom_call" | custom-call | flops 3623878656 | bytes 19595272 | tf_op jit(solution)/shard_map/forward/pallas_call | solution.py:64
  39.9 15.0 %all-to-all-start = ((bf16[8,48,2048]{2,1,0:T(8,128)(2,1)}), bf16[8,48,2048]{2,1,0:T(8,128)(2,1)S(1)}, u32[]{:S(2)}, u32[]{:S(2)}) async-start(bf16[8,48,2048]{2,1,0:T(8,128)(2,1)} %bitcast.23), calls=%async_computation | async-start | bytes 3145728 | tf_op jit(solution)/shard_map/all_to_all | solution.py:620
  56.9 38.6 %collective-permute-done.8.refs_2_ = bf16[512,768]{1,0:T(8,128)(2,1)S(1)} collective-permute-done((bf16[512,768]{1,0:T(8,128)(2,1)}, bf16[512,768]{1,0:T(8,128)(2,1)S(1)}, u32[]{:S(2)}, u32[]{:S(2)}) %collective-permute-start.8) | collective-permute-done | bytes 786464 | tf_op jit(solution)/shard_map/ppermute | solution.py:633
  96.4 3.5 %mix.1 = (bf16[48,2048]{1,0:T(8,128)(2,1)S(1)}, bf16[48,2048]{1,0:T(8,128)(2,1)S(1)}, bf16[48,2048]{1,0:T(8,128)(2,1)S(1)}, bf16[48,2048]{1,0:T(8,128)(2,1)S(1)}...) custom-call(bf16[384,2048]{1,0:T(8,128)(2,1)S(1)} %bitcast.14, ...), custom_call_target="tpu_custom_call" | custom-call | flops 805306368 | bytes 5637632 | tf_op jit(solution)/shard_map/mix/pallas_call | solution.py:64
  99.9 7.7 %backward_local.1 = (f32[128,2048]{1,0:T(8,128)}, bf16[2048,768]{1,0:T(8,128)(2,1)S(1)}, bf16[2048,768]{1,0:T(8,128)(2,1)S(1)}, bf16[768,2048]{1,0:T(8,128)(2,1)...) custom-call(s32[2]{0:T(128)S(1)} %pad_add_fusion.ids_ref, ...), custom_call_target="tpu_custom_call" | custom-call | flops 1207959552 | bytes 27262984 | tf_op jit(solution)/shard_map/backward_local/pallas_call | solution.py:64
  114.8 4.2 %collective-permute-done.10.refs_2_ = bf16[48,2048]{1,0:T(8,128)(2,1)S(1)} collective-permute-done((bf16[48,2048]{1,0:T(8,128)(2,1)S(1)}, bf16[48,2048]{1,0:T(8,128)(2,1)S(1)}, u32[]{:S(2)}, u32[]{:S(2)}) %collective-permute-start.10) | collective-permute-done | bytes 196640 | tf_op jit(solution)/shard_map/ppermute | solution.py:628
  119.0 16.9 %collective-permute-start.13 = (bf16[48,2048]{1,0:T(8,128)(2,1)S(1)}, bf16[48,2048]{1,0:T(8,128)(2,1)S(1)}, u32[]{:S(2)}, u32[]{:S(2)}) collective-permute-start(bf16[48,2048]{1,0:T(8,128)(2,1)S(1)} %get-tuple-element.87), channel_id=1, source_target_pairs={{0,5},{1,6},{2,7},{3,0},{4,1},{5,2},{6,3},{7,4},{8,13},{9,14},{10,... | collective-permute-start | bytes 589832 | tf_op jit(solution)/shard_map/ppermute | solution.py:628
  135.9 5.0 %collective-permute-start.14 = (bf16[48,2048]{1,0:T(8,128)(2,1)S(1)}, bf16[48,2048]{1,0:T(8,128)(2,1)S(1)}, u32[]{:S(2)}, u32[]{:S(2)}) collective-permute-start(bf16[48,2048]{1,0:T(8,128)(2,1)S(1)} %get-tuple-element.88), channel_id=1, source_target_pairs={{0,6},{1,7},{2,0},{3,1},{4,2},{5,3},{6,4},{7,5},{8,14},{9,15},{10,... | collective-permute-start | bytes 589832 | tf_op jit(solution)/shard_map/ppermute | solution.py:628
  144.9 3.8 %collective-permute-done.15.refs_7_ = bf16[48,2048]{1,0:T(8,128)(2,1)S(1)} collective-permute-done((bf16[48,2048]{1,0:T(8,128)(2,1)S(1)}, bf16[48,2048]{1,0:T(8,128)(2,1)S(1)}, u32[]{:S(2)}, u32[]{:S(2)}) %collective-permute-start.15) | collective-permute-done | bytes 196640 | tf_op jit(solution)/shard_map/ppermute | solution.py:628
  148.7 2.7 %collective-permute-done.9.refs_1_ = bf16[48,2048]{1,0:T(8,128)(2,1)S(1)} collective-permute-done((bf16[48,2048]{1,0:T(8,128)(2,1)S(1)}, bf16[48,2048]{1,0:T(8,128)(2,1)S(1)}, u32[]{:S(2)}, u32[]{:S(2)}) %collective-permute-start.9) | collective-permute-done | bytes 196640 | tf_op jit(solution)/shard_map/ppermute | solution.py:628
  153.8 5.7 %backward.1 = (bf16[384,2048]{1,0:T(8,128)(2,1)}, bf16[384,768]{1,0:T(8,128)(2,1)}, bf16[384,768]{1,0:T(8,128)(2,1)}) custom-call(s32[2]{0:T(128)S(1)} %pad_add_fusion.ids_ref, bf16[384,2048]{1,0:T(8,128)(2,1)S(1)} %get-tuple-element.104.cots_ref.refs_8_, f32[384,768]{1,0:T(8,128)S(1)} %get-tuple-element.105.silu_ref, ...), custom_call_target="tpu_custom_call" | custom-call | flops 3623878656 | bytes 16121864 | tf_op jit(solution)/shard_map/backward/pallas_call | solution.py:64
  159.6 3.6 %all-to-all-start.1 = ((bf16[8,48,2048]{2,1,0:T(8,128)(2,1)}), bf16[8,48,2048]{2,1,0:T(8,128)(2,1)S(1)}, u32[]{:S(2)}, u32[]{:S(2)}) async-start(bf16[8,48,2048]{2,1,0:T(8,128)(2,1)} %bitcast.22), calls=%async_computation.1 | async-start | bytes 3145728 | tf_op jit(solution)/shard_map/all_to_all | solution.py:620
  166.0 17.4 %collective-permute-done.19.refs_0_ = bf16[384,1024]{1,0:T(8,128)(2,1)S(1)} collective-permute-done((bf16[384,1024]{1,0:T(8,128)(2,1)}, bf16[384,1024]{1,0:T(8,128)(2,1)S(1)}, u32[]{:S(2)}, u32[]{:S(2)}) %collective-permute-start.19) | collective-permute-done | bytes 786464 | tf_op jit(solution)/shard_map/ppermute | solution.py:633
  186.1 7.9 %weight_sums.3.refs_6_ = f32[512,2304]{1,0:T(8,128)} custom-call(s32[2]{0:T(128)S(1)} %pad_add_fusion.ids_ref, bf16[512,2048]{1,0:T(8,128)(2,1)} %get-tuple-element.118.refs_0_, bf16[384,768]{1,0:T(8,128)(2,1)} %get-tuple-element.113.refs_1_, bf16[128,2560]{1,0:T(8,128)(2,1)} %copy-done.2, bf16[384,768]{1,0:T(8,128)(2,1)} %get-tuple-element.115.refs_3_, ...), custom_call_target="tpu_custom_call" | custom-call | flops 2415919104 | bytes 17301512 | tf_op jit(solution)/shard_map/weight_sums/pallas_call | solution.py:64
  194.0 6.4 %collective-permute-done.17.refs_1_ = bf16[384,768]{1,0:T(8,128)(2,1)S(1)} collective-permute-done((bf16[384,768]{1,0:T(8,128)(2,1)}, bf16[384,768]{1,0:T(8,128)(2,1)S(1)}, u32[]{:S(2)}, u32[]{:S(2)}) %collective-permute-start.17) | collective-permute-done | bytes 589856 | tf_op jit(solution)/shard_map/ppermute | solution.py:633
  202.3 4.8 %weight_sums.4.refs_8_ = f32[512,2304]{1,0:T(8,128)} custom-call(s32[2]{0:T(128)S(1)} %pad_add_fusion.ids_ref, bf16[384,1024]{1,0:T(8,128)(2,1)} %copy-done.9, bf16[128,2560]{1,0:T(8,128)(2,1)} %copy-done.5, bf16[512,768]{1,0:T(8,128)(2,1)} %copy-done.8, bf16[384,1024]{1,0:T(8,128)(2,1)} %copy-done.11, ...), custom_call_target="tpu_custom_call", output_to_operand_aliasing={{}: (7, {})} | custom-call | flops 805306368 | bytes 13893640 | tf_op jit(solution)/shard_map/weight_sums/pallas_call | solution.py:64
  207.1 5.0 %collective-permute-done.18.refs_3_ = bf16[384,768]{1,0:T(8,128)(2,1)S(1)} collective-permute-done((bf16[384,768]{1,0:T(8,128)(2,1)}, bf16[384,768]{1,0:T(8,128)(2,1)S(1)}, u32[]{:S(2)}, u32[]{:S(2)}) %collective-permute-start.18) | collective-permute-done | bytes 589856 | tf_op jit(solution)/shard_map/ppermute | solution.py:633
  215.1 7.1 %weight_sums.5 = f32[512,2304]{1,0:T(8,128)} custom-call(s32[2]{0:T(128)S(1)} %pad_add_fusion.ids_ref, bf16[512,1024]{1,0:T(8,128)(2,1)} %collective-permute-done.7.refs_0_, bf16[384,768]{1,0:T(8,128)(2,1)} %copy-done.13, bf16[128,2560]{1,0:T(8,128)(2,1)} %copy-done.5, bf16[384,768]{1,0:T(8,128)(2,1)} %copy-done.14, ...), custom_call_target="tpu_custom_call", output_to_operand_aliasing={{}: (9, {})} | custom-call | flops 1610612736 | bytes 15204360 | tf_op jit(solution)/shard_map/weight_sums/pallas_call | solution.py:64
  (94 shorter events, 40.0 us)
Async XLA Ops:
  8.8 23.4 %collective-permute-start.2 = (bf16[48,2048]{1,0:T(8,128)(2,1)S(1)}, bf16[48,2048]{1,0:T(8,128)(2,1)S(1)}, u32[]{:S(2)}, u32[]{:S(2)}) collective-permute-start(bf16[48,2048]{1,0:T(8,128)(2,1)S(1)} %get-tuple-element.65), channel_id=1, source_target_pairs={{0,3},{1,4},{2,5},{3,6},{4,7},{5,0},{6,1},{7,2},{8,11},{9,12},{10,... | collective-permute-start | bytes 589832 | tf_op jit(solution)/shard_map/ppermute | solution.py:628
  11.3 21.1 %collective-permute-start.3 = (bf16[48,2048]{1,0:T(8,128)(2,1)S(1)}, bf16[48,2048]{1,0:T(8,128)(2,1)S(1)}, u32[]{:S(2)}, u32[]{:S(2)}) collective-permute-start(bf16[48,2048]{1,0:T(8,128)(2,1)S(1)} %get-tuple-element.66), channel_id=1, source_target_pairs={{0,4},{1,5},{2,6},{3,7},{4,0},{5,1},{6,2},{7,3},{8,12},{9,13},{10,... | collective-permute-start | bytes 589832 | tf_op jit(solution)/shard_map/ppermute | solution.py:628
  12.6 19.8 %collective-permute-start.4 = (bf16[48,2048]{1,0:T(8,128)(2,1)S(1)}, bf16[48,2048]{1,0:T(8,128)(2,1)S(1)}, u32[]{:S(2)}, u32[]{:S(2)}) collective-permute-start(bf16[48,2048]{1,0:T(8,128)(2,1)S(1)} %get-tuple-element.67), channel_id=1, source_target_pairs={{0,5},{1,6},{2,7},{3,0},{4,1},{5,2},{6,3},{7,4},{8,13},{9,14},{10,... | collective-permute-start | bytes 589832 | tf_op jit(solution)/shard_map/ppermute | solution.py:628
  16.2 16.2 %collective-permute-start.5 = (bf16[48,2048]{1,0:T(8,128)(2,1)S(1)}, bf16[48,2048]{1,0:T(8,128)(2,1)S(1)}, u32[]{:S(2)}, u32[]{:S(2)}) collective-permute-start(bf16[48,2048]{1,0:T(8,128)(2,1)S(1)} %get-tuple-element.68), channel_id=1, source_target_pairs={{0,6},{1,7},{2,0},{3,1},{4,2},{5,3},{6,4},{7,5},{8,14},{9,15},{10,... | collective-permute-start | bytes 589832 | tf_op jit(solution)/shard_map/ppermute | solution.py:628
  39.9 56.5 %all-to-all-start = ((bf16[8,48,2048]{2,1,0:T(8,128)(2,1)}), bf16[8,48,2048]{2,1,0:T(8,128)(2,1)S(1)}, u32[]{:S(2)}, u32[]{:S(2)}) async-start(bf16[8,48,2048]{2,1,0:T(8,128)(2,1)} %bitcast.23), calls=%async_computation | async-start | bytes 3145728 | tf_op jit(solution)/shard_map/all_to_all | solution.py:620
  54.9 41.5 %collective-permute-start.7 = (bf16[512,1024]{1,0:T(8,128)(2,1)S(1)}, bf16[512,1024]{1,0:T(8,128)(2,1)}, u32[]{:S(2)}, u32[]{:S(2)}) collective-permute-start(bf16[512,1024]{1,0:T(8,128)(2,1)S(1)} %get-tuple-element.76), channel_id=1, source_target_pairs={{0,16},{8,24},{16,0},{24,8},{1,17},{9,25},{17,1},{25,9},{2,18},{10... | collective-permute-start | bytes 3145736 | tf_op jit(solution)/shard_map/ppermute | solution.py:633
  56.4 39.1 %collective-permute-start.8 = (bf16[512,768]{1,0:T(8,128)(2,1)}, bf16[512,768]{1,0:T(8,128)(2,1)S(1)}, u32[]{:S(2)}, u32[]{:S(2)}) collective-permute-start(bf16[512,768]{1,0:T(8,128)(2,1)} %get-tuple-element.77.refs_9_), channel_id=1, source_target_pairs={{0,16},{8,24},{16,0},{24,8},{1,17},{9,25},{17,1},{25,9},{2,18},{10... | collective-permute-start | bytes 2359304 | tf_op jit(solution)/shard_map/ppermute | solution.py:633
  56.9 107.4 %collective-permute-start.23 = (bf16[512,2048]{1,0:T(8,128)(2,1)}, bf16[512,2048]{1,0:T(8,128)(2,1)}, u32[]{:S(2)}, u32[]{:S(2)}) collective-permute-start(bf16[512,2048]{1,0:T(8,128)(2,1)} %get-tuple-element.118.refs_0_), channel_id=1, source_target_pairs={{0,8},{8,0},{16,24},{24,16},{1,9},{9,1},{17,25},{25,17},{2,10},{10... | collective-permute-start | bytes 6291464 | tf_op jit(solution)/shard_map/ppermute | solution.py:646
  107.6 43.7 %collective-permute-start.16 = (bf16[128,2560]{1,0:T(8,128)(2,1)S(1)}, bf16[128,2560]{1,0:T(8,128)(2,1)S(1)}, u32[]{:S(2)}, u32[]{:S(2)}) collective-permute-start(bf16[128,2560]{1,0:T(8,128)(2,1)S(1)} %get-tuple-element.95), channel_id=1, source_target_pairs={{0,16},{8,24},{16,0},{24,8},{1,17},{9,25},{17,1},{25,9},{2,18},{10... | collective-permute-start | bytes 1966088 | tf_op jit(solution)/shard_map/ppermute | solution.py:633
  111.0 24.9 %collective-permute-start.11 = (bf16[48,2048]{1,0:T(8,128)(2,1)S(1)}, bf16[48,2048]{1,0:T(8,128)(2,1)S(1)}, u32[]{:S(2)}, u32[]{:S(2)}) collective-permute-start(bf16[48,2048]{1,0:T(8,128)(2,1)S(1)} %get-tuple-element.85), channel_id=1, source_target_pairs={{0,3},{1,4},{2,5},{3,6},{4,7},{5,0},{6,1},{7,2},{8,11},{9,12},{10,... | collective-permute-start | bytes 589832 | tf_op jit(solution)/shard_map/ppermute | solution.py:628
  113.3 27.6 %collective-permute-start.12 = (bf16[48,2048]{1,0:T(8,128)(2,1)S(1)}, bf16[48,2048]{1,0:T(8,128)(2,1)S(1)}, u32[]{:S(2)}, u32[]{:S(2)}) collective-permute-start(bf16[48,2048]{1,0:T(8,128)(2,1)S(1)} %get-tuple-element.86), channel_id=1, source_target_pairs={{0,4},{1,5},{2,6},{3,7},{4,0},{5,1},{6,2},{7,3},{8,12},{9,13},{10,... | collective-permute-start | bytes 589832 | tf_op jit(solution)/shard_map/ppermute | solution.py:628
  119.0 24.0 %collective-permute-start.13 = (bf16[48,2048]{1,0:T(8,128)(2,1)S(1)}, bf16[48,2048]{1,0:T(8,128)(2,1)S(1)}, u32[]{:S(2)}, u32[]{:S(2)}) collective-permute-start(bf16[48,2048]{1,0:T(8,128)(2,1)S(1)} %get-tuple-element.87), channel_id=1, source_target_pairs={{0,5},{1,6},{2,7},{3,0},{4,1},{5,2},{6,3},{7,4},{8,13},{9,14},{10,... | collective-permute-start | bytes 589832 | tf_op jit(solution)/shard_map/ppermute | solution.py:628
  144.9 19.4 %collective-permute-start.28 = (bf16[512,768]{1,0:T(8,128)(2,1)}, bf16[512,768]{1,0:T(8,128)(2,1)}, u32[]{:S(2)}, u32[]{:S(2)}) collective-permute-start(bf16[512,768]{1,0:T(8,128)(2,1)} %get-tuple-element.77.refs_9_), channel_id=1, source_target_pairs={{0,8},{8,0},{16,24},{24,16},{1,9},{9,1},{17,25},{25,17},{2,10},{10... | collective-permute-start | bytes 2359304 | tf_op jit(solution)/shard_map/ppermute | solution.py:646
  153.8 32.2 %collective-permute-start.27 = (bf16[384,2048]{1,0:T(8,128)(2,1)S(1)}, bf16[384,2048]{1,0:T(8,128)(2,1)}, u32[]{:S(2)}, u32[]{:S(2)}) collective-permute-start(bf16[384,2048]{1,0:T(8,128)(2,1)S(1)} %get-tuple-element.104.cots_ref.refs_8_), channel_id=1, source_target_pairs={{0,8},{8,0},{16,24},{24,16},{1,9},{9,1},{17,25},{25,17},{2,10},{10... | collective-permute-start | bytes 4718600 | tf_op jit(solution)/shard_map/ppermute | solution.py:646
  159.6 62.6 %all-to-all-start.1 = ((bf16[8,48,2048]{2,1,0:T(8,128)(2,1)}), bf16[8,48,2048]{2,1,0:T(8,128)(2,1)S(1)}, u32[]{:S(2)}, u32[]{:S(2)}) async-start(bf16[8,48,2048]{2,1,0:T(8,128)(2,1)} %bitcast.22), calls=%async_computation.1 | async-start | bytes 3145728 | tf_op jit(solution)/shard_map/all_to_all | solution.py:620
  163.7 19.7 %collective-permute-start.19 = (bf16[384,1024]{1,0:T(8,128)(2,1)}, bf16[384,1024]{1,0:T(8,128)(2,1)S(1)}, u32[]{:S(2)}, u32[]{:S(2)}) collective-permute-start(bf16[384,1024]{1,0:T(8,128)(2,1)} %copy-done.4), channel_id=1, source_target_pairs={{0,16},{8,24},{16,0},{24,8},{1,17},{9,25},{17,1},{25,9},{2,18},{10... | collective-permute-start | bytes 2359304 | tf_op jit(solution)/shard_map/ppermute | solution.py:633
  164.3 19.2 %collective-permute-start.22 = (bf16[512,768]{1,0:T(8,128)(2,1)}, bf16[512,768]{1,0:T(8,128)(2,1)S(1)}, u32[]{:S(2)}, u32[]{:S(2)}) collective-permute-start(bf16[512,768]{1,0:T(8,128)(2,1)} %copy-done.8), channel_id=1, source_target_pairs={{0,8},{8,0},{16,24},{24,16},{1,9},{9,1},{17,25},{25,17},{2,10},{10... | collective-permute-start | bytes 2359304 | tf_op jit(solution)/shard_map/ppermute | solution.py:646
  164.3 19.7 %collective-permute-start.24 = (bf16[384,768]{1,0:T(8,128)(2,1)}, bf16[384,768]{1,0:T(8,128)(2,1)S(1)}, u32[]{:S(2)}, u32[]{:S(2)}) collective-permute-start(bf16[384,768]{1,0:T(8,128)(2,1)} %get-tuple-element.113.refs_1_), channel_id=1, source_target_pairs={{0,8},{8,0},{16,24},{24,16},{1,9},{9,1},{17,25},{25,17},{2,10},{10... | collective-permute-start | bytes 1769480 | tf_op jit(solution)/shard_map/ppermute | solution.py:646
  165.7 18.9 %collective-permute-start.26 = (bf16[384,768]{1,0:T(8,128)(2,1)}, bf16[384,768]{1,0:T(8,128)(2,1)S(1)}, u32[]{:S(2)}, u32[]{:S(2)}) collective-permute-start(bf16[384,768]{1,0:T(8,128)(2,1)} %get-tuple-element.115.refs_3_), channel_id=1, source_target_pairs={{0,8},{8,0},{16,24},{24,16},{1,9},{9,1},{17,25},{25,17},{2,10},{10... | collective-permute-start | bytes 1769480 | tf_op jit(solution)/shard_map/ppermute | solution.py:646
  183.5 17.0 %collective-permute-start.20 = (bf16[384,1024]{1,0:T(8,128)(2,1)S(1)}, bf16[384,1024]{1,0:T(8,128)(2,1)S(1)}, u32[]{:S(2)}, u32[]{:S(2)}) collective-permute-start(bf16[384,1024]{1,0:T(8,128)(2,1)S(1)} %collective-permute-done.19.refs_0_), channel_id=1, source_target_pairs={{0,8},{8,0},{16,24},{24,16},{1,9},{9,1},{17,25},{25,17},{2,10},{10... | collective-permute-start | bytes 2359304 | tf_op jit(solution)/shard_map/ppermute | solution.py:646
  183.5 16.9 %collective-permute-start.21 = (bf16[128,2560]{1,0:T(8,128)(2,1)}, bf16[128,2560]{1,0:T(8,128)(2,1)S(1)}, u32[]{:S(2)}, u32[]{:S(2)}) collective-permute-start(bf16[128,2560]{1,0:T(8,128)(2,1)} %copy-done.5), channel_id=1, source_target_pairs={{0,8},{8,0},{16,24},{24,16},{1,9},{9,1},{17,25},{25,17},{2,10},{10... | collective-permute-start | bytes 1966088 | tf_op jit(solution)/shard_map/ppermute | solution.py:646
  184.0 16.4 %collective-permute-start.17 = (bf16[384,768]{1,0:T(8,128)(2,1)}, bf16[384,768]{1,0:T(8,128)(2,1)S(1)}, u32[]{:S(2)}, u32[]{:S(2)}) collective-permute-start(bf16[384,768]{1,0:T(8,128)(2,1)} %get-tuple-element.113.refs_1_), channel_id=1, source_target_pairs={{0,16},{8,24},{16,0},{24,8},{1,17},{9,25},{17,1},{25,9},{2,18},{10... | collective-permute-start | bytes 1769480 | tf_op jit(solution)/shard_map/ppermute | solution.py:633
  184.5 27.6 %collective-permute-start.18 = (bf16[384,768]{1,0:T(8,128)(2,1)}, bf16[384,768]{1,0:T(8,128)(2,1)S(1)}, u32[]{:S(2)}, u32[]{:S(2)}) collective-permute-start(bf16[384,768]{1,0:T(8,128)(2,1)} %get-tuple-element.115.refs_3_), channel_id=1, source_target_pairs={{0,16},{8,24},{16,0},{24,8},{1,17},{9,25},{17,1},{25,9},{2,18},{10... | collective-permute-start | bytes 1769480 | tf_op jit(solution)/shard_map/ppermute | solution.py:633
  186.0 26.1 %collective-permute-start.29 = (bf16[512,1024]{1,0:T(8,128)(2,1)}, bf16[512,1024]{1,0:T(8,128)(2,1)S(1)}, u32[]{:S(2)}, u32[]{:S(2)}) collective-permute-start(bf16[512,1024]{1,0:T(8,128)(2,1)} %collective-permute-done.7.refs_0_), channel_id=1, source_target_pairs={{0,8},{8,0},{16,24},{24,16},{1,9},{9,1},{17,25},{25,17},{2,10},{10... | collective-permute-start | bytes 3145736 | tf_op jit(solution)/shard_map/ppermute | solution.py:646
  (29 other events, 218.8 us)

commit v3 on v2

--- a/solution.py
+++ b/solution.py
@@ -1,5 +1,3 @@
-import math
-
 import jax
 import jax.numpy as jnp
 from jax import lax
@@ -10,6 +8,7 @@
 F32 = jnp.float32
 BF16 = jnp.bfloat16
 MIB = 1 << 20
+LONG = 20_000_000_000
 VMEM = pl.BlockSpec(memory_space=pltpu.VMEM)
 SMEM = pl.BlockSpec(memory_space=pltpu.SMEM)
 HBM = pl.BlockSpec(memory_space=pltpu.HBM)
@@ -59,8 +58,7 @@
     return pltpu.HBM(tuple(dims), kind)
 
 
-def call(kernel, outs, operands, specs, flops, limit, scratch=(), name=None, aliases=None):
-    total = sum(math.prod(o.shape) * o.dtype.itemsize for o in (*outs, *operands))
+def call(kernel, outs, operands, specs, limit, scratch=(), name=None, aliases=None, weight=0):
     return pl.pallas_call(
         kernel,
         out_shape=tuple(outs),
@@ -69,7 +67,7 @@
         scratch_shapes=list(scratch),
         input_output_aliases=aliases or {},
         compiler_params=pltpu.CompilerParams(vmem_limit_bytes=limit * MIB),
-        cost_estimate=pl.CostEstimate(flops=int(flops), bytes_accessed=int(total), transcendentals=0),
+        cost_estimate=pl.CostEstimate(flops=weight, bytes_accessed=0, transcendentals=0),
         name=name,
     )(*operands)
 
@@ -138,7 +136,7 @@
     step = tile_of(width, 512)
 
     def kernel(ids_ref, tokens_hbm, routes_hbm, *refs):
-        blocks, (place_ref, pick_ref, tokens_ref, routes_ref, sems) = refs[:n_blocks], refs[n_blocks:]
+        blocks, (place_hbm, pick_hbm, place_ref, pick_ref, tokens_ref, routes_ref, sems) = refs[:n_blocks], refs[n_blocks:]
         copies = Copies(sems)
         routes_in = copies.start(routes_hbm, routes_ref)
         tokens_in = copies.start(tokens_hbm, tokens_ref)
@@ -164,21 +162,29 @@
             both += hit
             hit = (slot_ids == mine * capacity + slot).astype(F32)
             pick_ref[k * tok : (k + 1) * tok, :] = hit.T.astype(BF16)
+        copies.start(place_ref, place_hbm, True)
+        copies.start(pick_ref, pick_hbm, True)
         both = both.astype(BF16)
         tokens_in.wait()
         for n in range(0, width, step):
             cols = pl.ds(n, step)
             split(dot(both, tokens_ref[:, cols]).astype(BF16), blocks, cols)
+        copies.finish()
 
     outs = call(
         kernel,
         [on_chip((slots // n_blocks, width), BF16)] * n_blocks
-        + [on_chip((slots, pairs), BF16), on_chip((pairs, slots), BF16)],
+        + [in_hbm((slots, pairs), BF16), in_hbm((pairs, slots), BF16)],
         [ids, held(tokens), held(routes_t)],
         [SMEM, HBM, HBM],
-        2 * slots * tok * width,
         8,
-        [room(tokens), room(routes_t), pltpu.SemaphoreType.DMA((2,))],
+        [
+            pltpu.VMEM((slots, pairs), BF16),
+            pltpu.VMEM((pairs, slots), BF16),
+            room(tokens),
+            room(routes_t),
+            pltpu.SemaphoreType.DMA((4,)),
+        ],
         name="dispatch",
     )
     return list(outs[:n_blocks]), *outs[n_blocks:]
@@ -241,7 +247,6 @@
         ],
         [held(array) for array in (tokens, w_gate, w_up, w_down, keep_row)],
         [HBM] * 5,
-        6 * count * width * units,
         8,
         [
             room(keep_row),
@@ -251,6 +256,7 @@
             pltpu.SemaphoreType.DMA((8,)),
         ],
         name="forward_local",
+        weight=LONG,
     )
 
 
@@ -302,7 +308,6 @@
         + [on_chip((total, cores * part), BF16)] * (chips - 1),
         [ids] + [pinned(array) for array in (*blocks, tokens, local_hidden, w_gate, w_up, w_down)],
         [SMEM] + [VMEM] * (n_blocks + 5),
-        6 * count * width * units,
         16,
         [
             pltpu.VMEM((count, width), BF16),
@@ -349,7 +354,6 @@
         [on_chip((slots // n_blocks, width), BF16)] * n_blocks + [on_chip((tok, width), BF16)],
         [returned] + [held(array) for array in brought],
         [VMEM] + [HBM] * 6,
-        4 * slots * choose * tok * width,
         10,
         [room(array) for array in brought] + [pltpu.SemaphoreType.DMA((6,))],
         name="mix",
@@ -405,7 +409,6 @@
         + [on_chip((count, span + 2 * units), BF16)] * chips,
         [ids, pinned(cots)] + [held(array) for array in (silu, factor, w_gate, w_up, w_down, *kept)],
         [SMEM, VMEM] + [HBM] * (5 + n_kept),
-        6 * count * width * units,
         10,
         [
             pltpu.VMEM((count, width), F32),
@@ -416,6 +419,7 @@
             pltpu.SemaphoreType.DMA((6 + n_kept,)),
         ],
         name="backward_local",
+        weight=LONG,
     )
     return outs[0], outs[1:4], outs[4 : 4 + n_kept], list(outs[4 + n_kept :])
 
@@ -426,20 +430,25 @@
     count, span = n_blocks * size, cores * part
 
     def kernel(ids_ref, *refs):
-        ins, (rows_ref, *sent) = refs[:n_blocks], refs[n_blocks:]
+        ins, rows_ref, sent, (sent_ref, sems) = refs[:n_blocks], refs[n_blocks], refs[n_blocks + 1 : -2], refs[-2:]
+        copies = Copies(sems)
         for i, ref in enumerate(ins):
-            rows = pl.ds(i * size, size)
-            rows_ref[rows, :] = ref[...]
-            for shift, target in enumerate(sent, 1):
-                target[rows, :] = ref[:, chip_columns(ids_ref, shift, chips, cores, part)]
+            rows_ref[i * size : (i + 1) * size, :] = ref[...]
+            for shift in range(1, chips):
+                sent_ref[shift - 1, i * size : (i + 1) * size, :] = ref[
+                    :, chip_columns(ids_ref, shift, chips, cores, part)
+                ]
+        for shift, target in enumerate(sent):
+            copies.start(sent_ref.at[shift], target, True)
+        copies.finish()
 
     outs = call(
         kernel,
-        [on_chip((count, width), BF16)] + [on_chip((count, span), BF16)] * (chips - 1),
+        [on_chip((count, width), BF16)] + [in_hbm((count, span), BF16)] * (chips - 1),
         [ids] + [pinned(block) for block in blocks],
         [SMEM] + [VMEM] * n_blocks,
-        0,
         8,
+        [pltpu.VMEM((max(chips - 1, 1), count, span), BF16), pltpu.SemaphoreType.DMA((max(chips - 1, 1),))],
         name="collect",
     )
     return outs[0], list(outs[1:])
@@ -452,8 +461,9 @@
     f_tile, d_tile = tile_of(units, 256), tile_of(width, 512)
 
     def kernel(ids_ref, cots_ref, silu_ref, factor_ref, gate_ref, up_ref, down_ref, *refs):
-        back_hbm, gate_hbm, up_hbm, back_ref, gate_back, up_back, sems = refs
-        copies = Copies(sems)
+        back_hbm, gate_hbm, up_hbm, cots_hbm, back_ref, gate_back, up_back, sems = refs
+        copies = Copies(sems)
+        copies.start(cots_ref, cots_hbm, True)
         gradients(cots_ref[...], silu_ref, factor_ref, down_ref, gate_back, up_back, f_tile)
         copies.start(gate_back, gate_hbm, True)
         copies.start(up_back, up_hbm, True)
@@ -469,18 +479,23 @@
 
     return call(
         kernel,
-        [in_hbm((count, width), BF16), in_hbm((count, units), BF16), in_hbm((count, units), BF16)],
+        [
+            in_hbm((count, width), BF16),
+            in_hbm((count, units), BF16),
+            in_hbm((count, units), BF16),
+            in_hbm((count, width), BF16),
+        ],
         [ids] + [pinned(array) for array in (cots, silu, factor, w_gate, w_up, w_down)],
         [SMEM] + [VMEM] * 6,
-        6 * count * width * units,
         10,
         [
             pltpu.VMEM((count, width), BF16),
             pltpu.VMEM((count, units), BF16),
             pltpu.VMEM((count, units), BF16),
-            pltpu.SemaphoreType.DMA((2 + n_blocks * (width // d_tile),)),
+            pltpu.SemaphoreType.DMA((3 + n_blocks * (width // d_tile),)),
         ],
         name="backward",
+        weight=LONG,
     )
 
 
@@ -543,7 +558,6 @@
         [in_hbm((part, 3 * units), F32)],
         operands,
         [SMEM] + [HBM] * (len(operands) - 1),
-        sum(2 * rows * part * wide * units for rows, (*_, wide) in zip(rows_of, terms)),
         20,
         [pltpu.VMEM((rows, part), BF16) for rows in rows_of]
         + [pltpu.VMEM((rows, wide * units), BF16) for rows, (*_, wide) in zip(rows_of, terms)]
@@ -552,6 +566,7 @@
             pltpu.SemaphoreType.DMA((n_copies + len(begun) * len(sections) + len(sections) * (units // step),)),
         ],
         name="weight_sums",
+        weight=0,
         aliases={len(operands) - 1: 0} if begun else None,
     )
     return out
@@ -580,7 +595,6 @@
         [in_hbm((tok, width), BF16)],
         [returned, held(pick), held(local_back)],
         [VMEM, HBM, HBM],
-        2 * slots * tok * width,
         8,
         [
             room(pick),
@@ -657,26 +671,26 @@
     returned = at_once(out)
     x_far = to_chips(x_send)
     h_far = to_others(hidden)
-    returned, x_far, h_far = together((returned, x_far, h_far))
+    returned, x_far = together((returned, x_far))
     blocks, local_cot = mix(returned, place, pick, gates.T, keep_row, cotangent, local_out, n_blocks)
     blocks = step_by_step(blocks)
+    local_cot, h_far = together((local_cot, h_far))
     local_back, on, kept, l_send = backward_local(
         ids, local_cot, local_silu, local_factor, *weights, (silu, factor), chips, cores, part
     )
     l_own, l_far = l_send[0], to_chips(l_send[1:])
-    blocks, l_far = together((blocks, l_far))
     cots, c_send = collect(ids, blocks, chips, cores, part)
-    back, gate_back, up_back = backward(ids, cots, *kept, *on, n_blocks)
+    back, gate_back, up_back, cots = backward(ids, cots, *kept, *on, n_blocks)
     returned = at_once(back)
+    c_send, l_far = together((c_send, l_far))
     c_far = to_chips(c_send)
+    gate_back, c_far = together((gate_back, c_far))
     g_far = to_others(gate_back)
-    u_far = to_others(up_back)
-
-    def terms_x(xs, at, gs, us, ls):
+
+    def terms_x(xs, at, rights, ls, section):
         return [
             ([(x, at)], [(right, 0), (l, span + section * units)], section, 1)
-            for x, g, u, l in zip(xs, gs, us, ls)
-            for section, right in enumerate((g, u))
+            for x, right, l in zip(xs, rights, ls)
         ]
 
     def terms_c(cs, at, ls, hs):
@@ -687,36 +701,40 @@
 
     x_near, h_near, l_near = both_cores([rows]), both_cores([hidden]), both_cores([l_own])
     g_near, u_near, c_near = both_cores([gate_back]), both_cores([up_back]), both_cores([cots])
-    x_far, h_far, l_far = both_cores(x_far), both_cores(h_far), both_cores(l_far)
-    c_far, g_far = both_cores(c_far), both_cores(g_far)
     scale = 1.0 / replicas
+    token_grads = combine(returned, pick, local_back, choose)
     totals = weight_sums(
         ids,
         cores,
         part,
-        terms_x(x_near, WHOLE, g_near, u_near, l_near) + terms_c(c_near, WHOLE, l_near, h_near),
+        terms_x(x_near, WHOLE, g_near, l_near, 0)
+        + terms_x(x_near, WHOLE, u_near, l_near, 1)
+        + terms_c(c_near, WHOLE, l_near, h_near),
         None,
         units,
         (0, 1, 2),
-        None,
+        None if chips > 1 else scale,
     )
     if chips > 1:
+        up_back, g_far, totals = together((up_back, g_far, totals))
+        u_far = to_others(up_back)
+        x_far, h_far, l_far = both_cores(x_far), both_cores(h_far), both_cores(l_far)
+        c_far, g_far = both_cores(c_far), both_cores(g_far)
         totals = weight_sums(
-            ids, cores, part, terms_c(c_far, CHIP, l_far, h_far), totals, units, (2,), scale
+            ids,
+            cores,
+            part,
+            terms_x(x_far, CHIP, g_far, l_far, 0) + terms_c(c_far, CHIP, l_far, h_far),
+            totals,
+            units,
+            (2, 0),
+            scale,
         )
-        u_far, totals = together((u_far, totals))
-    u_far = both_cores(u_far)
-    totals = weight_sums(
-        ids,
-        cores,
-        part,
-        terms_x(x_far, CHIP, g_far, u_far, l_far),
-        totals,
-        units,
-        (0, 1) if chips > 1 else (0, 1, 2),
-        scale,
-    )
-    token_grads = combine(returned, pick, local_back, choose)
+        u_far, totals, token_grads = together((u_far, totals, token_grads))
+        u_far = both_cores(u_far)
+        totals = weight_sums(
+            ids, cores, part, terms_x(x_far, CHIP, u_far, l_far, 1), totals, units, (1,), scale
+        )
     return (token_grads, totals[None])
 
 

time: 225 us -> 204 us (0.907)
  starting transfers between devices: 72.5 us -> 61.1 us
  waiting for transfers between devices: 90.5 us -> 83.3 us
  local copies, waits for them, and re-layouts: 6.73 us -> 3.48 us
    ppermute x6, waiting for transfers between devices: 67.4 us -> 50.3 us  [to_chips(): lax.ppermute(array, 'dp', [(start * cores + i, (start + shift) % chips *...]
    ppermute x14, starting transfers between devices: 45.8 us -> 30.4 us  [step_by_step(): lax.ppermute(blocks[k], 'expert', [(i, (i + k) % groups) for i in range(g...]
    all_to_all x2, waiting for transfers between devices: 0.01 us -> 10 us  [at_once(): lax.all_to_all(block, 'expert', split_axis=0, concat_axis=0, tiled=True)]
    unnamed x38 -> x32, local copies, waits for them, and re-layouts: 6.73 us -> 3.48 us
  transfers between devices with their start and end apart: 34 -> 34, of which waited for: 14 -> 15; matrix products, arithmetic and copies ran while one was open for 0% -> 0% of each run, Pallas kernels for 19% -> 20%
where the time goes in v3:
time: 204 us
  waiting for transfers between devices  83.3 us (41%)
  starting transfers between devices  61.1 us (30%)
  Pallas kernels  54.9 us (27%)
  local copies, waits for them, and re-layouts  3.48 us (2%)
    pallas_call x11, Pallas kernels, call(): pl.pallas_call(kernel, out_shape=tuple(outs), in_specs=specs, out_specs=t...  54.9 us
    ppermute x6, waiting for transfers between devices, to_chips(): lax.ppermute(array, 'dp', [(start * cores + i, (start + shift) % chips *...  50.3 us
    ppermute x14, starting transfers between devices, step_by_step(): lax.ppermute(blocks[k], 'expert', [(i, (i + k) % groups) for i in range(g...  30.4 us
    all_to_all x2, starting transfers between devices, at_once(): lax.all_to_all(block, 'expert', split_axis=0, concat_axis=0, tiled=True)  20.4 us
    ppermute x14, waiting for transfers between devices, step_by_step(): lax.ppermute(blocks[k], 'expert', [(i, (i + k) % groups) for i in range(g...  19.8 us
    all_to_all x2, waiting for transfers between devices, at_once(): lax.all_to_all(block, 'expert', split_axis=0, concat_axis=0, tiled=True)  10 us
    ppermute x6, starting transfers between devices, to_chips(): lax.ppermute(array, 'dp', [(start * cores + i, (start + shift) % chips *...  8.11 us
  transfers between devices with their start and end apart: 34, of which 15 were waited for; matrix products, arithmetic and copies ran while one was open for 0% of the time, Pallas kernels for 20%

profile of v3, /device:TPU:0, one launch (start us, length us, event | category | flops | bytes accessed | tf_op | source)
XLA Modules:
  0.0 204.0 jit_solution(12584496516547362015)
XLA Ops:
  3.0 3.0 %collective-permute-start = (bf16[48,2048]{1,0:T(8,128)(2,1)S(1)}, bf16[48,2048]{1,0:T(8,128)(2,1)S(1)}, u32[]{:S(2)}, u32[]{:S(2)}) collective-permute-start(bf16[48,2048]{1,0:T(8,128)(2,1)S(1)} %get-tuple-element.64), channel_id=1, source_target_pairs={{0,1},{1,2},{2,3},{3,4},{4,5},{5,6},{6,7},{7,0},{8,9},{9,10},{10,1... | collective-permute-start | bytes 589832 | tf_op jit(solution)/shard_map/ppermute | solution.py:642
  7.6 2.5 %collective-permute-start.2 = (bf16[48,2048]{1,0:T(8,128)(2,1)S(1)}, bf16[48,2048]{1,0:T(8,128)(2,1)S(1)}, u32[]{:S(2)}, u32[]{:S(2)}) collective-permute-start(bf16[48,2048]{1,0:T(8,128)(2,1)S(1)} %get-tuple-element.66), channel_id=1, source_target_pairs={{0,3},{1,4},{2,5},{3,6},{4,7},{5,0},{6,1},{7,2},{8,11},{9,12},{10,... | collective-permute-start | bytes 589832 | tf_op jit(solution)/shard_map/ppermute | solution.py:642
  11.4 2.6 %collective-permute-start.4 = (bf16[48,2048]{1,0:T(8,128)(2,1)S(1)}, bf16[48,2048]{1,0:T(8,128)(2,1)S(1)}, u32[]{:S(2)}, u32[]{:S(2)}) collective-permute-start(bf16[48,2048]{1,0:T(8,128)(2,1)S(1)} %get-tuple-element.68), channel_id=1, source_target_pairs={{0,5},{1,6},{2,7},{3,0},{4,1},{5,2},{6,3},{7,4},{8,13},{9,14},{10,... | collective-permute-start | bytes 589832 | tf_op jit(solution)/shard_map/ppermute | solution.py:642
  16.8 3.4 %collective-permute-start.6 = (bf16[48,2048]{1,0:T(8,128)(2,1)S(1)}, bf16[48,2048]{1,0:T(8,128)(2,1)S(1)}, u32[]{:S(2)}, u32[]{:S(2)}) collective-permute-start(bf16[48,2048]{1,0:T(8,128)(2,1)S(1)} %get-tuple-element.70), channel_id=1, source_target_pairs={{0,7},{1,0},{2,1},{3,2},{4,3},{5,4},{6,5},{7,6},{8,15},{9,8},{10,9... | collective-permute-start | bytes 589832 | tf_op jit(solution)/shard_map/ppermute | solution.py:642
  20.2 5.7 %forward_local.1 = (f32[128,2048]{1,0:T(8,128)}, f32[128,768]{1,0:T(8,128)}, f32[128,768]{1,0:T(8,128)}, bf16[128,768]{1,0:T(8,128)(2,1)S(1)}, bf16[128,2048]{1,...) custom-call(bf16[128,2048]{1,0:T(8,128)(2,1)} %tokens_hbm.3, ...), custom_call_target="tpu_custom_call" | custom-call | flops 20000000000 | tf_op jit(solution)/shard_map/forward_local/pallas_call | solution.py:62
  26.0 5.0 %collective-permute-done.2.refs_3_ = bf16[48,2048]{1,0:T(8,128)(2,1)S(1)} collective-permute-done((bf16[48,2048]{1,0:T(8,128)(2,1)S(1)}, bf16[48,2048]{1,0:T(8,128)(2,1)S(1)}, u32[]{:S(2)}, u32[]{:S(2)}) %collective-permute-start.2) | collective-permute-done | bytes 196640 | tf_op jit(solution)/shard_map/ppermute | solution.py:642
  32.6 6.1 %forward.1 = (bf16[384,2048]{1,0:T(8,128)(2,1)}, bf16[512,2048]{1,0:T(8,128)(2,1)}, bf16[512,768]{1,0:T(8,128)(2,1)}, f32[384,768]{1,0:T(8,128)}, f32[384,768]{1,0:T(8,128)}, /*index=5*/bf16[512,1024]{1,0:T(8,128)(2,1)S(1)}) custom-call(s32[2]{0:T(128)S(1)} %pad_add_fusion.ids_ref, bf16[48,2048]{1,0:T(8,128)(2,1)S(1)} %get-tuple-element.63.refs_0_, ...), custom_call_target="tpu_custom_call" | custom-call | tf_op jit(solution)/shard_map/forward/pallas_call | solution.py:62
  38.7 15.0 %all-to-all-start = ((bf16[8,48,2048]{2,1,0:T(8,128)(2,1)}), bf16[8,48,2048]{2,1,0:T(8,128)(2,1)S(1)}, u32[]{:S(2)}, u32[]{:S(2)}) async-start(bf16[8,48,2048]{2,1,0:T(8,128)(2,1)} %bitcast.17), calls=%async_computation | async-start | bytes 3145728 | tf_op jit(solution)/shard_map/all_to_all | solution.py:634
  55.7 24.2 %collective-permute-done.7.refs_0_ = bf16[512,1024]{1,0:T(8,128)(2,1)} collective-permute-done((bf16[512,1024]{1,0:T(8,128)(2,1)S(1)}, bf16[512,1024]{1,0:T(8,128)(2,1)}, u32[]{:S(2)}, u32[]{:S(2)}) %collective-permute-start.7) | collective-permute-done | bytes 1048608 | tf_op jit(solution)/shard_map/ppermute | solution.py:647
  79.9 10.0 %all-to-all-done = bf16[8,48,2048]{2,1,0:T(8,128)(2,1)S(1)} async-done(((bf16[8,48,2048]{2,1,0:T(8,128)(2,1)}), bf16[8,48,2048]{2,1,0:T(8,128)(2,1)S(1)}, u32[]{:S(2)}, u32[]{:S(2)}) %all-to-all-start) | async-done | bytes 1572896 | tf_op jit(solution)/shard_map/all_to_all | solution.py:634
  89.9 3.5 %mix.1 = (bf16[48,2048]{1,0:T(8,128)(2,1)S(1)}, bf16[48,2048]{1,0:T(8,128)(2,1)S(1)}, bf16[48,2048]{1,0:T(8,128)(2,1)S(1)}, bf16[48,2048]{1,0:T(8,128)(2,1)S(1)}...) custom-call(bf16[384,2048]{1,0:T(8,128)(2,1)S(1)} %bitcast.14, ...), custom_call_target="tpu_custom_call" | custom-call | tf_op jit(solution)/shard_map/mix/pallas_call | solution.py:62
  93.5 2.8 %collective-permute-start.11 = (bf16[48,2048]{1,0:T(8,128)(2,1)S(1)}, bf16[48,2048]{1,0:T(8,128)(2,1)S(1)}, u32[]{:S(2)}, u32[]{:S(2)}) collective-permute-start(bf16[48,2048]{1,0:T(8,128)(2,1)S(1)} %get-tuple-element.86), channel_id=1, source_target_pairs={{0,4},{1,5},{2,6},{3,7},{4,0},{5,1},{6,2},{7,3},{8,12},{9,13},{10,... | collective-permute-start | bytes 589832 | tf_op jit(solution)/shard_map/ppermute | solution.py:642
  99.4 3.0 %collective-permute-start.14 = (bf16[48,2048]{1,0:T(8,128)(2,1)S(1)}, bf16[48,2048]{1,0:T(8,128)(2,1)S(1)}, u32[]{:S(2)}, u32[]{:S(2)}) collective-permute-start(bf16[48,2048]{1,0:T(8,128)(2,1)S(1)} %get-tuple-element.89), channel_id=1, source_target_pairs={{0,7},{1,0},{2,1},{3,2},{4,3},{5,4},{6,5},{7,6},{8,15},{9,8},{10,9... | collective-permute-start | bytes 589832 | tf_op jit(solution)/shard_map/ppermute | solution.py:642
  102.4 7.0 %collective-permute-done.10.refs_3_ = bf16[48,2048]{1,0:T(8,128)(2,1)S(1)} collective-permute-done((bf16[48,2048]{1,0:T(8,128)(2,1)S(1)}, bf16[48,2048]{1,0:T(8,128)(2,1)S(1)}, u32[]{:S(2)}, u32[]{:S(2)}) %collective-permute-start.10) | collective-permute-done | bytes 196640 | tf_op jit(solution)/shard_map/ppermute | solution.py:642
  109.5 5.2 %collective-permute-done.11.refs_4_ = bf16[48,2048]{1,0:T(8,128)(2,1)S(1)} collective-permute-done((bf16[48,2048]{1,0:T(8,128)(2,1)S(1)}, bf16[48,2048]{1,0:T(8,128)(2,1)S(1)}, u32[]{:S(2)}, u32[]{:S(2)}) %collective-permute-start.11) | collective-permute-done | bytes 196640 | tf_op jit(solution)/shard_map/ppermute | solution.py:642
  114.6 5.2 %collective-permute-start.9 = (bf16[48,2048]{1,0:T(8,128)(2,1)S(1)}, bf16[48,2048]{1,0:T(8,128)(2,1)S(1)}, u32[]{:S(2)}, u32[]{:S(2)}) collective-permute-start(bf16[48,2048]{1,0:T(8,128)(2,1)S(1)} %get-tuple-element.84), channel_id=1, source_target_pairs={{0,2},{1,3},{2,4},{3,5},{4,6},{5,7},{6,0},{7,1},{8,10},{9,11},{10,... | collective-permute-start | bytes 589832 | tf_op jit(solution)/shard_map/ppermute | solution.py:642
  119.8 7.7 %backward_local.1 = (f32[128,2048]{1,0:T(8,128)}, bf16[2048,768]{1,0:T(8,128)(2,1)S(1)}, bf16[2048,768]{1,0:T(8,128)(2,1)S(1)}, bf16[768,2048]{1,0:T(8,128)(2,1)...) custom-call(s32[2]{0:T(128)S(1)} %pad_add_fusion.ids_ref, ...), custom_call_target="tpu_custom_call" | custom-call | flops 20000000000 | tf_op jit(solution)/shard_map/backward_local/pallas_call | solution.py:62
  130.7 5.7 %backward.1 = (bf16[384,2048]{1,0:T(8,128)(2,1)}, bf16[384,768]{1,0:T(8,128)(2,1)}, bf16[384,768]{1,0:T(8,128)(2,1)}, bf16[384,2048]{1,0:T(8,128)(2,1)}) custom-call(s32[2]{0:T(128)S(1)} %pad_add_fusion.ids_ref, bf16[384,2048]{1,0:T(8,128)(2,1)S(1)} %get-tuple-element.90.cots_ref, f32[384,768]{1,0:T(8,128)S(1)} %get-tuple-element.98.silu_ref, ...), custom_call_target="tpu_custom_call" | custom-call | flops 20000000000 | tf_op jit(solution)/shard_map/backward/pallas_call | solution.py:62
  136.5 5.4 %all-to-all-start.1 = ((bf16[8,48,2048]{2,1,0:T(8,128)(2,1)}), bf16[8,48,2048]{2,1,0:T(8,128)(2,1)S(1)}, u32[]{:S(2)}, u32[]{:S(2)}) async-start(bf16[8,48,2048]{2,1,0:T(8,128)(2,1)} %bitcast.16), calls=%async_computation.1 | async-start | bytes 3145728 | tf_op jit(solution)/shard_map/all_to_all | solution.py:634
  146.8 17.3 %collective-permute-done.17.refs_6_ = bf16[384,1024]{1,0:T(8,128)(2,1)S(1)} collective-permute-done((bf16[384,1024]{1,0:T(8,128)(2,1)}, bf16[384,1024]{1,0:T(8,128)(2,1)S(1)}, u32[]{:S(2)}, u32[]{:S(2)}) %collective-permute-start.17) | collective-permute-done | bytes 786464 | tf_op jit(solution)/shard_map/ppermute | solution.py:647
  168.3 7.8 %weight_sums.3.refs_10_ = f32[512,2304]{1,0:T(8,128)} custom-call(s32[2]{0:T(128)S(1)} %pad_add_fusion.ids_ref, bf16[512,2048]{1,0:T(8,128)(2,1)} %get-tuple-element.109.refs_0_, bf16[384,768]{1,0:T(8,128)(2,1)} %get-tuple-element.108.refs_1_, bf16[128,2560]{1,0:T(8,128)(2,1)} %copy-done, bf16[512,2048]{1,0:T(8,128)(2,1)} %collective-permute-done.19.refs_3_, ...), custom_call_target="tpu_custom_call" | custom-call | tf_op jit(solution)/shard_map/weight_sums/pallas_call | solution.py:62
  176.2 4.0 %collective-permute-done.18.refs_1_ = bf16[384,768]{1,0:T(8,128)(2,1)S(1)} collective-permute-done((bf16[384,768]{1,0:T(8,128)(2,1)}, bf16[384,768]{1,0:T(8,128)(2,1)S(1)}, u32[]{:S(2)}, u32[]{:S(2)}) %collective-permute-start.18) | collective-permute-done | bytes 589856 | tf_op jit(solution)/shard_map/ppermute | solution.py:647
  184.0 7.1 %weight_sums.4.refs_6_ = f32[512,2304]{1,0:T(8,128)} custom-call(s32[2]{0:T(128)S(1)} %pad_add_fusion.ids_ref, bf16[512,1024]{1,0:T(8,128)(2,1)} %collective-permute-done.7.refs_0_, bf16[384,768]{1,0:T(8,128)(2,1)} %copy-done.10, bf16[128,2560]{1,0:T(8,128)(2,1)} %copy-done.2, bf16[512,1024]{1,0:T(8,128)(2,1)} %copy-done.1, ...), custom_call_target="tpu_custom_call", output_to_operand_aliasing={{}: (11, {})} | custom-call | tf_op jit(solution)/shard_map/weight_sums/pallas_call | solution.py:62
  199.0 4.8 %weight_sums.5 = f32[512,2304]{1,0:T(8,128)} custom-call(s32[2]{0:T(128)S(1)} %pad_add_fusion.ids_ref, bf16[512,1024]{1,0:T(8,128)(2,1)} %collective-permute-done.7.refs_0_, bf16[384,768]{1,0:T(8,128)(2,1)} %copy-done.12, bf16[128,2560]{1,0:T(8,128)(2,1)} %copy-done.2, bf16[512,1024]{1,0:T(8,128)(2,1)} %copy-done.1, ...), custom_call_target="tpu_custom_call", output_to_operand_aliasing={{}: (7, {})} | custom-call | tf_op jit(solution)/shard_map/weight_sums/pallas_call | solution.py:62
  (88 shorter events, 38.7 us)
Async XLA Ops:
  7.6 23.4 %collective-permute-start.2 = (bf16[48,2048]{1,0:T(8,128)(2,1)S(1)}, bf16[48,2048]{1,0:T(8,128)(2,1)S(1)}, u32[]{:S(2)}, u32[]{:S(2)}) collective-permute-start(bf16[48,2048]{1,0:T(8,128)(2,1)S(1)} %get-tuple-element.66), channel_id=1, source_target_pairs={{0,3},{1,4},{2,5},{3,6},{4,7},{5,0},{6,1},{7,2},{8,11},{9,12},{10,... | collective-permute-start | bytes 589832 | tf_op jit(solution)/shard_map/ppermute | solution.py:642
  10.1 21.1 %collective-permute-start.3 = (bf16[48,2048]{1,0:T(8,128)(2,1)S(1)}, bf16[48,2048]{1,0:T(8,128)(2,1)S(1)}, u32[]{:S(2)}, u32[]{:S(2)}) collective-permute-start(bf16[48,2048]{1,0:T(8,128)(2,1)S(1)} %get-tuple-element.67), channel_id=1, source_target_pairs={{0,4},{1,5},{2,6},{3,7},{4,0},{5,1},{6,2},{7,3},{8,12},{9,13},{10,... | collective-permute-start | bytes 589832 | tf_op jit(solution)/shard_map/ppermute | solution.py:642
  11.4 19.8 %collective-permute-start.4 = (bf16[48,2048]{1,0:T(8,128)(2,1)S(1)}, bf16[48,2048]{1,0:T(8,128)(2,1)S(1)}, u32[]{:S(2)}, u32[]{:S(2)}) collective-permute-start(bf16[48,2048]{1,0:T(8,128)(2,1)S(1)} %get-tuple-element.68), channel_id=1, source_target_pairs={{0,5},{1,6},{2,7},{3,0},{4,1},{5,2},{6,3},{7,4},{8,13},{9,14},{10,... | collective-permute-start | bytes 589832 | tf_op jit(solution)/shard_map/ppermute | solution.py:642
  15.0 16.2 %collective-permute-start.5 = (bf16[48,2048]{1,0:T(8,128)(2,1)S(1)}, bf16[48,2048]{1,0:T(8,128)(2,1)S(1)}, u32[]{:S(2)}, u32[]{:S(2)}) collective-permute-start(bf16[48,2048]{1,0:T(8,128)(2,1)S(1)} %get-tuple-element.69), channel_id=1, source_target_pairs={{0,6},{1,7},{2,0},{3,1},{4,2},{5,3},{6,4},{7,5},{8,14},{9,15},{10,... | collective-permute-start | bytes 589832 | tf_op jit(solution)/shard_map/ppermute | solution.py:642
  16.8 15.8 %collective-permute-start.6 = (bf16[48,2048]{1,0:T(8,128)(2,1)S(1)}, bf16[48,2048]{1,0:T(8,128)(2,1)S(1)}, u32[]{:S(2)}, u32[]{:S(2)}) collective-permute-start(bf16[48,2048]{1,0:T(8,128)(2,1)S(1)} %get-tuple-element.70), channel_id=1, source_target_pairs={{0,7},{1,0},{2,1},{3,2},{4,3},{5,4},{6,5},{7,6},{8,15},{9,8},{10,9... | collective-permute-start | bytes 589832 | tf_op jit(solution)/shard_map/ppermute | solution.py:642
  38.7 51.2 %all-to-all-start = ((bf16[8,48,2048]{2,1,0:T(8,128)(2,1)}), bf16[8,48,2048]{2,1,0:T(8,128)(2,1)S(1)}, u32[]{:S(2)}, u32[]{:S(2)}) async-start(bf16[8,48,2048]{2,1,0:T(8,128)(2,1)} %bitcast.17), calls=%async_computation | async-start | bytes 3145728 | tf_op jit(solution)/shard_map/all_to_all | solution.py:634
  53.7 26.2 %collective-permute-start.7 = (bf16[512,1024]{1,0:T(8,128)(2,1)S(1)}, bf16[512,1024]{1,0:T(8,128)(2,1)}, u32[]{:S(2)}, u32[]{:S(2)}) collective-permute-start(bf16[512,1024]{1,0:T(8,128)(2,1)S(1)} %get-tuple-element.77), channel_id=1, source_target_pairs={{0,16},{8,24},{16,0},{24,8},{1,17},{9,25},{17,1},{25,9},{2,18},{10... | collective-permute-start | bytes 3145736 | tf_op jit(solution)/shard_map/ppermute | solution.py:647
  55.2 41.1 %collective-permute-start.15 = (bf16[512,768]{1,0:T(8,128)(2,1)}, bf16[512,768]{1,0:T(8,128)(2,1)}, u32[]{:S(2)}, u32[]{:S(2)}) collective-permute-start(bf16[512,768]{1,0:T(8,128)(2,1)} %get-tuple-element.92.refs_9_), channel_id=1, source_target_pairs={{0,16},{8,24},{16,0},{24,8},{1,17},{9,25},{17,1},{25,9},{2,18},{10... | collective-permute-start | bytes 2359304 | tf_op jit(solution)/shard_map/ppermute | solution.py:647
  93.4 16.0 %collective-permute-start.10 = (bf16[48,2048]{1,0:T(8,128)(2,1)S(1)}, bf16[48,2048]{1,0:T(8,128)(2,1)S(1)}, u32[]{:S(2)}, u32[]{:S(2)}) collective-permute-start(bf16[48,2048]{1,0:T(8,128)(2,1)S(1)} %get-tuple-element.85), channel_id=1, source_target_pairs={{0,3},{1,4},{2,5},{3,6},{4,7},{5,0},{6,1},{7,2},{8,11},{9,12},{10,... | collective-permute-start | bytes 589832 | tf_op jit(solution)/shard_map/ppermute | solution.py:642
  93.5 21.2 %collective-permute-start.11 = (bf16[48,2048]{1,0:T(8,128)(2,1)S(1)}, bf16[48,2048]{1,0:T(8,128)(2,1)S(1)}, u32[]{:S(2)}, u32[]{:S(2)}) collective-permute-start(bf16[48,2048]{1,0:T(8,128)(2,1)S(1)} %get-tuple-element.86), channel_id=1, source_target_pairs={{0,4},{1,5},{2,6},{3,7},{4,0},{5,1},{6,2},{7,3},{8,12},{9,13},{10,... | collective-permute-start | bytes 589832 | tf_op jit(solution)/shard_map/ppermute | solution.py:642
  96.3 31.3 %collective-permute-start.12 = (bf16[48,2048]{1,0:T(8,128)(2,1)S(1)}, bf16[48,2048]{1,0:T(8,128)(2,1)S(1)}, u32[]{:S(2)}, u32[]{:S(2)}) collective-permute-start(bf16[48,2048]{1,0:T(8,128)(2,1)S(1)} %get-tuple-element.87), channel_id=1, source_target_pairs={{0,5},{1,6},{2,7},{3,0},{4,1},{5,2},{6,3},{7,4},{8,13},{9,14},{10,... | collective-permute-start | bytes 589832 | tf_op jit(solution)/shard_map/ppermute | solution.py:642
  97.9 29.7 %collective-permute-start.13 = (bf16[48,2048]{1,0:T(8,128)(2,1)S(1)}, bf16[48,2048]{1,0:T(8,128)(2,1)S(1)}, u32[]{:S(2)}, u32[]{:S(2)}) collective-permute-start(bf16[48,2048]{1,0:T(8,128)(2,1)S(1)} %get-tuple-element.88), channel_id=1, source_target_pairs={{0,6},{1,7},{2,0},{3,1},{4,2},{5,3},{6,4},{7,5},{8,14},{9,15},{10,... | collective-permute-start | bytes 589832 | tf_op jit(solution)/shard_map/ppermute | solution.py:642
  99.4 29.8 %collective-permute-start.14 = (bf16[48,2048]{1,0:T(8,128)(2,1)S(1)}, bf16[48,2048]{1,0:T(8,128)(2,1)S(1)}, u32[]{:S(2)}, u32[]{:S(2)}) collective-permute-start(bf16[48,2048]{1,0:T(8,128)(2,1)S(1)} %get-tuple-element.89), channel_id=1, source_target_pairs={{0,7},{1,0},{2,1},{3,2},{4,3},{5,4},{6,5},{7,6},{8,15},{9,8},{10,9... | collective-permute-start | bytes 589832 | tf_op jit(solution)/shard_map/ppermute | solution.py:642
  109.5 19.8 %collective-permute-start.8 = (bf16[48,2048]{1,0:T(8,128)(2,1)S(1)}, bf16[48,2048]{1,0:T(8,128)(2,1)S(1)}, u32[]{:S(2)}, u32[]{:S(2)}) collective-permute-start(bf16[48,2048]{1,0:T(8,128)(2,1)S(1)} %get-tuple-element.83), channel_id=1, source_target_pairs={{0,1},{1,2},{2,3},{3,4},{4,5},{5,6},{6,7},{7,0},{8,9},{9,10},{10,1... | collective-permute-start | bytes 589832 | tf_op jit(solution)/shard_map/ppermute | solution.py:642
  127.6 36.5 %collective-permute-start.19 = (bf16[512,2048]{1,0:T(8,128)(2,1)}, bf16[512,2048]{1,0:T(8,128)(2,1)}, u32[]{:S(2)}, u32[]{:S(2)}) collective-permute-start(bf16[512,2048]{1,0:T(8,128)(2,1)} %get-tuple-element.109.refs_0_), channel_id=1, source_target_pairs={{0,8},{8,0},{16,24},{24,16},{1,9},{9,1},{17,25},{25,17},{2,10},{10... | collective-permute-start | bytes 6291464 | tf_op jit(solution)/shard_map/ppermute | solution.py:660
  127.7 17.1 %collective-permute-start.16 = (bf16[128,2560]{1,0:T(8,128)(2,1)S(1)}, bf16[128,2560]{1,0:T(8,128)(2,1)S(1)}, u32[]{:S(2)}, u32[]{:S(2)}) collective-permute-start(bf16[128,2560]{1,0:T(8,128)(2,1)S(1)} %get-tuple-element.106), channel_id=1, source_target_pairs={{0,16},{8,24},{16,0},{24,8},{1,17},{9,25},{17,1},{25,9},{2,18},{10... | collective-permute-start | bytes 1966088 | tf_op jit(solution)/shard_map/ppermute | solution.py:647
  136.5 54.6 %all-to-all-start.1 = ((bf16[8,48,2048]{2,1,0:T(8,128)(2,1)}), bf16[8,48,2048]{2,1,0:T(8,128)(2,1)S(1)}, u32[]{:S(2)}, u32[]{:S(2)}) async-start(bf16[8,48,2048]{2,1,0:T(8,128)(2,1)} %bitcast.16), calls=%async_computation.1 | async-start | bytes 3145728 | tf_op jit(solution)/shard_map/all_to_all | solution.py:634
  141.9 24.2 %collective-permute-start.23 = (bf16[384,2048]{1,0:T(8,128)(2,1)}, bf16[384,2048]{1,0:T(8,128)(2,1)S(1)}, u32[]{:S(2)}, u32[]{:S(2)}) collective-permute-start(bf16[384,2048]{1,0:T(8,128)(2,1)} %get-tuple-element.111.refs_8_), channel_id=1, source_target_pairs={{0,8},{8,0},{16,24},{24,16},{1,9},{9,1},{17,25},{25,17},{2,10},{10... | collective-permute-start | bytes 4718600 | tf_op jit(solution)/shard_map/ppermute | solution.py:660
  144.8 19.3 %collective-permute-start.17 = (bf16[384,1024]{1,0:T(8,128)(2,1)}, bf16[384,1024]{1,0:T(8,128)(2,1)S(1)}, u32[]{:S(2)}, u32[]{:S(2)}) collective-permute-start(bf16[384,1024]{1,0:T(8,128)(2,1)} %get-tuple-element.107), channel_id=1, source_target_pairs={{0,16},{8,24},{16,0},{24,8},{1,17},{9,25},{17,1},{25,9},{2,18},{10... | collective-permute-start | bytes 2359304 | tf_op jit(solution)/shard_map/ppermute | solution.py:647
  146.3 18.3 %collective-permute-start.21 = (bf16[128,2560]{1,0:T(8,128)(2,1)S(1)}, bf16[128,2560]{1,0:T(8,128)(2,1)S(1)}, u32[]{:S(2)}, u32[]{:S(2)}) collective-permute-start(bf16[128,2560]{1,0:T(8,128)(2,1)S(1)} %get-tuple-element.110.refs_2_), channel_id=1, source_target_pairs={{0,8},{8,0},{16,24},{24,16},{1,9},{9,1},{17,25},{25,17},{2,10},{10... | collective-permute-start | bytes 1966088 | tf_op jit(solution)/shard_map/ppermute | solution.py:660
  146.3 19.8 %collective-permute-start.22 = (bf16[384,768]{1,0:T(8,128)(2,1)}, bf16[384,768]{1,0:T(8,128)(2,1)S(1)}, u32[]{:S(2)}, u32[]{:S(2)}) collective-permute-start(bf16[384,768]{1,0:T(8,128)(2,1)} %get-tuple-element.112.refs_6_), channel_id=1, source_target_pairs={{0,8},{8,0},{16,24},{24,16},{1,9},{9,1},{17,25},{25,17},{2,10},{10... | collective-permute-start | bytes 1769480 | tf_op jit(solution)/shard_map/ppermute | solution.py:660
  164.1 16.1 %collective-permute-start.30 = (bf16[512,768]{1,0:T(8,128)(2,1)}, bf16[512,768]{1,0:T(8,128)(2,1)S(1)}, u32[]{:S(2)}, u32[]{:S(2)}) collective-permute-start(bf16[512,768]{1,0:T(8,128)(2,1)} %collective-permute-done.15.refs_7_), channel_id=1, source_target_pairs={{0,8},{8,0},{16,24},{24,16},{1,9},{9,1},{17,25},{25,17},{2,10},{10... | collective-permute-start | bytes 2359304 | tf_op jit(solution)/shard_map/ppermute | solution.py:660
  166.1 15.6 %collective-permute-start.26 = (bf16[512,1024]{1,0:T(8,128)(2,1)}, bf16[512,1024]{1,0:T(8,128)(2,1)S(1)}, u32[]{:S(2)}, u32[]{:S(2)}) collective-permute-start(bf16[512,1024]{1,0:T(8,128)(2,1)} %collective-permute-done.7.refs_0_), channel_id=1, source_target_pairs={{0,8},{8,0},{16,24},{24,16},{1,9},{9,1},{17,25},{25,17},{2,10},{10... | collective-permute-start | bytes 3145736 | tf_op jit(solution)/shard_map/ppermute | solution.py:660
  180.2 16.0 %collective-permute-start.25 = (bf16[384,768]{1,0:T(8,128)(2,1)}, bf16[384,768]{1,0:T(8,128)(2,1)S(1)}, u32[]{:S(2)}, u32[]{:S(2)}) collective-permute-start(bf16[384,768]{1,0:T(8,128)(2,1)} %get-tuple-element.112.refs_6_), channel_id=1, source_target_pairs={{0,16},{8,24},{16,0},{24,8},{1,17},{9,25},{17,1},{25,9},{2,18},{10... | collective-permute-start | bytes 1769480 | tf_op jit(solution)/shard_map/ppermute | solution.py:647
  (26 other events, 196.0 us)

commit v4 on v3

--- a/solution.py
+++ b/solution.py
@@ -9,6 +9,10 @@
 BF16 = jnp.bfloat16
 MIB = 1 << 20
 LONG = 20_000_000_000
+BACK = 2_000_000_000
+SUMS = 5_000_000_000
+LATE = True
+LATE_ONES = (6, 1)
 VMEM = pl.BlockSpec(memory_space=pltpu.VMEM)
 SMEM = pl.BlockSpec(memory_space=pltpu.SMEM)
 HBM = pl.BlockSpec(memory_space=pltpu.HBM)
@@ -424,45 +428,50 @@
     return outs[0], outs[1:4], outs[4 : 4 + n_kept], list(outs[4 + n_kept :])
 
 
-def collect(ids, blocks, chips, cores, part):
+def cut(ids, blocks, chips, cores, part):
     n_blocks = len(blocks)
     size, width = blocks[0].shape
     count, span = n_blocks * size, cores * part
+    if chips == 1:
+        return []
 
     def kernel(ids_ref, *refs):
-        ins, rows_ref, sent, (sent_ref, sems) = refs[:n_blocks], refs[n_blocks], refs[n_blocks + 1 : -2], refs[-2:]
+        ins, sent, (sent_ref, sems) = refs[:n_blocks], refs[n_blocks:-2], refs[-2:]
+        copies = Copies(sems)
+        for shift, target in enumerate(sent, 1):
+            for i, ref in enumerate(ins):
+                columns = chip_columns(ids_ref, shift, chips, cores, part)
+                sent_ref[shift - 1, i * size : (i + 1) * size, :] = ref[:, columns]
+            copies.start(sent_ref.at[shift - 1], target, True)
+        copies.finish()
+
+    return list(
+        call(
+            kernel,
+            [in_hbm((count, span), BF16)] * (chips - 1),
+            [ids] + [pinned(block) for block in blocks],
+            [SMEM] + [VMEM] * n_blocks,
+            8,
+            [pltpu.VMEM((chips - 1, count, span), BF16), pltpu.SemaphoreType.DMA((chips - 1,))],
+            name="cut",
+        )
+    )
+
+
+def backward(ids, blocks, silu, factor, w_gate, w_up, w_down):
+    n_blocks = len(blocks)
+    size, width = blocks[0].shape
+    count = n_blocks * size
+    units = w_gate.shape[1]
+    f_tile, d_tile = tile_of(units, 256), tile_of(width, 512)
+
+    def kernel(ids_ref, *refs):
+        ins, refs = refs[:n_blocks], refs[n_blocks:]
+        silu_ref, factor_ref, gate_ref, up_ref, down_ref, back_hbm, gate_hbm, up_hbm, cots_hbm = refs[:9]
+        cots_ref, back_ref, gate_back, up_back, sems = refs[9:]
         copies = Copies(sems)
         for i, ref in enumerate(ins):
-            rows_ref[i * size : (i + 1) * size, :] = ref[...]
-            for shift in range(1, chips):
-                sent_ref[shift - 1, i * size : (i + 1) * size, :] = ref[
-                    :, chip_columns(ids_ref, shift, chips, cores, part)
-                ]
-        for shift, target in enumerate(sent):
-            copies.start(sent_ref.at[shift], target, True)
-        copies.finish()
-
-    outs = call(
-        kernel,
-        [on_chip((count, width), BF16)] + [in_hbm((count, span), BF16)] * (chips - 1),
-        [ids] + [pinned(block) for block in blocks],
-        [SMEM] + [VMEM] * n_blocks,
-        8,
-        [pltpu.VMEM((max(chips - 1, 1), count, span), BF16), pltpu.SemaphoreType.DMA((max(chips - 1, 1),))],
-        name="collect",
-    )
-    return outs[0], list(outs[1:])
-
-
-def backward(ids, cots, silu, factor, w_gate, w_up, w_down, n_blocks):
-    count, width = cots.shape
-    units = w_gate.shape[1]
-    size = count // n_blocks
-    f_tile, d_tile = tile_of(units, 256), tile_of(width, 512)
-
-    def kernel(ids_ref, cots_ref, silu_ref, factor_ref, gate_ref, up_ref, down_ref, *refs):
-        back_hbm, gate_hbm, up_hbm, cots_hbm, back_ref, gate_back, up_back, sems = refs
-        copies = Copies(sems)
+            cots_ref[i * size : (i + 1) * size, :] = ref[...]
         copies.start(cots_ref, cots_hbm, True)
         gradients(cots_ref[...], silu_ref, factor_ref, down_ref, gate_back, up_back, f_tile)
         copies.start(gate_back, gate_hbm, True)
@@ -485,24 +494,25 @@
             in_hbm((count, units), BF16),
             in_hbm((count, width), BF16),
         ],
-        [ids] + [pinned(array) for array in (cots, silu, factor, w_gate, w_up, w_down)],
-        [SMEM] + [VMEM] * 6,
-        10,
-        [
+        [ids] + [pinned(array) for array in (*blocks, silu, factor, w_gate, w_up, w_down)],
+        [SMEM] + [VMEM] * (n_blocks + 5),
+        12,
+        [
+            pltpu.VMEM((count, width), BF16),
             pltpu.VMEM((count, width), BF16),
             pltpu.VMEM((count, units), BF16),
             pltpu.VMEM((count, units), BF16),
             pltpu.SemaphoreType.DMA((3 + n_blocks * (width // d_tile),)),
         ],
         name="backward",
-        weight=LONG,
+        weight=BACK,
     )
 
 
 WHOLE, CHIP = -1, -2
 
 
-def weight_sums(ids, cores, part, terms, previous, units, sections, scale):
+def weight_sums(ids, cores, part, terms, previous, units, sections, scale, at_hand=()):
     step = tile_of(units, 256)
     begun = [] if previous is None else [previous]
     arrays = []
@@ -552,12 +562,13 @@
                 copies.start(out_ref.at[:, cols], out_hbm.at[:, cols], True)
         copies.finish()
 
-    operands = [ids] + [held(array) for array in (*arrays, *begun)]
+    here = [any(array is other for other in at_hand) for array in (*arrays, *begun)]
+    operands = [ids] + [pinned(a) if on else held(a) for a, on in zip((*arrays, *begun), here)]
     (out,) = call(
         kernel,
         [in_hbm((part, 3 * units), F32)],
         operands,
-        [SMEM] + [HBM] * (len(operands) - 1),
+        [SMEM] + [VMEM if on else HBM for on in here],
         20,
         [pltpu.VMEM((rows, part), BF16) for rows in rows_of]
         + [pltpu.VMEM((rows, wide * units), BF16) for rows, (*_, wide) in zip(rows_of, terms)]
@@ -566,7 +577,7 @@
             pltpu.SemaphoreType.DMA((n_copies + len(begun) * len(sections) + len(sections) * (units // step),)),
         ],
         name="weight_sums",
-        weight=0,
+        weight=SUMS if len(sections) > 1 else 0,
         aliases={len(operands) - 1: 0} if begun else None,
     )
     return out
@@ -628,19 +639,20 @@
     keep_row = keep[None]
     together = lax.optimization_barrier
     far_first = sorted(range(1, groups), key=lambda k: abs(k - groups / 2))
+    late = [k for k in LATE_ONES if k < groups - 1]
 
     def at_once(block):
         block = block.reshape(groups, capacity, -1)
         moved = lax.all_to_all(block, "expert", split_axis=0, concat_axis=0, tiled=True)
         return moved.reshape(slots, -1)
 
-    def step_by_step(blocks):
-        if not apart:
-            return [at_once(blocks[0])]
-        moved = [blocks[0]] + [None] * (groups - 1)
-        for k in far_first:
-            moved[k] = lax.ppermute(blocks[k], "expert", [(i, (i + k) % groups) for i in range(groups)])
-        return moved
+    def steps(blocks, ks):
+        return {
+            k: lax.ppermute(blocks[k], "expert", [(i, (i + k) % groups) for i in range(groups)]) for k in ks
+        }
+
+    def arranged(own, moved):
+        return [own] + [moved[k] for k in range(1, groups)]
 
     def to_chips(arrays):
         return [
@@ -663,7 +675,7 @@
         return to_chips([array] * (chips - 1))
 
     blocks, place, pick = dispatch(ids, tokens, routes.T, groups, capacity, n_blocks)
-    blocks = step_by_step(blocks)
+    blocks = arranged(blocks[0], steps(blocks, far_first)) if apart else [at_once(blocks[0])]
     local_out, local_silu, local_factor, local_hidden, tokens_on, *on = forward_local(tokens, *weights, keep_row)
     out, rows, hidden, silu, factor, x_send = forward(
         ids, blocks, tokens_on, local_hidden, *on, chips, cores, part
@@ -673,14 +685,25 @@
     h_far = to_others(hidden)
     returned, x_far = together((returned, x_far))
     blocks, local_cot = mix(returned, place, pick, gates.T, keep_row, cotangent, local_out, n_blocks)
-    blocks = step_by_step(blocks)
-    local_cot, h_far = together((local_cot, h_far))
+    if apart:
+        moved = steps(blocks, [k for k in far_first if k not in late])
+        local_cot, h_far, moved[groups - 1] = together((local_cot, h_far, moved[groups - 1]))
+    else:
+        local_cot, h_far = together((local_cot, h_far))
     local_back, on, kept, l_send = backward_local(
         ids, local_cot, local_silu, local_factor, *weights, (silu, factor), chips, cores, part
     )
+    if apart:
+        if LATE:
+            l_send, later = together((l_send, {k: blocks[k] for k in late}))
+        else:
+            later = blocks
+        blocks = arranged(blocks[0], moved | steps(later, late))
+    else:
+        blocks = [at_once(blocks[0])]
     l_own, l_far = l_send[0], to_chips(l_send[1:])
-    cots, c_send = collect(ids, blocks, chips, cores, part)
-    back, gate_back, up_back, cots = backward(ids, cots, *kept, *on, n_blocks)
+    c_send = cut(ids, blocks, chips, cores, part)
+    back, gate_back, up_back, cots = backward(ids, blocks, *kept, *on)
     returned = at_once(back)
     c_send, l_far = together((c_send, l_far))
     c_far = to_chips(c_send)
@@ -731,9 +754,10 @@
             scale,
         )
         u_far, totals, token_grads = together((u_far, totals, token_grads))
-        u_far = both_cores(u_far)
+        u_other = from_sibling(u_far)
+        u_far = u_far + u_other
         totals = weight_sums(
-            ids, cores, part, terms_x(x_far, CHIP, u_far, l_far, 1), totals, units, (1,), scale
+            ids, cores, part, terms_x(x_far, CHIP, u_far, l_far, 1), totals, units, (1,), scale, u_other
         )
     return (token_grads, totals[None])
 

time: 204 us -> 197 us (0.966)
  starting transfers between devices: 61.1 us -> 56.5 us
  waiting for transfers between devices: 83.3 us -> 81.2 us
    ppermute x6, waiting for transfers between devices: 50.3 us -> 43.5 us  [to_chips(): lax.ppermute(array, 'dp', [(start * cores + i, (start + shift) % chips *...]
    ppermute x14, waiting for transfers between devices: 19.8 us -> 24.9 us  [steps(): lax.ppermute(blocks[k], 'expert', [(i, (i + k) % groups) for i in range(g...]
    ppermute x14, starting transfers between devices: 30.4 us -> 25.9 us  [steps(): lax.ppermute(blocks[k], 'expert', [(i, (i + k) % groups) for i in range(g...]
  transfers between devices with their start and end apart: 34 -> 34, of which waited for: 15 -> 17; matrix products, arithmetic and copies ran while one was open for 0% -> 0% of each run, Pallas kernels for 20% -> 21%
where the time goes in v4:
time: 197 us; the launch traced here: 196 us
  waiting for transfers between devices  81.2 us (41%)
  starting transfers between devices  56.5 us (29%)
  Pallas kernels  54.7 us (28%)
  local copies, waits for them, and re-layouts  2.54 us (1%)
    pallas_call x11, Pallas kernels, call(): pl.pallas_call(kernel, out_shape=tuple(outs), in_specs=specs, out_specs=t...  54.7 us
    ppermute x6, waiting for transfers between devices, to_chips(): lax.ppermute(array, 'dp', [(start * cores + i, (start + shift) % chips *...  43.5 us
    ppermute x14, starting transfers between devices, steps(): lax.ppermute(blocks[k], 'expert', [(i, (i + k) % groups) for i in range(g...  25.9 us
    ppermute x14, waiting for transfers between devices, steps(): lax.ppermute(blocks[k], 'expert', [(i, (i + k) % groups) for i in range(g...  24.9 us
    all_to_all x2, starting transfers between devices, at_once(): lax.all_to_all(block, 'expert', split_axis=0, concat_axis=0, tiled=True)  20.8 us
    all_to_all x2, waiting for transfers between devices, at_once(): lax.all_to_all(block, 'expert', split_axis=0, concat_axis=0, tiled=True)  10 us
    ppermute x6, starting transfers between devices, to_chips(): lax.ppermute(array, 'dp', [(start * cores + i, (start + shift) % chips *...  8.19 us
  transfers between devices with their start and end apart: 34, of which 17 were waited for; matrix products, arithmetic and copies ran while one was open for 0% of the time, Pallas kernels for 21%

profile of v4, /device:TPU:0, one launch (start us, length us, event | category | flops | bytes accessed | tf_op | source)
XLA Modules:
  0.0 196.0 jit_solution(15936117677095068171)
XLA Ops:
  3.0 3.0 %collective-permute-start = (bf16[48,2048]{1,0:T(8,128)(2,1)S(1)}, bf16[48,2048]{1,0:T(8,128)(2,1)S(1)}, u32[]{:S(2)}, u32[]{:S(2)}) collective-permute-start(bf16[48,2048]{1,0:T(8,128)(2,1)S(1)} %get-tuple-element.67), channel_id=1, source_target_pairs={{0,1},{1,2},{2,3},{3,4},{4,5},{5,6},{6,7},{7,0},{8,9},{9,10},{10,1... | collective-permute-start | bytes 589832 | tf_op jit(solution)/shard_map/ppermute | solution.py:651
  7.6 2.5 %collective-permute-start.2 = (bf16[48,2048]{1,0:T(8,128)(2,1)S(1)}, bf16[48,2048]{1,0:T(8,128)(2,1)S(1)}, u32[]{:S(2)}, u32[]{:S(2)}) collective-permute-start(bf16[48,2048]{1,0:T(8,128)(2,1)S(1)} %get-tuple-element.69), channel_id=1, source_target_pairs={{0,3},{1,4},{2,5},{3,6},{4,7},{5,0},{6,1},{7,2},{8,11},{9,12},{10,... | collective-permute-start | bytes 589832 | tf_op jit(solution)/shard_map/ppermute | solution.py:651
  11.3 2.6 %collective-permute-start.4 = (bf16[48,2048]{1,0:T(8,128)(2,1)S(1)}, bf16[48,2048]{1,0:T(8,128)(2,1)S(1)}, u32[]{:S(2)}, u32[]{:S(2)}) collective-permute-start(bf16[48,2048]{1,0:T(8,128)(2,1)S(1)} %get-tuple-element.71), channel_id=1, source_target_pairs={{0,5},{1,6},{2,7},{3,0},{4,1},{5,2},{6,3},{7,4},{8,13},{9,14},{10,... | collective-permute-start | bytes 589832 | tf_op jit(solution)/shard_map/ppermute | solution.py:651
  16.8 3.4 %collective-permute-start.6 = (bf16[48,2048]{1,0:T(8,128)(2,1)S(1)}, bf16[48,2048]{1,0:T(8,128)(2,1)S(1)}, u32[]{:S(2)}, u32[]{:S(2)}) collective-permute-start(bf16[48,2048]{1,0:T(8,128)(2,1)S(1)} %get-tuple-element.73), channel_id=1, source_target_pairs={{0,7},{1,0},{2,1},{3,2},{4,3},{5,4},{6,5},{7,6},{8,15},{9,8},{10,9... | collective-permute-start | bytes 589832 | tf_op jit(solution)/shard_map/ppermute | solution.py:651
  20.2 5.7 %forward_local.1 = (f32[128,2048]{1,0:T(8,128)}, f32[128,768]{1,0:T(8,128)}, f32[128,768]{1,0:T(8,128)}, bf16[128,768]{1,0:T(8,128)(2,1)S(1)}, bf16[128,2048]{1,...) custom-call(bf16[128,2048]{1,0:T(8,128)(2,1)} %tokens_hbm.3, ...), custom_call_target="tpu_custom_call" | custom-call | flops 20000000000 | tf_op jit(solution)/shard_map/forward_local/pallas_call | solution.py:66
  25.9 5.0 %collective-permute-done.2.refs_3_ = bf16[48,2048]{1,0:T(8,128)(2,1)S(1)} collective-permute-done((bf16[48,2048]{1,0:T(8,128)(2,1)S(1)}, bf16[48,2048]{1,0:T(8,128)(2,1)S(1)}, u32[]{:S(2)}, u32[]{:S(2)}) %collective-permute-start.2) | collective-permute-done | bytes 196640 | tf_op jit(solution)/shard_map/ppermute | solution.py:651
  32.6 6.1 %forward.1 = (bf16[384,2048]{1,0:T(8,128)(2,1)}, bf16[512,2048]{1,0:T(8,128)(2,1)}, bf16[512,768]{1,0:T(8,128)(2,1)}, f32[384,768]{1,0:T(8,128)}, f32[384,768]{1,0:T(8,128)}, /*index=5*/bf16[512,1024]{1,0:T(8,128)(2,1)S(1)}) custom-call(s32[2]{0:T(128)S(1)} %pad_add_fusion.ids_ref, bf16[48,2048]{1,0:T(8,128)(2,1)S(1)} %get-tuple-element.66.refs_0_, ...), custom_call_target="tpu_custom_call" | custom-call | tf_op jit(solution)/shard_map/forward/pallas_call | solution.py:66
  38.7 15.0 %all-to-all-start = ((bf16[8,48,2048]{2,1,0:T(8,128)(2,1)}), bf16[8,48,2048]{2,1,0:T(8,128)(2,1)S(1)}, u32[]{:S(2)}, u32[]{:S(2)}) async-start(bf16[8,48,2048]{2,1,0:T(8,128)(2,1)} %bitcast.17), calls=%async_computation | async-start | bytes 3145728 | tf_op jit(solution)/shard_map/all_to_all | solution.py:646
  55.7 24.2 %collective-permute-done.7.refs_0_ = bf16[512,1024]{1,0:T(8,128)(2,1)} collective-permute-done((bf16[512,1024]{1,0:T(8,128)(2,1)S(1)}, bf16[512,1024]{1,0:T(8,128)(2,1)}, u32[]{:S(2)}, u32[]{:S(2)}) %collective-permute-start.7) | collective-permute-done | bytes 1048608 | tf_op jit(solution)/shard_map/ppermute | solution.py:659
  79.9 10.0 %all-to-all-done = bf16[8,48,2048]{2,1,0:T(8,128)(2,1)S(1)} async-done(((bf16[8,48,2048]{2,1,0:T(8,128)(2,1)}), bf16[8,48,2048]{2,1,0:T(8,128)(2,1)S(1)}, u32[]{:S(2)}, u32[]{:S(2)}) %all-to-all-start) | async-done | bytes 1572896 | tf_op jit(solution)/shard_map/all_to_all | solution.py:646
  89.9 3.5 %mix.1 = (bf16[48,2048]{1,0:T(8,128)(2,1)S(1)}, bf16[48,2048]{1,0:T(8,128)(2,1)S(1)}, bf16[48,2048]{1,0:T(8,128)(2,1)S(1)}, bf16[48,2048]{1,0:T(8,128)(2,1)S(1)}...) custom-call(bf16[384,2048]{1,0:T(8,128)(2,1)S(1)} %bitcast.14, ...), custom_call_target="tpu_custom_call" | custom-call | tf_op jit(solution)/shard_map/mix/pallas_call | solution.py:66
  96.2 3.1 %collective-permute-start.13 = (bf16[48,2048]{1,0:T(8,128)(2,1)S(1)}, bf16[48,2048]{1,0:T(8,128)(2,1)S(1)}, u32[]{:S(2)}, u32[]{:S(2)}) collective-permute-start(bf16[48,2048]{1,0:T(8,128)(2,1)S(1)} %get-tuple-element.101), channel_id=1, source_target_pairs={{0,4},{1,5},{2,6},{3,7},{4,0},{5,1},{6,2},{7,3},{8,12},{9,13},{10,... | collective-permute-start | bytes 589832 | tf_op jit(solution)/shard_map/ppermute | solution.py:651
  101.0 7.7 %backward_local.1 = (f32[128,2048]{1,0:T(8,128)}, bf16[2048,768]{1,0:T(8,128)(2,1)S(1)}, bf16[2048,768]{1,0:T(8,128)(2,1)S(1)}, bf16[768,2048]{1,0:T(8,128)(2,1)...) custom-call(s32[2]{0:T(128)S(1)} %pad_add_fusion.ids_ref, ...), custom_call_target="tpu_custom_call" | custom-call | flops 20000000000 | tf_op jit(solution)/shard_map/backward_local/pallas_call | solution.py:66
  110.3 6.5 %collective-permute-done.12.refs_3_ = bf16[48,2048]{1,0:T(8,128)(2,1)S(1)} collective-permute-done((bf16[48,2048]{1,0:T(8,128)(2,1)S(1)}, bf16[48,2048]{1,0:T(8,128)(2,1)S(1)}, u32[]{:S(2)}, u32[]{:S(2)}) %collective-permute-start.12) | collective-permute-done | bytes 196640 | tf_op jit(solution)/shard_map/ppermute | solution.py:651
  116.8 4.9 %collective-permute-done.13.refs_4_ = bf16[48,2048]{1,0:T(8,128)(2,1)S(1)} collective-permute-done((bf16[48,2048]{1,0:T(8,128)(2,1)S(1)}, bf16[48,2048]{1,0:T(8,128)(2,1)S(1)}, u32[]{:S(2)}, u32[]{:S(2)}) %collective-permute-start.13) | collective-permute-done | bytes 196640 | tf_op jit(solution)/shard_map/ppermute | solution.py:651
  121.7 3.7 %collective-permute-start.15 = (bf16[48,2048]{1,0:T(8,128)(2,1)S(1)}, bf16[48,2048]{1,0:T(8,128)(2,1)S(1)}, u32[]{:S(2)}, u32[]{:S(2)}) collective-permute-start(bf16[48,2048]{1,0:T(8,128)(2,1)S(1)} %get-tuple-element.103), channel_id=1, source_target_pairs={{0,6},{1,7},{2,0},{3,1},{4,2},{5,3},{6,4},{7,5},{8,14},{9,15},{10,... | collective-permute-start | bytes 589832 | tf_op jit(solution)/shard_map/ppermute | solution.py:651
  125.4 4.1 %collective-permute-done.14.refs_5_ = bf16[48,2048]{1,0:T(8,128)(2,1)S(1)} collective-permute-done((bf16[48,2048]{1,0:T(8,128)(2,1)S(1)}, bf16[48,2048]{1,0:T(8,128)(2,1)S(1)}, u32[]{:S(2)}, u32[]{:S(2)}) %collective-permute-start.14) | collective-permute-done | bytes 196640 | tf_op jit(solution)/shard_map/ppermute | solution.py:651
  129.6 5.7 %backward.1 = (bf16[384,2048]{1,0:T(8,128)(2,1)}, bf16[384,768]{1,0:T(8,128)(2,1)}, bf16[384,768]{1,0:T(8,128)(2,1)}, bf16[384,2048]{1,0:T(8,128)(2,1)}) custom-call(s32[2]{0:T(128)S(1)} %pad_add_fusion.ids_ref, bf16[48,2048]{1,0:T(8,128)(2,1)S(1)} %get-tuple-element.85.refs_0_, bf16[48,2048]{1,0:T(8,128)(2,1)S(1)} %collective-permute-done.10.refs_1_, ...), custom_call_target="tpu_custom_call" | custom-call | flops 2000000000 | tf_op jit(solution)/shard_map/backward/pallas_call | solution.py:66
  138.8 5.8 %all-to-all-start.1 = ((bf16[8,48,2048]{2,1,0:T(8,128)(2,1)}), bf16[8,48,2048]{2,1,0:T(8,128)(2,1)S(1)}, u32[]{:S(2)}, u32[]{:S(2)}) async-start(bf16[8,48,2048]{2,1,0:T(8,128)(2,1)} %bitcast.16), calls=%async_computation.1 | async-start | bytes 3145728 | tf_op jit(solution)/shard_map/all_to_all | solution.py:646
  144.7 12.6 %collective-permute-done.17.refs_6_ = bf16[384,1024]{1,0:T(8,128)(2,1)} collective-permute-done((bf16[384,1024]{1,0:T(8,128)(2,1)}, bf16[384,1024]{1,0:T(8,128)(2,1)}, u32[]{:S(2)}, u32[]{:S(2)}) %collective-permute-start.17) | collective-permute-done | bytes 786464 | tf_op jit(solution)/shard_map/ppermute | solution.py:659
  161.0 7.8 %weight_sums.3.refs_10_ = f32[512,2304]{1,0:T(8,128)} custom-call(s32[2]{0:T(128)S(1)} %pad_add_fusion.ids_ref, bf16[512,2048]{1,0:T(8,128)(2,1)} %get-tuple-element.115.refs_0_, bf16[384,768]{1,0:T(8,128)(2,1)} %get-tuple-element.114.refs_1_, bf16[128,2560]{1,0:T(8,128)(2,1)} %copy-done, bf16[512,2048]{1,0:T(8,128)(2,1)} %collective-permute-done.19.refs_3_, ...), custom_call_target="tpu_custom_call" | custom-call | flops 5000000000 | tf_op jit(solution)/shard_map/weight_sums/pallas_call | solution.py:66
  168.9 4.3 %collective-permute-done.18.refs_1_ = bf16[384,768]{1,0:T(8,128)(2,1)S(1)} collective-permute-done((bf16[384,768]{1,0:T(8,128)(2,1)S(1)}, bf16[384,768]{1,0:T(8,128)(2,1)S(1)}, u32[]{:S(2)}, u32[]{:S(2)}) %collective-permute-start.18) | collective-permute-done | bytes 589856 | tf_op jit(solution)/shard_map/ppermute | solution.py:659
  177.0 7.1 %weight_sums.4.refs_6_ = f32[512,2304]{1,0:T(8,128)} custom-call(s32[2]{0:T(128)S(1)} %pad_add_fusion.ids_ref, bf16[512,1024]{1,0:T(8,128)(2,1)} %collective-permute-done.7.refs_0_, bf16[384,768]{1,0:T(8,128)(2,1)} %copy-done.10, bf16[128,2560]{1,0:T(8,128)(2,1)} %copy-done.2, bf16[512,1024]{1,0:T(8,128)(2,1)} %copy-done.1, ...), custom_call_target="tpu_custom_call", output_to_operand_aliasing={{}: (11, {})} | custom-call | flops 5000000000 | tf_op jit(solution)/shard_map/weight_sums/pallas_call | solution.py:66
  191.1 4.7 %weight_sums.5 = f32[512,2304]{1,0:T(8,128)} custom-call(s32[2]{0:T(128)S(1)} %pad_add_fusion.ids_ref, bf16[512,1024]{1,0:T(8,128)(2,1)} %collective-permute-done.7.refs_0_, bf16[384,768]{1,0:T(8,128)(2,1)} %copy-done.4, bf16[128,2560]{1,0:T(8,128)(2,1)} %copy-done.2, bf16[512,1024]{1,0:T(8,128)(2,1)} %copy-done.1, ...), custom_call_target="tpu_custom_call", output_to_operand_aliasing={{}: (7, {})} | custom-call | tf_op jit(solution)/shard_map/weight_sums/pallas_call | solution.py:66
  (84 shorter events, 35.8 us)
Async XLA Ops:
  7.6 23.4 %collective-permute-start.2 = (bf16[48,2048]{1,0:T(8,128)(2,1)S(1)}, bf16[48,2048]{1,0:T(8,128)(2,1)S(1)}, u32[]{:S(2)}, u32[]{:S(2)}) collective-permute-start(bf16[48,2048]{1,0:T(8,128)(2,1)S(1)} %get-tuple-element.69), channel_id=1, source_target_pairs={{0,3},{1,4},{2,5},{3,6},{4,7},{5,0},{6,1},{7,2},{8,11},{9,12},{10,... | collective-permute-start | bytes 589832 | tf_op jit(solution)/shard_map/ppermute | solution.py:651
  10.1 21.1 %collective-permute-start.3 = (bf16[48,2048]{1,0:T(8,128)(2,1)S(1)}, bf16[48,2048]{1,0:T(8,128)(2,1)S(1)}, u32[]{:S(2)}, u32[]{:S(2)}) collective-permute-start(bf16[48,2048]{1,0:T(8,128)(2,1)S(1)} %get-tuple-element.70), channel_id=1, source_target_pairs={{0,4},{1,5},{2,6},{3,7},{4,0},{5,1},{6,2},{7,3},{8,12},{9,13},{10,... | collective-permute-start | bytes 589832 | tf_op jit(solution)/shard_map/ppermute | solution.py:651
  11.3 19.8 %collective-permute-start.4 = (bf16[48,2048]{1,0:T(8,128)(2,1)S(1)}, bf16[48,2048]{1,0:T(8,128)(2,1)S(1)}, u32[]{:S(2)}, u32[]{:S(2)}) collective-permute-start(bf16[48,2048]{1,0:T(8,128)(2,1)S(1)} %get-tuple-element.71), channel_id=1, source_target_pairs={{0,5},{1,6},{2,7},{3,0},{4,1},{5,2},{6,3},{7,4},{8,13},{9,14},{10,... | collective-permute-start | bytes 589832 | tf_op jit(solution)/shard_map/ppermute | solution.py:651
  15.0 16.2 %collective-permute-start.5 = (bf16[48,2048]{1,0:T(8,128)(2,1)S(1)}, bf16[48,2048]{1,0:T(8,128)(2,1)S(1)}, u32[]{:S(2)}, u32[]{:S(2)}) collective-permute-start(bf16[48,2048]{1,0:T(8,128)(2,1)S(1)} %get-tuple-element.72), channel_id=1, source_target_pairs={{0,6},{1,7},{2,0},{3,1},{4,2},{5,3},{6,4},{7,5},{8,14},{9,15},{10,... | collective-permute-start | bytes 589832 | tf_op jit(solution)/shard_map/ppermute | solution.py:651
  16.8 15.8 %collective-permute-start.6 = (bf16[48,2048]{1,0:T(8,128)(2,1)S(1)}, bf16[48,2048]{1,0:T(8,128)(2,1)S(1)}, u32[]{:S(2)}, u32[]{:S(2)}) collective-permute-start(bf16[48,2048]{1,0:T(8,128)(2,1)S(1)} %get-tuple-element.73), channel_id=1, source_target_pairs={{0,7},{1,0},{2,1},{3,2},{4,3},{5,4},{6,5},{7,6},{8,15},{9,8},{10,9... | collective-permute-start | bytes 589832 | tf_op jit(solution)/shard_map/ppermute | solution.py:651
  38.7 51.2 %all-to-all-start = ((bf16[8,48,2048]{2,1,0:T(8,128)(2,1)}), bf16[8,48,2048]{2,1,0:T(8,128)(2,1)S(1)}, u32[]{:S(2)}, u32[]{:S(2)}) async-start(bf16[8,48,2048]{2,1,0:T(8,128)(2,1)} %bitcast.17), calls=%async_computation | async-start | bytes 3145728 | tf_op jit(solution)/shard_map/all_to_all | solution.py:646
  53.7 26.2 %collective-permute-start.7 = (bf16[512,1024]{1,0:T(8,128)(2,1)S(1)}, bf16[512,1024]{1,0:T(8,128)(2,1)}, u32[]{:S(2)}, u32[]{:S(2)}) collective-permute-start(bf16[512,1024]{1,0:T(8,128)(2,1)S(1)} %get-tuple-element.80), channel_id=1, source_target_pairs={{0,16},{8,24},{16,0},{24,8},{1,17},{9,25},{17,1},{25,9},{2,18},{10... | collective-permute-start | bytes 3145736 | tf_op jit(solution)/shard_map/ppermute | solution.py:659
  55.2 41.1 %collective-permute-start.8 = (bf16[512,768]{1,0:T(8,128)(2,1)}, bf16[512,768]{1,0:T(8,128)(2,1)S(1)}, u32[]{:S(2)}, u32[]{:S(2)}) collective-permute-start(bf16[512,768]{1,0:T(8,128)(2,1)} %get-tuple-element.87.refs_9_), channel_id=1, source_target_pairs={{0,16},{8,24},{16,0},{24,8},{1,17},{9,25},{17,1},{25,9},{2,18},{10... | collective-permute-start | bytes 2359304 | tf_op jit(solution)/shard_map/ppermute | solution.py:659
  95.7 62.2 %collective-permute-start.19 = (bf16[512,2048]{1,0:T(8,128)(2,1)}, bf16[512,2048]{1,0:T(8,128)(2,1)}, u32[]{:S(2)}, u32[]{:S(2)}) collective-permute-start(bf16[512,2048]{1,0:T(8,128)(2,1)} %get-tuple-element.115.refs_0_), channel_id=1, source_target_pairs={{0,8},{8,0},{16,24},{24,16},{1,9},{9,1},{17,25},{25,17},{2,10},{10... | collective-permute-start | bytes 6291464 | tf_op jit(solution)/shard_map/ppermute | solution.py:672
  95.7 14.6 %collective-permute-start.11 = (bf16[48,2048]{1,0:T(8,128)(2,1)S(1)}, bf16[48,2048]{1,0:T(8,128)(2,1)S(1)}, u32[]{:S(2)}, u32[]{:S(2)}) collective-permute-start(bf16[48,2048]{1,0:T(8,128)(2,1)S(1)} %get-tuple-element.99), channel_id=1, source_target_pairs={{0,2},{1,3},{2,4},{3,5},{4,6},{5,7},{6,0},{7,1},{8,10},{9,11},{10,... | collective-permute-start | bytes 589832 | tf_op jit(solution)/shard_map/ppermute | solution.py:651
  96.2 20.6 %collective-permute-start.12 = (bf16[48,2048]{1,0:T(8,128)(2,1)S(1)}, bf16[48,2048]{1,0:T(8,128)(2,1)S(1)}, u32[]{:S(2)}, u32[]{:S(2)}) collective-permute-start(bf16[48,2048]{1,0:T(8,128)(2,1)S(1)} %get-tuple-element.100), channel_id=1, source_target_pairs={{0,3},{1,4},{2,5},{3,6},{4,7},{5,0},{6,1},{7,2},{8,11},{9,12},{10,... | collective-permute-start | bytes 589832 | tf_op jit(solution)/shard_map/ppermute | solution.py:651
  96.2 25.5 %collective-permute-start.13 = (bf16[48,2048]{1,0:T(8,128)(2,1)S(1)}, bf16[48,2048]{1,0:T(8,128)(2,1)S(1)}, u32[]{:S(2)}, u32[]{:S(2)}) collective-permute-start(bf16[48,2048]{1,0:T(8,128)(2,1)S(1)} %get-tuple-element.101), channel_id=1, source_target_pairs={{0,4},{1,5},{2,6},{3,7},{4,0},{5,1},{6,2},{7,3},{8,12},{9,13},{10,... | collective-permute-start | bytes 589832 | tf_op jit(solution)/shard_map/ppermute | solution.py:651
  108.8 28.2 %collective-permute-start.16 = (bf16[128,2560]{1,0:T(8,128)(2,1)S(1)}, bf16[128,2560]{1,0:T(8,128)(2,1)S(1)}, u32[]{:S(2)}, u32[]{:S(2)}) collective-permute-start(bf16[128,2560]{1,0:T(8,128)(2,1)S(1)} %get-tuple-element.112), channel_id=1, source_target_pairs={{0,16},{8,24},{16,0},{24,8},{1,17},{9,25},{17,1},{25,9},{2,18},{10... | collective-permute-start | bytes 1966088 | tf_op jit(solution)/shard_map/ppermute | solution.py:659
  110.3 19.1 %collective-permute-start.14 = (bf16[48,2048]{1,0:T(8,128)(2,1)S(1)}, bf16[48,2048]{1,0:T(8,128)(2,1)S(1)}, u32[]{:S(2)}, u32[]{:S(2)}) collective-permute-start(bf16[48,2048]{1,0:T(8,128)(2,1)S(1)} %get-tuple-element.102), channel_id=1, source_target_pairs={{0,5},{1,6},{2,7},{3,0},{4,1},{5,2},{6,3},{7,4},{8,13},{9,14},{10,... | collective-permute-start | bytes 589832 | tf_op jit(solution)/shard_map/ppermute | solution.py:651
  135.4 24.5 %collective-permute-start.23 = (bf16[384,2048]{1,0:T(8,128)(2,1)}, bf16[384,2048]{1,0:T(8,128)(2,1)}, u32[]{:S(2)}, u32[]{:S(2)}) collective-permute-start(bf16[384,2048]{1,0:T(8,128)(2,1)} %get-tuple-element.117.refs_8_), channel_id=1, source_target_pairs={{0,8},{8,0},{16,24},{24,16},{1,9},{9,1},{17,25},{25,17},{2,10},{10... | collective-permute-start | bytes 4718600 | tf_op jit(solution)/shard_map/ppermute | solution.py:672
  137.0 20.3 %collective-permute-start.17 = (bf16[384,1024]{1,0:T(8,128)(2,1)}, bf16[384,1024]{1,0:T(8,128)(2,1)}, u32[]{:S(2)}, u32[]{:S(2)}) collective-permute-start(bf16[384,1024]{1,0:T(8,128)(2,1)} %cut.1), channel_id=1, source_target_pairs={{0,16},{8,24},{16,0},{24,8},{1,17},{9,25},{17,1},{25,9},{2,18},{10... | collective-permute-start | bytes 2359304 | tf_op jit(solution)/shard_map/ppermute | solution.py:659
  138.6 18.8 %collective-permute-start.24 = (bf16[512,768]{1,0:T(8,128)(2,1)}, bf16[512,768]{1,0:T(8,128)(2,1)}, u32[]{:S(2)}, u32[]{:S(2)}) collective-permute-start(bf16[512,768]{1,0:T(8,128)(2,1)} %get-tuple-element.87.refs_9_), channel_id=1, source_target_pairs={{0,8},{8,0},{16,24},{24,16},{1,9},{9,1},{17,25},{25,17},{2,10},{10... | collective-permute-start | bytes 2359304 | tf_op jit(solution)/shard_map/ppermute | solution.py:672
  138.8 45.4 %all-to-all-start.1 = ((bf16[8,48,2048]{2,1,0:T(8,128)(2,1)}), bf16[8,48,2048]{2,1,0:T(8,128)(2,1)S(1)}, u32[]{:S(2)}, u32[]{:S(2)}) async-start(bf16[8,48,2048]{2,1,0:T(8,128)(2,1)} %bitcast.16), calls=%async_computation.1 | async-start | bytes 3145728 | tf_op jit(solution)/shard_map/all_to_all | solution.py:646
  144.6 14.7 %collective-permute-start.21 = (bf16[128,2560]{1,0:T(8,128)(2,1)S(1)}, bf16[128,2560]{1,0:T(8,128)(2,1)S(1)}, u32[]{:S(2)}, u32[]{:S(2)}) collective-permute-start(bf16[128,2560]{1,0:T(8,128)(2,1)S(1)} %get-tuple-element.116.refs_2_), channel_id=1, source_target_pairs={{0,8},{8,0},{16,24},{24,16},{1,9},{9,1},{17,25},{25,17},{2,10},{10... | collective-permute-start | bytes 1966088 | tf_op jit(solution)/shard_map/ppermute | solution.py:672
  157.8 15.3 %collective-permute-start.18 = (bf16[384,768]{1,0:T(8,128)(2,1)S(1)}, bf16[384,768]{1,0:T(8,128)(2,1)S(1)}, u32[]{:S(2)}, u32[]{:S(2)}) collective-permute-start(bf16[384,768]{1,0:T(8,128)(2,1)S(1)} %copy-done.9), channel_id=1, source_target_pairs={{0,16},{8,24},{16,0},{24,8},{1,17},{9,25},{17,1},{25,9},{2,18},{10... | collective-permute-start | bytes 1769480 | tf_op jit(solution)/shard_map/ppermute | solution.py:659
  159.3 15.4 %collective-permute-start.26 = (bf16[512,1024]{1,0:T(8,128)(2,1)}, bf16[512,1024]{1,0:T(8,128)(2,1)S(1)}, u32[]{:S(2)}, u32[]{:S(2)}) collective-permute-start(bf16[512,1024]{1,0:T(8,128)(2,1)} %collective-permute-done.7.refs_0_), channel_id=1, source_target_pairs={{0,8},{8,0},{16,24},{24,16},{1,9},{9,1},{17,25},{25,17},{2,10},{10... | collective-permute-start | bytes 3145736 | tf_op jit(solution)/shard_map/ppermute | solution.py:672
  159.9 14.9 %collective-permute-start.28 = (bf16[128,2560]{1,0:T(8,128)(2,1)S(1)}, bf16[128,2560]{1,0:T(8,128)(2,1)S(1)}, u32[]{:S(2)}, u32[]{:S(2)}) collective-permute-start(bf16[128,2560]{1,0:T(8,128)(2,1)S(1)} %collective-permute-done.16.refs_2_), channel_id=1, source_target_pairs={{0,8},{8,0},{16,24},{24,16},{1,9},{9,1},{17,25},{25,17},{2,10},{10... | collective-permute-start | bytes 1966088 | tf_op jit(solution)/shard_map/ppermute | solution.py:672
  160.2 14.6 %collective-permute-start.29 = (bf16[384,1024]{1,0:T(8,128)(2,1)}, bf16[384,1024]{1,0:T(8,128)(2,1)S(1)}, u32[]{:S(2)}, u32[]{:S(2)}) collective-permute-start(bf16[384,1024]{1,0:T(8,128)(2,1)} %collective-permute-done.17.refs_6_), channel_id=1, source_target_pairs={{0,8},{8,0},{16,24},{24,16},{1,9},{9,1},{17,25},{25,17},{2,10},{10... | collective-permute-start | bytes 2359304 | tf_op jit(solution)/shard_map/ppermute | solution.py:672
  173.2 16.0 %collective-permute-start.25 = (bf16[384,768]{1,0:T(8,128)(2,1)}, bf16[384,768]{1,0:T(8,128)(2,1)S(1)}, u32[]{:S(2)}, u32[]{:S(2)}) collective-permute-start(bf16[384,768]{1,0:T(8,128)(2,1)} %get-tuple-element.118.refs_6_), channel_id=1, source_target_pairs={{0,16},{8,24},{16,0},{24,8},{1,17},{9,25},{17,1},{25,9},{2,18},{10... | collective-permute-start | bytes 1769480 | tf_op jit(solution)/shard_map/ppermute | solution.py:659
  (24 other events, 188.9 us)

commit v5 on v4

--- a/solution.py
+++ b/solution.py
@@ -9,9 +9,10 @@
 BF16 = jnp.bfloat16
 MIB = 1 << 20
 LONG = 20_000_000_000
-BACK = 2_000_000_000
-SUMS = 5_000_000_000
+BACK = 20_000_000_000
+SUMS = 4_000_000_000
 LATE = True
+CUT = True
 LATE_ONES = (6, 1)
 VMEM = pl.BlockSpec(memory_space=pltpu.VMEM)
 SMEM = pl.BlockSpec(memory_space=pltpu.SMEM)
@@ -703,6 +704,7 @@
         blocks = [at_once(blocks[0])]
     l_own, l_far = l_send[0], to_chips(l_send[1:])
     c_send = cut(ids, blocks, chips, cores, part)
+    blocks, c_send = together((blocks, c_send)) if CUT else (blocks, c_send)
     back, gate_back, up_back, cots = backward(ids, blocks, *kept, *on)
     returned = at_once(back)
     c_send, l_far = together((c_send, l_far))

time: 197 us -> 195 us (0.990)
  waiting for transfers between devices: 81.2 us -> 69.4 us
  starting transfers between devices: 56.5 us -> 65.3 us
    ppermute x14, waiting for transfers between devices: 24.9 us -> 15.5 us  [steps(): lax.ppermute(blocks[k], 'expert', [(i, (i + k) % groups) for i in range(g...]
    ppermute x14, starting transfers between devices: 25.9 us -> 32.2 us  [steps(): lax.ppermute(blocks[k], 'expert', [(i, (i + k) % groups) for i in range(g...]
    ppermute x6, waiting for transfers between devices: 43.5 us -> 41.2 us  [to_chips(): lax.ppermute(array, 'dp', [(start * cores + i, (start + shift) % chips *...]
    all_to_all x2, starting transfers between devices: 20.8 us -> 23 us  [at_once(): lax.all_to_all(block, 'expert', split_axis=0, concat_axis=0, tiled=True)]
  transfers between devices with their start and end apart: 34 -> 34, of which waited for: 17 -> 18; matrix products, arithmetic and copies ran while one was open for 0% -> 0% of each run, Pallas kernels for 21% -> 22%
where the time goes in v5:
time: 195 us; the launch traced here: 193 us
  waiting for transfers between devices  69.4 us (36%)
  starting transfers between devices  65.3 us (33%)
  Pallas kernels  54.8 us (28%)
  local copies, waits for them, and re-layouts  2.47 us (1%)
    pallas_call x11, Pallas kernels, call(): pl.pallas_call(kernel, out_shape=tuple(outs), in_specs=specs, out_specs=t...  54.8 us
    ppermute x6, waiting for transfers between devices, to_chips(): lax.ppermute(array, 'dp', [(start * cores + i, (start + shift) % chips *...  41.2 us
    ppermute x14, starting transfers between devices, steps(): lax.ppermute(blocks[k], 'expert', [(i, (i + k) % groups) for i in range(g...  32.2 us
    all_to_all x2, starting transfers between devices, at_once(): lax.all_to_all(block, 'expert', split_axis=0, concat_axis=0, tiled=True)  23 us
    ppermute x14, waiting for transfers between devices, steps(): lax.ppermute(blocks[k], 'expert', [(i, (i + k) % groups) for i in range(g...  15.5 us
    all_to_all x2, waiting for transfers between devices, at_once(): lax.all_to_all(block, 'expert', split_axis=0, concat_axis=0, tiled=True)  10 us
    ppermute x6, starting transfers between devices, to_chips(): lax.ppermute(array, 'dp', [(start * cores + i, (start + shift) % chips *...  8.07 us
  transfers between devices with their start and end apart: 34, of which 18 were waited for; matrix products, arithmetic and copies ran while one was open for 0% of the time, Pallas kernels for 22%

profile of v5, /device:TPU:0, one launch (start us, length us, event | category | flops | bytes accessed | tf_op | source)
XLA Modules:
  0.0 193.0 jit_solution(11279122563831859354)
XLA Ops:
  3.0 3.0 %collective-permute-start = (bf16[48,2048]{1,0:T(8,128)(2,1)S(1)}, bf16[48,2048]{1,0:T(8,128)(2,1)S(1)}, u32[]{:S(2)}, u32[]{:S(2)}) collective-permute-start(bf16[48,2048]{1,0:T(8,128)(2,1)S(1)} %get-tuple-element.76), channel_id=1, source_target_pairs={{0,1},{1,2},{2,3},{3,4},{4,5},{5,6},{6,7},{7,0},{8,9},{9,10},{10,1... | collective-permute-start | bytes 589832 | tf_op jit(solution)/shard_map/ppermute | solution.py:652
  7.6 2.5 %collective-permute-start.2 = (bf16[48,2048]{1,0:T(8,128)(2,1)S(1)}, bf16[48,2048]{1,0:T(8,128)(2,1)S(1)}, u32[]{:S(2)}, u32[]{:S(2)}) collective-permute-start(bf16[48,2048]{1,0:T(8,128)(2,1)S(1)} %get-tuple-element.78), channel_id=1, source_target_pairs={{0,3},{1,4},{2,5},{3,6},{4,7},{5,0},{6,1},{7,2},{8,11},{9,12},{10,... | collective-permute-start | bytes 589832 | tf_op jit(solution)/shard_map/ppermute | solution.py:652
  11.4 2.6 %collective-permute-start.4 = (bf16[48,2048]{1,0:T(8,128)(2,1)S(1)}, bf16[48,2048]{1,0:T(8,128)(2,1)S(1)}, u32[]{:S(2)}, u32[]{:S(2)}) collective-permute-start(bf16[48,2048]{1,0:T(8,128)(2,1)S(1)} %get-tuple-element.80), channel_id=1, source_target_pairs={{0,5},{1,6},{2,7},{3,0},{4,1},{5,2},{6,3},{7,4},{8,13},{9,14},{10,... | collective-permute-start | bytes 589832 | tf_op jit(solution)/shard_map/ppermute | solution.py:652
  16.8 3.4 %collective-permute-start.6 = (bf16[48,2048]{1,0:T(8,128)(2,1)S(1)}, bf16[48,2048]{1,0:T(8,128)(2,1)S(1)}, u32[]{:S(2)}, u32[]{:S(2)}) collective-permute-start(bf16[48,2048]{1,0:T(8,128)(2,1)S(1)} %get-tuple-element.82), channel_id=1, source_target_pairs={{0,7},{1,0},{2,1},{3,2},{4,3},{5,4},{6,5},{7,6},{8,15},{9,8},{10,9... | collective-permute-start | bytes 589832 | tf_op jit(solution)/shard_map/ppermute | solution.py:652
  20.2 5.7 %forward_local.1 = (f32[128,2048]{1,0:T(8,128)}, f32[128,768]{1,0:T(8,128)}, f32[128,768]{1,0:T(8,128)}, bf16[128,768]{1,0:T(8,128)(2,1)S(1)}, bf16[128,2048]{1,...) custom-call(bf16[128,2048]{1,0:T(8,128)(2,1)} %tokens_hbm.3, ...), custom_call_target="tpu_custom_call" | custom-call | flops 20000000000 | tf_op jit(solution)/shard_map/forward_local/pallas_call | solution.py:67
  26.0 5.0 %collective-permute-done.2.refs_3_ = bf16[48,2048]{1,0:T(8,128)(2,1)S(1)} collective-permute-done((bf16[48,2048]{1,0:T(8,128)(2,1)S(1)}, bf16[48,2048]{1,0:T(8,128)(2,1)S(1)}, u32[]{:S(2)}, u32[]{:S(2)}) %collective-permute-start.2) | collective-permute-done | bytes 196640 | tf_op jit(solution)/shard_map/ppermute | solution.py:652
  32.6 6.1 %forward.1 = (bf16[384,2048]{1,0:T(8,128)(2,1)}, bf16[512,2048]{1,0:T(8,128)(2,1)}, bf16[512,768]{1,0:T(8,128)(2,1)}, f32[384,768]{1,0:T(8,128)}, f32[384,768]{1,0:T(8,128)}, /*index=5*/bf16[512,1024]{1,0:T(8,128)(2,1)S(1)}) custom-call(s32[2]{0:T(128)S(1)} %pad_add_fusion.ids_ref, bf16[48,2048]{1,0:T(8,128)(2,1)S(1)} %get-tuple-element.75.refs_0_, ...), custom_call_target="tpu_custom_call" | custom-call | tf_op jit(solution)/shard_map/forward/pallas_call | solution.py:67
  38.7 15.0 %all-to-all-start = ((bf16[8,48,2048]{2,1,0:T(8,128)(2,1)}), bf16[8,48,2048]{2,1,0:T(8,128)(2,1)S(1)}, u32[]{:S(2)}, u32[]{:S(2)}) async-start(bf16[8,48,2048]{2,1,0:T(8,128)(2,1)} %bitcast.17), calls=%async_computation | async-start | bytes 3145728 | tf_op jit(solution)/shard_map/all_to_all | solution.py:647
  55.7 24.2 %collective-permute-done.7.refs_0_ = bf16[512,1024]{1,0:T(8,128)(2,1)} collective-permute-done((bf16[512,1024]{1,0:T(8,128)(2,1)S(1)}, bf16[512,1024]{1,0:T(8,128)(2,1)}, u32[]{:S(2)}, u32[]{:S(2)}) %collective-permute-start.7) | collective-permute-done | bytes 1048608 | tf_op jit(solution)/shard_map/ppermute | solution.py:660
  79.9 10.0 %all-to-all-done = bf16[8,48,2048]{2,1,0:T(8,128)(2,1)S(1)} async-done(((bf16[8,48,2048]{2,1,0:T(8,128)(2,1)}), bf16[8,48,2048]{2,1,0:T(8,128)(2,1)S(1)}, u32[]{:S(2)}, u32[]{:S(2)}) %all-to-all-start) | async-done | bytes 1572896 | tf_op jit(solution)/shard_map/all_to_all | solution.py:647
  89.9 3.5 %mix.1 = (bf16[48,2048]{1,0:T(8,128)(2,1)S(1)}, bf16[48,2048]{1,0:T(8,128)(2,1)S(1)}, bf16[48,2048]{1,0:T(8,128)(2,1)S(1)}, bf16[48,2048]{1,0:T(8,128)(2,1)S(1)}...) custom-call(bf16[384,2048]{1,0:T(8,128)(2,1)S(1)} %bitcast.14, ...), custom_call_target="tpu_custom_call" | custom-call | tf_op jit(solution)/shard_map/mix/pallas_call | solution.py:67
  96.2 3.1 %collective-permute-start.13 = (bf16[48,2048]{1,0:T(8,128)(2,1)S(1)}, bf16[48,2048]{1,0:T(8,128)(2,1)S(1)}, u32[]{:S(2)}, u32[]{:S(2)}) collective-permute-start(bf16[48,2048]{1,0:T(8,128)(2,1)S(1)} %get-tuple-element.110), channel_id=1, source_target_pairs={{0,4},{1,5},{2,6},{3,7},{4,0},{5,1},{6,2},{7,3},{8,12},{9,13},{10,... | collective-permute-start | bytes 589832 | tf_op jit(solution)/shard_map/ppermute | solution.py:652
  101.0 7.7 %backward_local.1 = (f32[128,2048]{1,0:T(8,128)}, bf16[2048,768]{1,0:T(8,128)(2,1)S(1)}, bf16[2048,768]{1,0:T(8,128)(2,1)S(1)}, bf16[768,2048]{1,0:T(8,128)(2,1)...) custom-call(s32[2]{0:T(128)S(1)} %pad_add_fusion.ids_ref, ...), custom_call_target="tpu_custom_call" | custom-call | flops 20000000000 | tf_op jit(solution)/shard_map/backward_local/pallas_call | solution.py:67
  108.8 9.3 %collective-permute-start.10 = (bf16[48,2048]{1,0:T(8,128)(2,1)S(1)}, bf16[48,2048]{1,0:T(8,128)(2,1)S(1)}, u32[]{:S(2)}, u32[]{:S(2)}) collective-permute-start(bf16[48,2048]{1,0:T(8,128)(2,1)S(1)} %get-tuple-element.107), channel_id=1, source_target_pairs={{0,1},{1,2},{2,3},{3,4},{4,5},{5,6},{6,7},{7,0},{8,9},{9,10},{10,1... | collective-permute-start | bytes 589832 | tf_op jit(solution)/shard_map/ppermute | solution.py:652
  118.1 3.0 %collective-permute-done.13.refs_4_ = bf16[48,2048]{1,0:T(8,128)(2,1)S(1)} collective-permute-done((bf16[48,2048]{1,0:T(8,128)(2,1)S(1)}, bf16[48,2048]{1,0:T(8,128)(2,1)S(1)}, u32[]{:S(2)}, u32[]{:S(2)}) %collective-permute-start.13) | collective-permute-done | bytes 196640 | tf_op jit(solution)/shard_map/ppermute | solution.py:652
  122.6 2.6 %collective-permute-done.10.refs_1_ = bf16[48,2048]{1,0:T(8,128)(2,1)S(1)} collective-permute-done((bf16[48,2048]{1,0:T(8,128)(2,1)S(1)}, bf16[48,2048]{1,0:T(8,128)(2,1)S(1)}, u32[]{:S(2)}, u32[]{:S(2)}) %collective-permute-start.10) | collective-permute-done | bytes 196640 | tf_op jit(solution)/shard_map/ppermute | solution.py:652
  128.2 5.8 %backward.1 = (bf16[384,2048]{1,0:T(8,128)(2,1)}, bf16[384,768]{1,0:T(8,128)(2,1)}, bf16[384,768]{1,0:T(8,128)(2,1)}, bf16[384,2048]{1,0:T(8,128)(2,1)}) custom-call(s32[2]{0:T(128)S(1)} %pad_add_fusion.ids_ref, bf16[48,2048]{1,0:T(8,128)(2,1)S(1)} %get-tuple-element.114.refs_0_, bf16[48,2048]{1,0:T(8,128)(2,1)S(1)} %collective-permute-done.10.refs_1_, ...), custom_call_target="tpu_custom_call" | custom-call | flops 20000000000 | tf_op jit(solution)/shard_map/backward/pallas_call | solution.py:67
  137.8 8.0 %all-to-all-start.1 = ((bf16[8,48,2048]{2,1,0:T(8,128)(2,1)}), bf16[8,48,2048]{2,1,0:T(8,128)(2,1)S(1)}, u32[]{:S(2)}, u32[]{:S(2)}) async-start(bf16[8,48,2048]{2,1,0:T(8,128)(2,1)} %bitcast.16), calls=%async_computation.1 | async-start | bytes 3145728 | tf_op jit(solution)/shard_map/all_to_all | solution.py:647
  146.4 7.9 %collective-permute-done.17.refs_6_ = bf16[384,1024]{1,0:T(8,128)(2,1)} collective-permute-done((bf16[384,1024]{1,0:T(8,128)(2,1)}, bf16[384,1024]{1,0:T(8,128)(2,1)}, u32[]{:S(2)}, u32[]{:S(2)}) %collective-permute-start.17) | collective-permute-done | bytes 786464 | tf_op jit(solution)/shard_map/ppermute | solution.py:660
  158.0 7.8 %weight_sums.3.refs_10_ = f32[512,2304]{1,0:T(8,128)} custom-call(s32[2]{0:T(128)S(1)} %pad_add_fusion.ids_ref, bf16[512,2048]{1,0:T(8,128)(2,1)} %get-tuple-element.133.refs_0_, bf16[384,768]{1,0:T(8,128)(2,1)} %get-tuple-element.132.refs_1_, bf16[128,2560]{1,0:T(8,128)(2,1)} %copy-done, bf16[512,2048]{1,0:T(8,128)(2,1)} %collective-permute-done.19.refs_3_, ...), custom_call_target="tpu_custom_call" | custom-call | flops 4000000000 | tf_op jit(solution)/shard_map/weight_sums/pallas_call | solution.py:67
  165.8 4.4 %collective-permute-done.18.refs_1_ = bf16[384,768]{1,0:T(8,128)(2,1)S(1)} collective-permute-done((bf16[384,768]{1,0:T(8,128)(2,1)S(1)}, bf16[384,768]{1,0:T(8,128)(2,1)S(1)}, u32[]{:S(2)}, u32[]{:S(2)}) %collective-permute-start.18) | collective-permute-done | bytes 589856 | tf_op jit(solution)/shard_map/ppermute | solution.py:660
  174.1 7.1 %weight_sums.4.refs_6_ = f32[512,2304]{1,0:T(8,128)} custom-call(s32[2]{0:T(128)S(1)} %pad_add_fusion.ids_ref, bf16[512,1024]{1,0:T(8,128)(2,1)} %collective-permute-done.7.refs_0_, bf16[384,768]{1,0:T(8,128)(2,1)} %copy-done.10, bf16[128,2560]{1,0:T(8,128)(2,1)} %copy-done.2, bf16[512,1024]{1,0:T(8,128)(2,1)} %copy-done.1, ...), custom_call_target="tpu_custom_call", output_to_operand_aliasing={{}: (11, {})} | custom-call | flops 4000000000 | tf_op jit(solution)/shard_map/weight_sums/pallas_call | solution.py:67
  181.2 2.5 %combine.1 = bf16[128,2048]{1,0:T(8,128)(2,1)} custom-call(bf16[384,2048]{1,0:T(8,128)(2,1)S(1)} %bitcast.13, bf16[256,384]{1,0:T(8,128)(2,1)} %get-tuple-element.91.refs_0_.pick_hbm, f32[128,2048]{1,0:T(8,128)} %get-tuple-element.144.local_hbm), custom_call_target="tpu_custom_call" | custom-call | tf_op jit(solution)/shard_map/combine/pallas_call | solution.py:67
  188.2 4.7 %weight_sums.5 = f32[512,2304]{1,0:T(8,128)} custom-call(s32[2]{0:T(128)S(1)} %pad_add_fusion.ids_ref, bf16[512,1024]{1,0:T(8,128)(2,1)} %collective-permute-done.7.refs_0_, bf16[384,768]{1,0:T(8,128)(2,1)} %copy-done.12, bf16[128,2560]{1,0:T(8,128)(2,1)} %copy-done.2, bf16[512,1024]{1,0:T(8,128)(2,1)} %copy-done.1, ...), custom_call_target="tpu_custom_call", output_to_operand_aliasing={{}: (7, {})} | custom-call | tf_op jit(solution)/shard_map/weight_sums/pallas_call | solution.py:67
  (86 shorter events, 37.1 us)
Async XLA Ops:
  7.6 23.4 %collective-permute-start.2 = (bf16[48,2048]{1,0:T(8,128)(2,1)S(1)}, bf16[48,2048]{1,0:T(8,128)(2,1)S(1)}, u32[]{:S(2)}, u32[]{:S(2)}) collective-permute-start(bf16[48,2048]{1,0:T(8,128)(2,1)S(1)} %get-tuple-element.78), channel_id=1, source_target_pairs={{0,3},{1,4},{2,5},{3,6},{4,7},{5,0},{6,1},{7,2},{8,11},{9,12},{10,... | collective-permute-start | bytes 589832 | tf_op jit(solution)/shard_map/ppermute | solution.py:652
  10.1 21.1 %collective-permute-start.3 = (bf16[48,2048]{1,0:T(8,128)(2,1)S(1)}, bf16[48,2048]{1,0:T(8,128)(2,1)S(1)}, u32[]{:S(2)}, u32[]{:S(2)}) collective-permute-start(bf16[48,2048]{1,0:T(8,128)(2,1)S(1)} %get-tuple-element.79), channel_id=1, source_target_pairs={{0,4},{1,5},{2,6},{3,7},{4,0},{5,1},{6,2},{7,3},{8,12},{9,13},{10,... | collective-permute-start | bytes 589832 | tf_op jit(solution)/shard_map/ppermute | solution.py:652
  11.4 19.8 %collective-permute-start.4 = (bf16[48,2048]{1,0:T(8,128)(2,1)S(1)}, bf16[48,2048]{1,0:T(8,128)(2,1)S(1)}, u32[]{:S(2)}, u32[]{:S(2)}) collective-permute-start(bf16[48,2048]{1,0:T(8,128)(2,1)S(1)} %get-tuple-element.80), channel_id=1, source_target_pairs={{0,5},{1,6},{2,7},{3,0},{4,1},{5,2},{6,3},{7,4},{8,13},{9,14},{10,... | collective-permute-start | bytes 589832 | tf_op jit(solution)/shard_map/ppermute | solution.py:652
  15.0 16.2 %collective-permute-start.5 = (bf16[48,2048]{1,0:T(8,128)(2,1)S(1)}, bf16[48,2048]{1,0:T(8,128)(2,1)S(1)}, u32[]{:S(2)}, u32[]{:S(2)}) collective-permute-start(bf16[48,2048]{1,0:T(8,128)(2,1)S(1)} %get-tuple-element.81), channel_id=1, source_target_pairs={{0,6},{1,7},{2,0},{3,1},{4,2},{5,3},{6,4},{7,5},{8,14},{9,15},{10,... | collective-permute-start | bytes 589832 | tf_op jit(solution)/shard_map/ppermute | solution.py:652
  16.8 15.8 %collective-permute-start.6 = (bf16[48,2048]{1,0:T(8,128)(2,1)S(1)}, bf16[48,2048]{1,0:T(8,128)(2,1)S(1)}, u32[]{:S(2)}, u32[]{:S(2)}) collective-permute-start(bf16[48,2048]{1,0:T(8,128)(2,1)S(1)} %get-tuple-element.82), channel_id=1, source_target_pairs={{0,7},{1,0},{2,1},{3,2},{4,3},{5,4},{6,5},{7,6},{8,15},{9,8},{10,9... | collective-permute-start | bytes 589832 | tf_op jit(solution)/shard_map/ppermute | solution.py:652
  38.7 51.2 %all-to-all-start = ((bf16[8,48,2048]{2,1,0:T(8,128)(2,1)}), bf16[8,48,2048]{2,1,0:T(8,128)(2,1)S(1)}, u32[]{:S(2)}, u32[]{:S(2)}) async-start(bf16[8,48,2048]{2,1,0:T(8,128)(2,1)} %bitcast.17), calls=%async_computation | async-start | bytes 3145728 | tf_op jit(solution)/shard_map/all_to_all | solution.py:647
  53.7 26.2 %collective-permute-start.7 = (bf16[512,1024]{1,0:T(8,128)(2,1)S(1)}, bf16[512,1024]{1,0:T(8,128)(2,1)}, u32[]{:S(2)}, u32[]{:S(2)}) collective-permute-start(bf16[512,1024]{1,0:T(8,128)(2,1)S(1)} %get-tuple-element.89), channel_id=1, source_target_pairs={{0,16},{8,24},{16,0},{24,8},{1,17},{9,25},{17,1},{25,9},{2,18},{10... | collective-permute-start | bytes 3145736 | tf_op jit(solution)/shard_map/ppermute | solution.py:660
  55.2 44.1 %collective-permute-start.8 = (bf16[512,768]{1,0:T(8,128)(2,1)}, bf16[512,768]{1,0:T(8,128)(2,1)S(1)}, u32[]{:S(2)}, u32[]{:S(2)}) collective-permute-start(bf16[512,768]{1,0:T(8,128)(2,1)} %get-tuple-element.96.refs_9_), channel_id=1, source_target_pairs={{0,16},{8,24},{16,0},{24,8},{1,17},{9,25},{17,1},{25,9},{2,18},{10... | collective-permute-start | bytes 2359304 | tf_op jit(solution)/shard_map/ppermute | solution.py:660
  95.7 22.3 %collective-permute-start.11 = (bf16[48,2048]{1,0:T(8,128)(2,1)S(1)}, bf16[48,2048]{1,0:T(8,128)(2,1)S(1)}, u32[]{:S(2)}, u32[]{:S(2)}) collective-permute-start(bf16[48,2048]{1,0:T(8,128)(2,1)S(1)} %get-tuple-element.108), channel_id=1, source_target_pairs={{0,2},{1,3},{2,4},{3,5},{4,6},{5,7},{6,0},{7,1},{8,10},{9,11},{10,... | collective-permute-start | bytes 589832 | tf_op jit(solution)/shard_map/ppermute | solution.py:652
  96.2 21.8 %collective-permute-start.12 = (bf16[48,2048]{1,0:T(8,128)(2,1)S(1)}, bf16[48,2048]{1,0:T(8,128)(2,1)S(1)}, u32[]{:S(2)}, u32[]{:S(2)}) collective-permute-start(bf16[48,2048]{1,0:T(8,128)(2,1)S(1)} %get-tuple-element.109), channel_id=1, source_target_pairs={{0,3},{1,4},{2,5},{3,6},{4,7},{5,0},{6,1},{7,2},{8,11},{9,12},{10,... | collective-permute-start | bytes 589832 | tf_op jit(solution)/shard_map/ppermute | solution.py:652
  96.2 24.8 %collective-permute-start.13 = (bf16[48,2048]{1,0:T(8,128)(2,1)S(1)}, bf16[48,2048]{1,0:T(8,128)(2,1)S(1)}, u32[]{:S(2)}, u32[]{:S(2)}) collective-permute-start(bf16[48,2048]{1,0:T(8,128)(2,1)S(1)} %get-tuple-element.110), channel_id=1, source_target_pairs={{0,4},{1,5},{2,6},{3,7},{4,0},{5,1},{6,2},{7,3},{8,12},{9,13},{10,... | collective-permute-start | bytes 589832 | tf_op jit(solution)/shard_map/ppermute | solution.py:652
  99.3 23.3 %collective-permute-start.14 = (bf16[48,2048]{1,0:T(8,128)(2,1)S(1)}, bf16[48,2048]{1,0:T(8,128)(2,1)S(1)}, u32[]{:S(2)}, u32[]{:S(2)}) collective-permute-start(bf16[48,2048]{1,0:T(8,128)(2,1)S(1)} %get-tuple-element.111), channel_id=1, source_target_pairs={{0,5},{1,6},{2,7},{3,0},{4,1},{5,2},{6,3},{7,4},{8,13},{9,14},{10,... | collective-permute-start | bytes 589832 | tf_op jit(solution)/shard_map/ppermute | solution.py:652
  108.8 16.4 %collective-permute-start.10 = (bf16[48,2048]{1,0:T(8,128)(2,1)S(1)}, bf16[48,2048]{1,0:T(8,128)(2,1)S(1)}, u32[]{:S(2)}, u32[]{:S(2)}) collective-permute-start(bf16[48,2048]{1,0:T(8,128)(2,1)S(1)} %get-tuple-element.107), channel_id=1, source_target_pairs={{0,1},{1,2},{2,3},{3,4},{4,5},{5,6},{6,7},{7,0},{8,9},{9,10},{10,1... | collective-permute-start | bytes 589832 | tf_op jit(solution)/shard_map/ppermute | solution.py:652
  118.0 36.9 %collective-permute-start.19 = (bf16[512,2048]{1,0:T(8,128)(2,1)}, bf16[512,2048]{1,0:T(8,128)(2,1)}, u32[]{:S(2)}, u32[]{:S(2)}) collective-permute-start(bf16[512,2048]{1,0:T(8,128)(2,1)} %get-tuple-element.133.refs_0_), channel_id=1, source_target_pairs={{0,8},{8,0},{16,24},{24,16},{1,9},{9,1},{17,25},{25,17},{2,10},{10... | collective-permute-start | bytes 6291464 | tf_op jit(solution)/shard_map/ppermute | solution.py:673
  121.1 15.3 %collective-permute-start.16 = (bf16[128,2560]{1,0:T(8,128)(2,1)S(1)}, bf16[128,2560]{1,0:T(8,128)(2,1)S(1)}, u32[]{:S(2)}, u32[]{:S(2)}) collective-permute-start(bf16[128,2560]{1,0:T(8,128)(2,1)S(1)} %get-tuple-element.130), channel_id=1, source_target_pairs={{0,16},{8,24},{16,0},{24,8},{1,17},{9,25},{17,1},{25,9},{2,18},{10... | collective-permute-start | bytes 1966088 | tf_op jit(solution)/shard_map/ppermute | solution.py:660
  134.0 22.9 %collective-permute-start.23 = (bf16[384,2048]{1,0:T(8,128)(2,1)}, bf16[384,2048]{1,0:T(8,128)(2,1)}, u32[]{:S(2)}, u32[]{:S(2)}) collective-permute-start(bf16[384,2048]{1,0:T(8,128)(2,1)} %get-tuple-element.135.refs_8_), channel_id=1, source_target_pairs={{0,8},{8,0},{16,24},{24,16},{1,9},{9,1},{17,25},{25,17},{2,10},{10... | collective-permute-start | bytes 4718600 | tf_op jit(solution)/shard_map/ppermute | solution.py:673
  136.4 18.0 %collective-permute-start.17 = (bf16[384,1024]{1,0:T(8,128)(2,1)}, bf16[384,1024]{1,0:T(8,128)(2,1)}, u32[]{:S(2)}, u32[]{:S(2)}) collective-permute-start(bf16[384,1024]{1,0:T(8,128)(2,1)} %cut.1), channel_id=1, source_target_pairs={{0,16},{8,24},{16,0},{24,8},{1,17},{9,25},{17,1},{25,9},{2,18},{10... | collective-permute-start | bytes 2359304 | tf_op jit(solution)/shard_map/ppermute | solution.py:660
  137.8 43.4 %all-to-all-start.1 = ((bf16[8,48,2048]{2,1,0:T(8,128)(2,1)}), bf16[8,48,2048]{2,1,0:T(8,128)(2,1)S(1)}, u32[]{:S(2)}, u32[]{:S(2)}) async-start(bf16[8,48,2048]{2,1,0:T(8,128)(2,1)} %bitcast.16), calls=%async_computation.1 | async-start | bytes 3145728 | tf_op jit(solution)/shard_map/all_to_all | solution.py:647
  154.9 15.3 %collective-permute-start.18 = (bf16[384,768]{1,0:T(8,128)(2,1)S(1)}, bf16[384,768]{1,0:T(8,128)(2,1)S(1)}, u32[]{:S(2)}, u32[]{:S(2)}) collective-permute-start(bf16[384,768]{1,0:T(8,128)(2,1)S(1)} %copy-done.9), channel_id=1, source_target_pairs={{0,16},{8,24},{16,0},{24,8},{1,17},{9,25},{17,1},{25,9},{2,18},{10... | collective-permute-start | bytes 1769480 | tf_op jit(solution)/shard_map/ppermute | solution.py:660
  156.4 15.4 %collective-permute-start.26 = (bf16[512,1024]{1,0:T(8,128)(2,1)}, bf16[512,1024]{1,0:T(8,128)(2,1)S(1)}, u32[]{:S(2)}, u32[]{:S(2)}) collective-permute-start(bf16[512,1024]{1,0:T(8,128)(2,1)} %collective-permute-done.7.refs_0_), channel_id=1, source_target_pairs={{0,8},{8,0},{16,24},{24,16},{1,9},{9,1},{17,25},{25,17},{2,10},{10... | collective-permute-start | bytes 3145736 | tf_op jit(solution)/shard_map/ppermute | solution.py:673
  156.5 13.7 %collective-permute-start.30 = (bf16[512,768]{1,0:T(8,128)(2,1)}, bf16[512,768]{1,0:T(8,128)(2,1)S(1)}, u32[]{:S(2)}, u32[]{:S(2)}) collective-permute-start(bf16[512,768]{1,0:T(8,128)(2,1)} %copy-done.4), channel_id=1, source_target_pairs={{0,8},{8,0},{16,24},{24,16},{1,9},{9,1},{17,25},{25,17},{2,10},{10... | collective-permute-start | bytes 2359304 | tf_op jit(solution)/shard_map/ppermute | solution.py:673
  156.9 14.9 %collective-permute-start.28 = (bf16[128,2560]{1,0:T(8,128)(2,1)S(1)}, bf16[128,2560]{1,0:T(8,128)(2,1)S(1)}, u32[]{:S(2)}, u32[]{:S(2)}) collective-permute-start(bf16[128,2560]{1,0:T(8,128)(2,1)S(1)} %collective-permute-done.16.refs_2_), channel_id=1, source_target_pairs={{0,8},{8,0},{16,24},{24,16},{1,9},{9,1},{17,25},{25,17},{2,10},{10... | collective-permute-start | bytes 1966088 | tf_op jit(solution)/shard_map/ppermute | solution.py:673
  157.2 14.7 %collective-permute-start.29 = (bf16[384,1024]{1,0:T(8,128)(2,1)}, bf16[384,1024]{1,0:T(8,128)(2,1)S(1)}, u32[]{:S(2)}, u32[]{:S(2)}) collective-permute-start(bf16[384,1024]{1,0:T(8,128)(2,1)} %collective-permute-done.17.refs_6_), channel_id=1, source_target_pairs={{0,8},{8,0},{16,24},{24,16},{1,9},{9,1},{17,25},{25,17},{2,10},{10... | collective-permute-start | bytes 2359304 | tf_op jit(solution)/shard_map/ppermute | solution.py:673
  170.2 16.0 %collective-permute-start.25 = (bf16[384,768]{1,0:T(8,128)(2,1)}, bf16[384,768]{1,0:T(8,128)(2,1)S(1)}, u32[]{:S(2)}, u32[]{:S(2)}) collective-permute-start(bf16[384,768]{1,0:T(8,128)(2,1)} %get-tuple-element.136.refs_6_), channel_id=1, source_target_pairs={{0,16},{8,24},{16,0},{24,8},{1,17},{9,25},{17,1},{25,9},{2,18},{10... | collective-permute-start | bytes 1769480 | tf_op jit(solution)/shard_map/ppermute | solution.py:660
  (25 other events, 179.8 us)

commit v6 on v4

--- a/solution.py
+++ b/solution.py
@@ -9,10 +9,7 @@
 BF16 = jnp.bfloat16
 MIB = 1 << 20
 LONG = 20_000_000_000
-BACK = 2_000_000_000
-SUMS = 5_000_000_000
-LATE = True
-LATE_ONES = (6, 1)
+SUMS = 4_500_000_000
 VMEM = pl.BlockSpec(memory_space=pltpu.VMEM)
 SMEM = pl.BlockSpec(memory_space=pltpu.SMEM)
 HBM = pl.BlockSpec(memory_space=pltpu.HBM)
@@ -338,13 +335,15 @@
         pick_ref, gates_ref, keep_ref, out_ref, cot_ref, place_ref = targets
         copies = Copies(sems)
         arriving = [copies.start(source, target) for source, target in zip(sources, targets)]
-        for copy in arriving:
+        for copy in arriving[:3]:
             copy.wait()
         gates = [column_of(gates_ref[k : k + 1, :]) for k in range(choose)]
         keep = column_of(keep_ref[...].astype(F32))
         for n in range(0, width, step):
             cols = pl.ds(n, step)
             picked = dot(pick_ref[...], returned_ref[:, cols])
+            for copy in arriving[3:] if n == 0 else []:
+                copy.wait()
             mixed = sum(gates[k] * picked[k * tok : (k + 1) * tok] for k in range(choose))
             difference = mixed - out_ref[:, cols]
             upstream = cot_ref[:, cols].astype(F32) + difference
@@ -505,7 +504,7 @@
             pltpu.SemaphoreType.DMA((3 + n_blocks * (width // d_tile),)),
         ],
         name="backward",
-        weight=BACK,
+        weight=LONG,
     )
 
 
@@ -639,7 +638,7 @@
     keep_row = keep[None]
     together = lax.optimization_barrier
     far_first = sorted(range(1, groups), key=lambda k: abs(k - groups / 2))
-    late = [k for k in LATE_ONES if k < groups - 1]
+    late = [k for k in (groups - 2, 1) if 0 < k < groups - 1]
 
     def at_once(block):
         block = block.reshape(groups, capacity, -1)
@@ -694,15 +693,13 @@
         ids, local_cot, local_silu, local_factor, *weights, (silu, factor), chips, cores, part
     )
     if apart:
-        if LATE:
-            l_send, later = together((l_send, {k: blocks[k] for k in late}))
-        else:
-            later = blocks
+        l_send, later = together((l_send, {k: blocks[k] for k in late}))
         blocks = arranged(blocks[0], moved | steps(later, late))
     else:
         blocks = [at_once(blocks[0])]
     l_own, l_far = l_send[0], to_chips(l_send[1:])
     c_send = cut(ids, blocks, chips, cores, part)
+    blocks, c_send = together((blocks, c_send))
     back, gate_back, up_back, cots = backward(ids, blocks, *kept, *on)
     returned = at_once(back)
     c_send, l_far = together((c_send, l_far))

time: 197 us -> 195 us (0.990)
  waiting for transfers between devices: 81.2 us -> 69.6 us
  starting transfers between devices: 56.5 us -> 65 us
    ppermute x14, waiting for transfers between devices: 24.9 us -> 15.5 us  [steps(): lax.ppermute(blocks[k], 'expert', [(i, (i + k) % groups) for i in range(g...]
    ppermute x14, starting transfers between devices: 25.9 us -> 32.2 us  [steps(): lax.ppermute(blocks[k], 'expert', [(i, (i + k) % groups) for i in range(g...]
    ppermute x6, waiting for transfers between devices: 43.5 us -> 38.9 us  [to_chips(): lax.ppermute(array, 'dp', [(start * cores + i, (start + shift) % chips *...]
    all_to_all x2, waiting for transfers between devices: 10 us -> 12.4 us  [at_once(): lax.all_to_all(block, 'expert', split_axis=0, concat_axis=0, tiled=True)]
    all_to_all x2, starting transfers between devices: 20.8 us -> 23 us  [at_once(): lax.all_to_all(block, 'expert', split_axis=0, concat_axis=0, tiled=True)]
where the time goes in v6:
time: 195 us; the launch traced here: 193 us
  waiting for transfers between devices  69.6 us (36%)
  starting transfers between devices  65 us (33%)
  Pallas kernels  54.5 us (28%)
  local copies, waits for them, and re-layouts  2.54 us (1%)
    pallas_call x11, Pallas kernels, call(): pl.pallas_call(kernel, out_shape=tuple(outs), in_specs=specs, out_specs=t...  54.5 us
    ppermute x6, waiting for transfers between devices, to_chips(): lax.ppermute(array, 'dp', [(start * cores + i, (start + shift) % chips *...  38.9 us
    ppermute x14, starting transfers between devices, steps(): lax.ppermute(blocks[k], 'expert', [(i, (i + k) % groups) for i in range(g...  32.2 us
    all_to_all x2, starting transfers between devices, at_once(): lax.all_to_all(block, 'expert', split_axis=0, concat_axis=0, tiled=True)  23 us
    ppermute x14, waiting for transfers between devices, steps(): lax.ppermute(blocks[k], 'expert', [(i, (i + k) % groups) for i in range(g...  15.5 us
    all_to_all x2, waiting for transfers between devices, at_once(): lax.all_to_all(block, 'expert', split_axis=0, concat_axis=0, tiled=True)  12.4 us
    ppermute x6, starting transfers between devices, to_chips(): lax.ppermute(array, 'dp', [(start * cores + i, (start + shift) % chips *...  8.06 us
  transfers between devices with their start and end apart: 34, of which 17 were waited for; matrix products, arithmetic and copies ran while one was open for 0% of the time, Pallas kernels for 21%

profile of v6, /device:TPU:0, one launch (start us, length us, event | category | flops | bytes accessed | tf_op | source)
XLA Modules:
  0.0 192.7 jit_solution(10411443552870453653)
XLA Ops:
  3.0 3.0 %collective-permute-start = (bf16[48,2048]{1,0:T(8,128)(2,1)S(1)}, bf16[48,2048]{1,0:T(8,128)(2,1)S(1)}, u32[]{:S(2)}, u32[]{:S(2)}) collective-permute-start(bf16[48,2048]{1,0:T(8,128)(2,1)S(1)} %get-tuple-element.76), channel_id=1, source_target_pairs={{0,1},{1,2},{2,3},{3,4},{4,5},{5,6},{6,7},{7,0},{8,9},{9,10},{10,1... | collective-permute-start | bytes 589832 | tf_op jit(solution)/shard_map/ppermute | solution.py:650
  7.6 2.5 %collective-permute-start.2 = (bf16[48,2048]{1,0:T(8,128)(2,1)S(1)}, bf16[48,2048]{1,0:T(8,128)(2,1)S(1)}, u32[]{:S(2)}, u32[]{:S(2)}) collective-permute-start(bf16[48,2048]{1,0:T(8,128)(2,1)S(1)} %get-tuple-element.78), channel_id=1, source_target_pairs={{0,3},{1,4},{2,5},{3,6},{4,7},{5,0},{6,1},{7,2},{8,11},{9,12},{10,... | collective-permute-start | bytes 589832 | tf_op jit(solution)/shard_map/ppermute | solution.py:650
  11.3 2.6 %collective-permute-start.4 = (bf16[48,2048]{1,0:T(8,128)(2,1)S(1)}, bf16[48,2048]{1,0:T(8,128)(2,1)S(1)}, u32[]{:S(2)}, u32[]{:S(2)}) collective-permute-start(bf16[48,2048]{1,0:T(8,128)(2,1)S(1)} %get-tuple-element.80), channel_id=1, source_target_pairs={{0,5},{1,6},{2,7},{3,0},{4,1},{5,2},{6,3},{7,4},{8,13},{9,14},{10,... | collective-permute-start | bytes 589832 | tf_op jit(solution)/shard_map/ppermute | solution.py:650
  16.8 3.4 %collective-permute-start.6 = (bf16[48,2048]{1,0:T(8,128)(2,1)S(1)}, bf16[48,2048]{1,0:T(8,128)(2,1)S(1)}, u32[]{:S(2)}, u32[]{:S(2)}) collective-permute-start(bf16[48,2048]{1,0:T(8,128)(2,1)S(1)} %get-tuple-element.82), channel_id=1, source_target_pairs={{0,7},{1,0},{2,1},{3,2},{4,3},{5,4},{6,5},{7,6},{8,15},{9,8},{10,9... | collective-permute-start | bytes 589832 | tf_op jit(solution)/shard_map/ppermute | solution.py:650
  20.2 5.7 %forward_local.1 = (f32[128,2048]{1,0:T(8,128)}, f32[128,768]{1,0:T(8,128)}, f32[128,768]{1,0:T(8,128)}, bf16[128,768]{1,0:T(8,128)(2,1)S(1)}, bf16[128,2048]{1,...) custom-call(bf16[128,2048]{1,0:T(8,128)(2,1)} %tokens_hbm.3, ...), custom_call_target="tpu_custom_call" | custom-call | flops 20000000000 | tf_op jit(solution)/shard_map/forward_local/pallas_call | solution.py:63
  26.0 5.0 %collective-permute-done.2.refs_3_ = bf16[48,2048]{1,0:T(8,128)(2,1)S(1)} collective-permute-done((bf16[48,2048]{1,0:T(8,128)(2,1)S(1)}, bf16[48,2048]{1,0:T(8,128)(2,1)S(1)}, u32[]{:S(2)}, u32[]{:S(2)}) %collective-permute-start.2) | collective-permute-done | bytes 196640 | tf_op jit(solution)/shard_map/ppermute | solution.py:650
  32.6 6.1 %forward.1 = (bf16[384,2048]{1,0:T(8,128)(2,1)}, bf16[512,2048]{1,0:T(8,128)(2,1)}, bf16[512,768]{1,0:T(8,128)(2,1)}, f32[384,768]{1,0:T(8,128)}, f32[384,768]{1,0:T(8,128)}, /*index=5*/bf16[512,1024]{1,0:T(8,128)(2,1)S(1)}) custom-call(s32[2]{0:T(128)S(1)} %pad_add_fusion.ids_ref, bf16[48,2048]{1,0:T(8,128)(2,1)S(1)} %get-tuple-element.75.refs_0_, ...), custom_call_target="tpu_custom_call" | custom-call | tf_op jit(solution)/shard_map/forward/pallas_call | solution.py:63
  38.7 15.0 %all-to-all-start = ((bf16[8,48,2048]{2,1,0:T(8,128)(2,1)}), bf16[8,48,2048]{2,1,0:T(8,128)(2,1)S(1)}, u32[]{:S(2)}, u32[]{:S(2)}) async-start(bf16[8,48,2048]{2,1,0:T(8,128)(2,1)} %bitcast.17), calls=%async_computation | async-start | bytes 3145728 | tf_op jit(solution)/shard_map/all_to_all | solution.py:645
  55.7 24.2 %collective-permute-done.7.refs_0_ = bf16[512,1024]{1,0:T(8,128)(2,1)} collective-permute-done((bf16[512,1024]{1,0:T(8,128)(2,1)S(1)}, bf16[512,1024]{1,0:T(8,128)(2,1)}, u32[]{:S(2)}, u32[]{:S(2)}) %collective-permute-start.7) | collective-permute-done | bytes 1048608 | tf_op jit(solution)/shard_map/ppermute | solution.py:658
  79.9 10.0 %all-to-all-done = bf16[8,48,2048]{2,1,0:T(8,128)(2,1)S(1)} async-done(((bf16[8,48,2048]{2,1,0:T(8,128)(2,1)}), bf16[8,48,2048]{2,1,0:T(8,128)(2,1)S(1)}, u32[]{:S(2)}, u32[]{:S(2)}) %all-to-all-start) | async-done | bytes 1572896 | tf_op jit(solution)/shard_map/all_to_all | solution.py:645
  89.9 3.2 %mix.1 = (bf16[48,2048]{1,0:T(8,128)(2,1)S(1)}, bf16[48,2048]{1,0:T(8,128)(2,1)S(1)}, bf16[48,2048]{1,0:T(8,128)(2,1)S(1)}, bf16[48,2048]{1,0:T(8,128)(2,1)S(1)}...) custom-call(bf16[384,2048]{1,0:T(8,128)(2,1)S(1)} %bitcast.14, ...), custom_call_target="tpu_custom_call" | custom-call | tf_op jit(solution)/shard_map/mix/pallas_call | solution.py:63
  96.0 3.1 %collective-permute-start.13 = (bf16[48,2048]{1,0:T(8,128)(2,1)S(1)}, bf16[48,2048]{1,0:T(8,128)(2,1)S(1)}, u32[]{:S(2)}, u32[]{:S(2)}) collective-permute-start(bf16[48,2048]{1,0:T(8,128)(2,1)S(1)} %get-tuple-element.110), channel_id=1, source_target_pairs={{0,4},{1,5},{2,6},{3,7},{4,0},{5,1},{6,2},{7,3},{8,12},{9,13},{10,... | collective-permute-start | bytes 589832 | tf_op jit(solution)/shard_map/ppermute | solution.py:650
  100.7 7.7 %backward_local.1 = (f32[128,2048]{1,0:T(8,128)}, bf16[2048,768]{1,0:T(8,128)(2,1)S(1)}, bf16[2048,768]{1,0:T(8,128)(2,1)S(1)}, bf16[768,2048]{1,0:T(8,128)(2,1)...) custom-call(s32[2]{0:T(128)S(1)} %pad_add_fusion.ids_ref, ...), custom_call_target="tpu_custom_call" | custom-call | flops 20000000000 | tf_op jit(solution)/shard_map/backward_local/pallas_call | solution.py:63
  108.5 9.2 %collective-permute-start.10 = (bf16[48,2048]{1,0:T(8,128)(2,1)S(1)}, bf16[48,2048]{1,0:T(8,128)(2,1)S(1)}, u32[]{:S(2)}, u32[]{:S(2)}) collective-permute-start(bf16[48,2048]{1,0:T(8,128)(2,1)S(1)} %get-tuple-element.107), channel_id=1, source_target_pairs={{0,1},{1,2},{2,3},{3,4},{4,5},{5,6},{6,7},{7,0},{8,9},{9,10},{10,1... | collective-permute-start | bytes 589832 | tf_op jit(solution)/shard_map/ppermute | solution.py:650
  117.8 3.0 %collective-permute-done.13.refs_4_ = bf16[48,2048]{1,0:T(8,128)(2,1)S(1)} collective-permute-done((bf16[48,2048]{1,0:T(8,128)(2,1)S(1)}, bf16[48,2048]{1,0:T(8,128)(2,1)S(1)}, u32[]{:S(2)}, u32[]{:S(2)}) %collective-permute-start.13) | collective-permute-done | bytes 196640 | tf_op jit(solution)/shard_map/ppermute | solution.py:650
  122.3 2.6 %collective-permute-done.10.refs_1_ = bf16[48,2048]{1,0:T(8,128)(2,1)S(1)} collective-permute-done((bf16[48,2048]{1,0:T(8,128)(2,1)S(1)}, bf16[48,2048]{1,0:T(8,128)(2,1)S(1)}, u32[]{:S(2)}, u32[]{:S(2)}) %collective-permute-start.10) | collective-permute-done | bytes 196640 | tf_op jit(solution)/shard_map/ppermute | solution.py:650
  127.9 5.8 %backward.1 = (bf16[384,2048]{1,0:T(8,128)(2,1)}, bf16[384,768]{1,0:T(8,128)(2,1)}, bf16[384,768]{1,0:T(8,128)(2,1)}, bf16[384,2048]{1,0:T(8,128)(2,1)}) custom-call(s32[2]{0:T(128)S(1)} %pad_add_fusion.ids_ref, bf16[48,2048]{1,0:T(8,128)(2,1)S(1)} %get-tuple-element.114.refs_0_, bf16[48,2048]{1,0:T(8,128)(2,1)S(1)} %collective-permute-done.10.refs_1_, ...), custom_call_target="tpu_custom_call" | custom-call | flops 20000000000 | tf_op jit(solution)/shard_map/backward/pallas_call | solution.py:63
  137.6 8.0 %all-to-all-start.1 = ((bf16[8,48,2048]{2,1,0:T(8,128)(2,1)}), bf16[8,48,2048]{2,1,0:T(8,128)(2,1)S(1)}, u32[]{:S(2)}, u32[]{:S(2)}) async-start(bf16[8,48,2048]{2,1,0:T(8,128)(2,1)} %bitcast.16), calls=%async_computation.1 | async-start | bytes 3145728 | tf_op jit(solution)/shard_map/all_to_all | solution.py:645
  145.9 8.1 %collective-permute-done.17.refs_6_ = bf16[384,1024]{1,0:T(8,128)(2,1)} collective-permute-done((bf16[384,1024]{1,0:T(8,128)(2,1)}, bf16[384,1024]{1,0:T(8,128)(2,1)}, u32[]{:S(2)}, u32[]{:S(2)}) %collective-permute-start.17) | collective-permute-done | bytes 786464 | tf_op jit(solution)/shard_map/ppermute | solution.py:658
  157.7 7.8 %weight_sums.3.refs_10_ = f32[512,2304]{1,0:T(8,128)} custom-call(s32[2]{0:T(128)S(1)} %pad_add_fusion.ids_ref, bf16[512,2048]{1,0:T(8,128)(2,1)} %get-tuple-element.133.refs_0_, bf16[384,768]{1,0:T(8,128)(2,1)} %get-tuple-element.132.refs_1_, bf16[128,2560]{1,0:T(8,128)(2,1)} %copy-done, bf16[512,2048]{1,0:T(8,128)(2,1)} %collective-permute-done.19.refs_3_, ...), custom_call_target="tpu_custom_call" | custom-call | flops 4499999744 | tf_op jit(solution)/shard_map/weight_sums/pallas_call | solution.py:63
  165.5 4.3 %collective-permute-done.18.refs_1_ = bf16[384,768]{1,0:T(8,128)(2,1)S(1)} collective-permute-done((bf16[384,768]{1,0:T(8,128)(2,1)S(1)}, bf16[384,768]{1,0:T(8,128)(2,1)S(1)}, u32[]{:S(2)}, u32[]{:S(2)}) %collective-permute-start.18) | collective-permute-done | bytes 589856 | tf_op jit(solution)/shard_map/ppermute | solution.py:658
  173.7 7.1 %weight_sums.4.refs_6_ = f32[512,2304]{1,0:T(8,128)} custom-call(s32[2]{0:T(128)S(1)} %pad_add_fusion.ids_ref, bf16[512,1024]{1,0:T(8,128)(2,1)} %collective-permute-done.7.refs_0_, bf16[384,768]{1,0:T(8,128)(2,1)} %copy-done.9, bf16[128,2560]{1,0:T(8,128)(2,1)} %copy-done.2, bf16[512,1024]{1,0:T(8,128)(2,1)} %copy-done.1, ...), custom_call_target="tpu_custom_call", output_to_operand_aliasing={{}: (11, {})} | custom-call | flops 4499999744 | tf_op jit(solution)/shard_map/weight_sums/pallas_call | solution.py:63
  183.2 2.5 %combine.1 = bf16[128,2048]{1,0:T(8,128)(2,1)} custom-call(bf16[384,2048]{1,0:T(8,128)(2,1)S(1)} %bitcast.13, bf16[256,384]{1,0:T(8,128)(2,1)} %get-tuple-element.91.refs_0_.pick_hbm, f32[128,2048]{1,0:T(8,128)} %get-tuple-element.144.local_hbm), custom_call_target="tpu_custom_call" | custom-call | tf_op jit(solution)/shard_map/combine/pallas_call | solution.py:63
  187.9 4.7 %weight_sums.5 = f32[512,2304]{1,0:T(8,128)} custom-call(s32[2]{0:T(128)S(1)} %pad_add_fusion.ids_ref, bf16[512,1024]{1,0:T(8,128)(2,1)} %collective-permute-done.7.refs_0_, bf16[384,768]{1,0:T(8,128)(2,1)} %copy-done.11, bf16[128,2560]{1,0:T(8,128)(2,1)} %copy-done.2, bf16[512,1024]{1,0:T(8,128)(2,1)} %copy-done.1, ...), custom_call_target="tpu_custom_call", output_to_operand_aliasing={{}: (7, {})} | custom-call | tf_op jit(solution)/shard_map/weight_sums/pallas_call | solution.py:63
  (84 shorter events, 36.9 us)
Async XLA Ops:
  7.6 23.4 %collective-permute-start.2 = (bf16[48,2048]{1,0:T(8,128)(2,1)S(1)}, bf16[48,2048]{1,0:T(8,128)(2,1)S(1)}, u32[]{:S(2)}, u32[]{:S(2)}) collective-permute-start(bf16[48,2048]{1,0:T(8,128)(2,1)S(1)} %get-tuple-element.78), channel_id=1, source_target_pairs={{0,3},{1,4},{2,5},{3,6},{4,7},{5,0},{6,1},{7,2},{8,11},{9,12},{10,... | collective-permute-start | bytes 589832 | tf_op jit(solution)/shard_map/ppermute | solution.py:650
  10.1 21.1 %collective-permute-start.3 = (bf16[48,2048]{1,0:T(8,128)(2,1)S(1)}, bf16[48,2048]{1,0:T(8,128)(2,1)S(1)}, u32[]{:S(2)}, u32[]{:S(2)}) collective-permute-start(bf16[48,2048]{1,0:T(8,128)(2,1)S(1)} %get-tuple-element.79), channel_id=1, source_target_pairs={{0,4},{1,5},{2,6},{3,7},{4,0},{5,1},{6,2},{7,3},{8,12},{9,13},{10,... | collective-permute-start | bytes 589832 | tf_op jit(solution)/shard_map/ppermute | solution.py:650
  11.3 19.8 %collective-permute-start.4 = (bf16[48,2048]{1,0:T(8,128)(2,1)S(1)}, bf16[48,2048]{1,0:T(8,128)(2,1)S(1)}, u32[]{:S(2)}, u32[]{:S(2)}) collective-permute-start(bf16[48,2048]{1,0:T(8,128)(2,1)S(1)} %get-tuple-element.80), channel_id=1, source_target_pairs={{0,5},{1,6},{2,7},{3,0},{4,1},{5,2},{6,3},{7,4},{8,13},{9,14},{10,... | collective-permute-start | bytes 589832 | tf_op jit(solution)/shard_map/ppermute | solution.py:650
  15.0 16.2 %collective-permute-start.5 = (bf16[48,2048]{1,0:T(8,128)(2,1)S(1)}, bf16[48,2048]{1,0:T(8,128)(2,1)S(1)}, u32[]{:S(2)}, u32[]{:S(2)}) collective-permute-start(bf16[48,2048]{1,0:T(8,128)(2,1)S(1)} %get-tuple-element.81), channel_id=1, source_target_pairs={{0,6},{1,7},{2,0},{3,1},{4,2},{5,3},{6,4},{7,5},{8,14},{9,15},{10,... | collective-permute-start | bytes 589832 | tf_op jit(solution)/shard_map/ppermute | solution.py:650
  16.8 15.8 %collective-permute-start.6 = (bf16[48,2048]{1,0:T(8,128)(2,1)S(1)}, bf16[48,2048]{1,0:T(8,128)(2,1)S(1)}, u32[]{:S(2)}, u32[]{:S(2)}) collective-permute-start(bf16[48,2048]{1,0:T(8,128)(2,1)S(1)} %get-tuple-element.82), channel_id=1, source_target_pairs={{0,7},{1,0},{2,1},{3,2},{4,3},{5,4},{6,5},{7,6},{8,15},{9,8},{10,9... | collective-permute-start | bytes 589832 | tf_op jit(solution)/shard_map/ppermute | solution.py:650
  38.7 51.2 %all-to-all-start = ((bf16[8,48,2048]{2,1,0:T(8,128)(2,1)}), bf16[8,48,2048]{2,1,0:T(8,128)(2,1)S(1)}, u32[]{:S(2)}, u32[]{:S(2)}) async-start(bf16[8,48,2048]{2,1,0:T(8,128)(2,1)} %bitcast.17), calls=%async_computation | async-start | bytes 3145728 | tf_op jit(solution)/shard_map/all_to_all | solution.py:645
  53.7 26.2 %collective-permute-start.7 = (bf16[512,1024]{1,0:T(8,128)(2,1)S(1)}, bf16[512,1024]{1,0:T(8,128)(2,1)}, u32[]{:S(2)}, u32[]{:S(2)}) collective-permute-start(bf16[512,1024]{1,0:T(8,128)(2,1)S(1)} %get-tuple-element.89), channel_id=1, source_target_pairs={{0,16},{8,24},{16,0},{24,8},{1,17},{9,25},{17,1},{25,9},{2,18},{10... | collective-permute-start | bytes 3145736 | tf_op jit(solution)/shard_map/ppermute | solution.py:658
  55.2 43.8 %collective-permute-start.8 = (bf16[512,768]{1,0:T(8,128)(2,1)}, bf16[512,768]{1,0:T(8,128)(2,1)S(1)}, u32[]{:S(2)}, u32[]{:S(2)}) collective-permute-start(bf16[512,768]{1,0:T(8,128)(2,1)} %get-tuple-element.96.refs_9_), channel_id=1, source_target_pairs={{0,16},{8,24},{16,0},{24,8},{1,17},{9,25},{17,1},{25,9},{2,18},{10... | collective-permute-start | bytes 2359304 | tf_op jit(solution)/shard_map/ppermute | solution.py:658
  95.4 22.3 %collective-permute-start.11 = (bf16[48,2048]{1,0:T(8,128)(2,1)S(1)}, bf16[48,2048]{1,0:T(8,128)(2,1)S(1)}, u32[]{:S(2)}, u32[]{:S(2)}) collective-permute-start(bf16[48,2048]{1,0:T(8,128)(2,1)S(1)} %get-tuple-element.108), channel_id=1, source_target_pairs={{0,2},{1,3},{2,4},{3,5},{4,6},{5,7},{6,0},{7,1},{8,10},{9,11},{10,... | collective-permute-start | bytes 589832 | tf_op jit(solution)/shard_map/ppermute | solution.py:650
  96.0 21.8 %collective-permute-start.12 = (bf16[48,2048]{1,0:T(8,128)(2,1)S(1)}, bf16[48,2048]{1,0:T(8,128)(2,1)S(1)}, u32[]{:S(2)}, u32[]{:S(2)}) collective-permute-start(bf16[48,2048]{1,0:T(8,128)(2,1)S(1)} %get-tuple-element.109), channel_id=1, source_target_pairs={{0,3},{1,4},{2,5},{3,6},{4,7},{5,0},{6,1},{7,2},{8,11},{9,12},{10,... | collective-permute-start | bytes 589832 | tf_op jit(solution)/shard_map/ppermute | solution.py:650
  96.0 24.8 %collective-permute-start.13 = (bf16[48,2048]{1,0:T(8,128)(2,1)S(1)}, bf16[48,2048]{1,0:T(8,128)(2,1)S(1)}, u32[]{:S(2)}, u32[]{:S(2)}) collective-permute-start(bf16[48,2048]{1,0:T(8,128)(2,1)S(1)} %get-tuple-element.110), channel_id=1, source_target_pairs={{0,4},{1,5},{2,6},{3,7},{4,0},{5,1},{6,2},{7,3},{8,12},{9,13},{10,... | collective-permute-start | bytes 589832 | tf_op jit(solution)/shard_map/ppermute | solution.py:650
  99.0 23.3 %collective-permute-start.14 = (bf16[48,2048]{1,0:T(8,128)(2,1)S(1)}, bf16[48,2048]{1,0:T(8,128)(2,1)S(1)}, u32[]{:S(2)}, u32[]{:S(2)}) collective-permute-start(bf16[48,2048]{1,0:T(8,128)(2,1)S(1)} %get-tuple-element.111), channel_id=1, source_target_pairs={{0,5},{1,6},{2,7},{3,0},{4,1},{5,2},{6,3},{7,4},{8,13},{9,14},{10,... | collective-permute-start | bytes 589832 | tf_op jit(solution)/shard_map/ppermute | solution.py:650
  108.5 16.4 %collective-permute-start.10 = (bf16[48,2048]{1,0:T(8,128)(2,1)S(1)}, bf16[48,2048]{1,0:T(8,128)(2,1)S(1)}, u32[]{:S(2)}, u32[]{:S(2)}) collective-permute-start(bf16[48,2048]{1,0:T(8,128)(2,1)S(1)} %get-tuple-element.107), channel_id=1, source_target_pairs={{0,1},{1,2},{2,3},{3,4},{4,5},{5,6},{6,7},{7,0},{8,9},{9,10},{10,1... | collective-permute-start | bytes 589832 | tf_op jit(solution)/shard_map/ppermute | solution.py:650
  117.7 36.8 %collective-permute-start.19 = (bf16[512,2048]{1,0:T(8,128)(2,1)}, bf16[512,2048]{1,0:T(8,128)(2,1)}, u32[]{:S(2)}, u32[]{:S(2)}) collective-permute-start(bf16[512,2048]{1,0:T(8,128)(2,1)} %get-tuple-element.133.refs_0_), channel_id=1, source_target_pairs={{0,8},{8,0},{16,24},{24,16},{1,9},{9,1},{17,25},{25,17},{2,10},{10... | collective-permute-start | bytes 6291464 | tf_op jit(solution)/shard_map/ppermute | solution.py:671
  120.8 15.3 %collective-permute-start.16 = (bf16[128,2560]{1,0:T(8,128)(2,1)S(1)}, bf16[128,2560]{1,0:T(8,128)(2,1)S(1)}, u32[]{:S(2)}, u32[]{:S(2)}) collective-permute-start(bf16[128,2560]{1,0:T(8,128)(2,1)S(1)} %get-tuple-element.130), channel_id=1, source_target_pairs={{0,16},{8,24},{16,0},{24,8},{1,17},{9,25},{17,1},{25,9},{2,18},{10... | collective-permute-start | bytes 1966088 | tf_op jit(solution)/shard_map/ppermute | solution.py:658
  133.6 22.9 %collective-permute-start.23 = (bf16[384,2048]{1,0:T(8,128)(2,1)}, bf16[384,2048]{1,0:T(8,128)(2,1)}, u32[]{:S(2)}, u32[]{:S(2)}) collective-permute-start(bf16[384,2048]{1,0:T(8,128)(2,1)} %get-tuple-element.135.refs_8_), channel_id=1, source_target_pairs={{0,8},{8,0},{16,24},{24,16},{1,9},{9,1},{17,25},{25,17},{2,10},{10... | collective-permute-start | bytes 4718600 | tf_op jit(solution)/shard_map/ppermute | solution.py:671
  136.1 17.9 %collective-permute-start.17 = (bf16[384,1024]{1,0:T(8,128)(2,1)}, bf16[384,1024]{1,0:T(8,128)(2,1)}, u32[]{:S(2)}, u32[]{:S(2)}) collective-permute-start(bf16[384,1024]{1,0:T(8,128)(2,1)} %cut.1), channel_id=1, source_target_pairs={{0,16},{8,24},{16,0},{24,8},{1,17},{9,25},{17,1},{25,9},{2,18},{10... | collective-permute-start | bytes 2359304 | tf_op jit(solution)/shard_map/ppermute | solution.py:658
  137.6 16.4 %collective-permute-start.24 = (bf16[512,768]{1,0:T(8,128)(2,1)}, bf16[512,768]{1,0:T(8,128)(2,1)}, u32[]{:S(2)}, u32[]{:S(2)}) collective-permute-start(bf16[512,768]{1,0:T(8,128)(2,1)} %get-tuple-element.96.refs_9_), channel_id=1, source_target_pairs={{0,8},{8,0},{16,24},{24,16},{1,9},{9,1},{17,25},{25,17},{2,10},{10... | collective-permute-start | bytes 2359304 | tf_op jit(solution)/shard_map/ppermute | solution.py:671
  137.6 45.7 %all-to-all-start.1 = ((bf16[8,48,2048]{2,1,0:T(8,128)(2,1)}), bf16[8,48,2048]{2,1,0:T(8,128)(2,1)S(1)}, u32[]{:S(2)}, u32[]{:S(2)}) async-start(bf16[8,48,2048]{2,1,0:T(8,128)(2,1)} %bitcast.16), calls=%async_computation.1 | async-start | bytes 3145728 | tf_op jit(solution)/shard_map/all_to_all | solution.py:645
  154.5 15.3 %collective-permute-start.18 = (bf16[384,768]{1,0:T(8,128)(2,1)S(1)}, bf16[384,768]{1,0:T(8,128)(2,1)S(1)}, u32[]{:S(2)}, u32[]{:S(2)}) collective-permute-start(bf16[384,768]{1,0:T(8,128)(2,1)S(1)} %copy-done.8), channel_id=1, source_target_pairs={{0,16},{8,24},{16,0},{24,8},{1,17},{9,25},{17,1},{25,9},{2,18},{10... | collective-permute-start | bytes 1769480 | tf_op jit(solution)/shard_map/ppermute | solution.py:658
  156.0 15.4 %collective-permute-start.26 = (bf16[512,1024]{1,0:T(8,128)(2,1)}, bf16[512,1024]{1,0:T(8,128)(2,1)S(1)}, u32[]{:S(2)}, u32[]{:S(2)}) collective-permute-start(bf16[512,1024]{1,0:T(8,128)(2,1)} %collective-permute-done.7.refs_0_), channel_id=1, source_target_pairs={{0,8},{8,0},{16,24},{24,16},{1,9},{9,1},{17,25},{25,17},{2,10},{10... | collective-permute-start | bytes 3145736 | tf_op jit(solution)/shard_map/ppermute | solution.py:671
  156.5 14.9 %collective-permute-start.28 = (bf16[128,2560]{1,0:T(8,128)(2,1)S(1)}, bf16[128,2560]{1,0:T(8,128)(2,1)S(1)}, u32[]{:S(2)}, u32[]{:S(2)}) collective-permute-start(bf16[128,2560]{1,0:T(8,128)(2,1)S(1)} %collective-permute-done.16.refs_2_), channel_id=1, source_target_pairs={{0,8},{8,0},{16,24},{24,16},{1,9},{9,1},{17,25},{25,17},{2,10},{10... | collective-permute-start | bytes 1966088 | tf_op jit(solution)/shard_map/ppermute | solution.py:671
  156.8 14.6 %collective-permute-start.29 = (bf16[384,1024]{1,0:T(8,128)(2,1)}, bf16[384,1024]{1,0:T(8,128)(2,1)S(1)}, u32[]{:S(2)}, u32[]{:S(2)}) collective-permute-start(bf16[384,1024]{1,0:T(8,128)(2,1)} %collective-permute-done.17.refs_6_), channel_id=1, source_target_pairs={{0,8},{8,0},{16,24},{24,16},{1,9},{9,1},{17,25},{25,17},{2,10},{10... | collective-permute-start | bytes 2359304 | tf_op jit(solution)/shard_map/ppermute | solution.py:671
  169.8 16.0 %collective-permute-start.25 = (bf16[384,768]{1,0:T(8,128)(2,1)}, bf16[384,768]{1,0:T(8,128)(2,1)S(1)}, u32[]{:S(2)}, u32[]{:S(2)}) collective-permute-start(bf16[384,768]{1,0:T(8,128)(2,1)} %get-tuple-element.136.refs_6_), channel_id=1, source_target_pairs={{0,16},{8,24},{16,0},{24,8},{1,17},{9,25},{17,1},{25,9},{2,18},{10... | collective-permute-start | bytes 1769480 | tf_op jit(solution)/shard_map/ppermute | solution.py:658
  (24 other events, 181.7 us)

commit v7 on v6

--- a/solution.py
+++ b/solution.py
@@ -539,24 +539,30 @@
                 row += count
             return started
 
-        arriving = []
-        for (left, right, _, wide), left_ref, right_ref in zip(terms, lefts, rights):
-            arriving += bring(left, left_ref, part) + bring(right, right_ref, wide * units)
+        arriving = [
+            bring(left, left_ref, part) + bring(right, right_ref, wide * units)
+            for (left, right, _, wide), left_ref, right_ref in zip(terms, lefts, rights)
+        ]
+        started = {}
         for source in begun_hbm:
             for section in sections:
                 cols = pl.ds(section * units, units)
-                arriving.append(copies.start(source.at[:, cols], out_ref.at[:, cols]))
-        for copy in arriving:
-            copy.wait()
+                started[section] = copies.start(source.at[:, cols], out_ref.at[:, cols])
         for section in sections:
             for at in range(0, units, step):
                 cols = pl.ds(section * units + at, step)
-                total = out_ref[:, cols] if begun else None
+                total = None
                 for i, (_, _, first, wide) in enumerate(terms):
                     if first <= section < first + wide:
                         begin = (section - first) * units + at
+                        while arriving[i]:
+                            arriving[i].pop().wait()
                         term = dot_rows(lefts[i][...], rights[i][:, begin : begin + step])
                         total = term if total is None else total + term
+                if begun:
+                    if at == 0:
+                        started[section].wait()
+                    total = out_ref[:, cols] if total is None else total + out_ref[:, cols]
                 out_ref[:, cols] = total if scale is None else total * scale
                 copies.start(out_ref.at[:, cols], out_hbm.at[:, cols], True)
         copies.finish()

time: 195 us -> 195 us (level)
  no operation moved by 1% of the time
where the time goes in v7:
time: 195 us; the launch traced here: 192 us
  waiting for transfers between devices  70.4 us (36%)
  starting transfers between devices  65 us (33%)
  Pallas kernels  53.4 us (27%)
  local copies, waits for them, and re-layouts  2.54 us (1%)
    pallas_call x11, Pallas kernels, call(): pl.pallas_call(kernel, out_shape=tuple(outs), in_specs=specs, out_specs=t...  53.4 us
    ppermute x6, waiting for transfers between devices, to_chips(): lax.ppermute(array, 'dp', [(start * cores + i, (start + shift) % chips *...  39.9 us
    ppermute x14, starting transfers between devices, steps(): lax.ppermute(blocks[k], 'expert', [(i, (i + k) % groups) for i in range(g...  32.2 us
    all_to_all x2, starting transfers between devices, at_once(): lax.all_to_all(block, 'expert', split_axis=0, concat_axis=0, tiled=True)  23 us
    ppermute x14, waiting for transfers between devices, steps(): lax.ppermute(blocks[k], 'expert', [(i, (i + k) % groups) for i in range(g...  15.5 us
    all_to_all x2, waiting for transfers between devices, at_once(): lax.all_to_all(block, 'expert', split_axis=0, concat_axis=0, tiled=True)  12.3 us
    ppermute x6, starting transfers between devices, to_chips(): lax.ppermute(array, 'dp', [(start * cores + i, (start + shift) % chips *...  8.06 us
  transfers between devices with their start and end apart: 34, of which 17 were waited for; matrix products, arithmetic and copies ran while one was open for 0% of the time, Pallas kernels for 21%

profile of v7, /device:TPU:0, one launch (start us, length us, event | category | flops | bytes accessed | tf_op | source)
XLA Modules:
  0.0 192.5 jit_solution(804026767159858633)
XLA Ops:
  3.0 3.0 %collective-permute-start = (bf16[48,2048]{1,0:T(8,128)(2,1)S(1)}, bf16[48,2048]{1,0:T(8,128)(2,1)S(1)}, u32[]{:S(2)}, u32[]{:S(2)}) collective-permute-start(bf16[48,2048]{1,0:T(8,128)(2,1)S(1)} %get-tuple-element.76), channel_id=1, source_target_pairs={{0,1},{1,2},{2,3},{3,4},{4,5},{5,6},{6,7},{7,0},{8,9},{9,10},{10,1... | collective-permute-start | bytes 589832 | tf_op jit(solution)/shard_map/ppermute | solution.py:656
  7.6 2.5 %collective-permute-start.2 = (bf16[48,2048]{1,0:T(8,128)(2,1)S(1)}, bf16[48,2048]{1,0:T(8,128)(2,1)S(1)}, u32[]{:S(2)}, u32[]{:S(2)}) collective-permute-start(bf16[48,2048]{1,0:T(8,128)(2,1)S(1)} %get-tuple-element.78), channel_id=1, source_target_pairs={{0,3},{1,4},{2,5},{3,6},{4,7},{5,0},{6,1},{7,2},{8,11},{9,12},{10,... | collective-permute-start | bytes 589832 | tf_op jit(solution)/shard_map/ppermute | solution.py:656
  11.3 2.6 %collective-permute-start.4 = (bf16[48,2048]{1,0:T(8,128)(2,1)S(1)}, bf16[48,2048]{1,0:T(8,128)(2,1)S(1)}, u32[]{:S(2)}, u32[]{:S(2)}) collective-permute-start(bf16[48,2048]{1,0:T(8,128)(2,1)S(1)} %get-tuple-element.80), channel_id=1, source_target_pairs={{0,5},{1,6},{2,7},{3,0},{4,1},{5,2},{6,3},{7,4},{8,13},{9,14},{10,... | collective-permute-start | bytes 589832 | tf_op jit(solution)/shard_map/ppermute | solution.py:656
  16.8 3.4 %collective-permute-start.6 = (bf16[48,2048]{1,0:T(8,128)(2,1)S(1)}, bf16[48,2048]{1,0:T(8,128)(2,1)S(1)}, u32[]{:S(2)}, u32[]{:S(2)}) collective-permute-start(bf16[48,2048]{1,0:T(8,128)(2,1)S(1)} %get-tuple-element.82), channel_id=1, source_target_pairs={{0,7},{1,0},{2,1},{3,2},{4,3},{5,4},{6,5},{7,6},{8,15},{9,8},{10,9... | collective-permute-start | bytes 589832 | tf_op jit(solution)/shard_map/ppermute | solution.py:656
  20.2 5.7 %forward_local.1 = (f32[128,2048]{1,0:T(8,128)}, f32[128,768]{1,0:T(8,128)}, f32[128,768]{1,0:T(8,128)}, bf16[128,768]{1,0:T(8,128)(2,1)S(1)}, bf16[128,2048]{1,...) custom-call(bf16[128,2048]{1,0:T(8,128)(2,1)} %tokens_hbm.3, ...), custom_call_target="tpu_custom_call" | custom-call | flops 20000000000 | tf_op jit(solution)/shard_map/forward_local/pallas_call | solution.py:63
  26.0 5.0 %collective-permute-done.2.refs_3_ = bf16[48,2048]{1,0:T(8,128)(2,1)S(1)} collective-permute-done((bf16[48,2048]{1,0:T(8,128)(2,1)S(1)}, bf16[48,2048]{1,0:T(8,128)(2,1)S(1)}, u32[]{:S(2)}, u32[]{:S(2)}) %collective-permute-start.2) | collective-permute-done | bytes 196640 | tf_op jit(solution)/shard_map/ppermute | solution.py:656
  32.6 6.1 %forward.1 = (bf16[384,2048]{1,0:T(8,128)(2,1)}, bf16[512,2048]{1,0:T(8,128)(2,1)}, bf16[512,768]{1,0:T(8,128)(2,1)}, f32[384,768]{1,0:T(8,128)}, f32[384,768]{1,0:T(8,128)}, /*index=5*/bf16[512,1024]{1,0:T(8,128)(2,1)S(1)}) custom-call(s32[2]{0:T(128)S(1)} %pad_add_fusion.ids_ref, bf16[48,2048]{1,0:T(8,128)(2,1)S(1)} %get-tuple-element.75.refs_0_, ...), custom_call_target="tpu_custom_call" | custom-call | tf_op jit(solution)/shard_map/forward/pallas_call | solution.py:63
  38.7 15.0 %all-to-all-start = ((bf16[8,48,2048]{2,1,0:T(8,128)(2,1)}), bf16[8,48,2048]{2,1,0:T(8,128)(2,1)S(1)}, u32[]{:S(2)}, u32[]{:S(2)}) async-start(bf16[8,48,2048]{2,1,0:T(8,128)(2,1)} %bitcast.17), calls=%async_computation | async-start | bytes 3145728 | tf_op jit(solution)/shard_map/all_to_all | solution.py:651
  55.7 24.2 %collective-permute-done.7.refs_0_ = bf16[512,1024]{1,0:T(8,128)(2,1)} collective-permute-done((bf16[512,1024]{1,0:T(8,128)(2,1)S(1)}, bf16[512,1024]{1,0:T(8,128)(2,1)}, u32[]{:S(2)}, u32[]{:S(2)}) %collective-permute-start.7) | collective-permute-done | bytes 1048608 | tf_op jit(solution)/shard_map/ppermute | solution.py:664
  79.9 10.0 %all-to-all-done = bf16[8,48,2048]{2,1,0:T(8,128)(2,1)S(1)} async-done(((bf16[8,48,2048]{2,1,0:T(8,128)(2,1)}), bf16[8,48,2048]{2,1,0:T(8,128)(2,1)S(1)}, u32[]{:S(2)}, u32[]{:S(2)}) %all-to-all-start) | async-done | bytes 1572896 | tf_op jit(solution)/shard_map/all_to_all | solution.py:651
  89.9 3.2 %mix.1 = (bf16[48,2048]{1,0:T(8,128)(2,1)S(1)}, bf16[48,2048]{1,0:T(8,128)(2,1)S(1)}, bf16[48,2048]{1,0:T(8,128)(2,1)S(1)}, bf16[48,2048]{1,0:T(8,128)(2,1)S(1)}...) custom-call(bf16[384,2048]{1,0:T(8,128)(2,1)S(1)} %bitcast.14, ...), custom_call_target="tpu_custom_call" | custom-call | tf_op jit(solution)/shard_map/mix/pallas_call | solution.py:63
  96.0 3.1 %collective-permute-start.13 = (bf16[48,2048]{1,0:T(8,128)(2,1)S(1)}, bf16[48,2048]{1,0:T(8,128)(2,1)S(1)}, u32[]{:S(2)}, u32[]{:S(2)}) collective-permute-start(bf16[48,2048]{1,0:T(8,128)(2,1)S(1)} %get-tuple-element.110), channel_id=1, source_target_pairs={{0,4},{1,5},{2,6},{3,7},{4,0},{5,1},{6,2},{7,3},{8,12},{9,13},{10,... | collective-permute-start | bytes 589832 | tf_op jit(solution)/shard_map/ppermute | solution.py:656
  100.7 7.7 %backward_local.1 = (f32[128,2048]{1,0:T(8,128)}, bf16[2048,768]{1,0:T(8,128)(2,1)S(1)}, bf16[2048,768]{1,0:T(8,128)(2,1)S(1)}, bf16[768,2048]{1,0:T(8,128)(2,1)...) custom-call(s32[2]{0:T(128)S(1)} %pad_add_fusion.ids_ref, ...), custom_call_target="tpu_custom_call" | custom-call | flops 20000000000 | tf_op jit(solution)/shard_map/backward_local/pallas_call | solution.py:63
  108.5 9.2 %collective-permute-start.10 = (bf16[48,2048]{1,0:T(8,128)(2,1)S(1)}, bf16[48,2048]{1,0:T(8,128)(2,1)S(1)}, u32[]{:S(2)}, u32[]{:S(2)}) collective-permute-start(bf16[48,2048]{1,0:T(8,128)(2,1)S(1)} %get-tuple-element.107), channel_id=1, source_target_pairs={{0,1},{1,2},{2,3},{3,4},{4,5},{5,6},{6,7},{7,0},{8,9},{9,10},{10,1... | collective-permute-start | bytes 589832 | tf_op jit(solution)/shard_map/ppermute | solution.py:656
  117.8 3.0 %collective-permute-done.13.refs_4_ = bf16[48,2048]{1,0:T(8,128)(2,1)S(1)} collective-permute-done((bf16[48,2048]{1,0:T(8,128)(2,1)S(1)}, bf16[48,2048]{1,0:T(8,128)(2,1)S(1)}, u32[]{:S(2)}, u32[]{:S(2)}) %collective-permute-start.13) | collective-permute-done | bytes 196640 | tf_op jit(solution)/shard_map/ppermute | solution.py:656
  122.3 2.6 %collective-permute-done.10.refs_1_ = bf16[48,2048]{1,0:T(8,128)(2,1)S(1)} collective-permute-done((bf16[48,2048]{1,0:T(8,128)(2,1)S(1)}, bf16[48,2048]{1,0:T(8,128)(2,1)S(1)}, u32[]{:S(2)}, u32[]{:S(2)}) %collective-permute-start.10) | collective-permute-done | bytes 196640 | tf_op jit(solution)/shard_map/ppermute | solution.py:656
  127.9 5.8 %backward.1 = (bf16[384,2048]{1,0:T(8,128)(2,1)}, bf16[384,768]{1,0:T(8,128)(2,1)}, bf16[384,768]{1,0:T(8,128)(2,1)}, bf16[384,2048]{1,0:T(8,128)(2,1)}) custom-call(s32[2]{0:T(128)S(1)} %pad_add_fusion.ids_ref, bf16[48,2048]{1,0:T(8,128)(2,1)S(1)} %get-tuple-element.114.refs_0_, bf16[48,2048]{1,0:T(8,128)(2,1)S(1)} %collective-permute-done.10.refs_1_, ...), custom_call_target="tpu_custom_call" | custom-call | flops 20000000000 | tf_op jit(solution)/shard_map/backward/pallas_call | solution.py:63
  137.6 8.0 %all-to-all-start.1 = ((bf16[8,48,2048]{2,1,0:T(8,128)(2,1)}), bf16[8,48,2048]{2,1,0:T(8,128)(2,1)S(1)}, u32[]{:S(2)}, u32[]{:S(2)}) async-start(bf16[8,48,2048]{2,1,0:T(8,128)(2,1)} %bitcast.16), calls=%async_computation.1 | async-start | bytes 3145728 | tf_op jit(solution)/shard_map/all_to_all | solution.py:651
  145.9 8.1 %collective-permute-done.17.refs_6_ = bf16[384,1024]{1,0:T(8,128)(2,1)} collective-permute-done((bf16[384,1024]{1,0:T(8,128)(2,1)}, bf16[384,1024]{1,0:T(8,128)(2,1)}, u32[]{:S(2)}, u32[]{:S(2)}) %collective-permute-start.17) | collective-permute-done | bytes 786464 | tf_op jit(solution)/shard_map/ppermute | solution.py:664
  157.7 6.9 %weight_sums.3.refs_10_ = f32[512,2304]{1,0:T(8,128)} custom-call(s32[2]{0:T(128)S(1)} %pad_add_fusion.ids_ref, bf16[512,2048]{1,0:T(8,128)(2,1)} %get-tuple-element.133.refs_0_, bf16[384,768]{1,0:T(8,128)(2,1)} %get-tuple-element.132.refs_1_, bf16[128,2560]{1,0:T(8,128)(2,1)} %copy-done, bf16[512,2048]{1,0:T(8,128)(2,1)} %collective-permute-done.19.refs_3_, ...), custom_call_target="tpu_custom_call" | custom-call | flops 4499999744 | tf_op jit(solution)/shard_map/weight_sums/pallas_call | solution.py:63
  164.6 5.2 %collective-permute-done.18.refs_1_ = bf16[384,768]{1,0:T(8,128)(2,1)S(1)} collective-permute-done((bf16[384,768]{1,0:T(8,128)(2,1)S(1)}, bf16[384,768]{1,0:T(8,128)(2,1)S(1)}, u32[]{:S(2)}, u32[]{:S(2)}) %collective-permute-start.18) | collective-permute-done | bytes 589856 | tf_op jit(solution)/shard_map/ppermute | solution.py:664
  173.7 7.2 %weight_sums.4.refs_6_ = f32[512,2304]{1,0:T(8,128)} custom-call(s32[2]{0:T(128)S(1)} %pad_add_fusion.ids_ref, bf16[512,1024]{1,0:T(8,128)(2,1)} %collective-permute-done.7.refs_0_, bf16[384,768]{1,0:T(8,128)(2,1)} %copy-done.9, bf16[128,2560]{1,0:T(8,128)(2,1)} %copy-done.2, bf16[512,1024]{1,0:T(8,128)(2,1)} %copy-done.1, ...), custom_call_target="tpu_custom_call", output_to_operand_aliasing={{}: (11, {})} | custom-call | flops 4499999744 | tf_op jit(solution)/shard_map/weight_sums/pallas_call | solution.py:63
  183.2 2.5 %combine.1 = bf16[128,2048]{1,0:T(8,128)(2,1)} custom-call(bf16[384,2048]{1,0:T(8,128)(2,1)S(1)} %bitcast.13, bf16[256,384]{1,0:T(8,128)(2,1)} %get-tuple-element.91.refs_0_.pick_hbm, f32[128,2048]{1,0:T(8,128)} %get-tuple-element.144.local_hbm), custom_call_target="tpu_custom_call" | custom-call | tf_op jit(solution)/shard_map/combine/pallas_call | solution.py:63
  187.9 4.4 %weight_sums.5 = f32[512,2304]{1,0:T(8,128)} custom-call(s32[2]{0:T(128)S(1)} %pad_add_fusion.ids_ref, bf16[512,1024]{1,0:T(8,128)(2,1)} %collective-permute-done.7.refs_0_, bf16[384,768]{1,0:T(8,128)(2,1)} %copy-done.11, bf16[128,2560]{1,0:T(8,128)(2,1)} %copy-done.2, bf16[512,1024]{1,0:T(8,128)(2,1)} %copy-done.1, ...), custom_call_target="tpu_custom_call", output_to_operand_aliasing={{}: (7, {})} | custom-call | tf_op jit(solution)/shard_map/weight_sums/pallas_call | solution.py:63
  (84 shorter events, 36.8 us)
Async XLA Ops:
  7.6 23.4 %collective-permute-start.2 = (bf16[48,2048]{1,0:T(8,128)(2,1)S(1)}, bf16[48,2048]{1,0:T(8,128)(2,1)S(1)}, u32[]{:S(2)}, u32[]{:S(2)}) collective-permute-start(bf16[48,2048]{1,0:T(8,128)(2,1)S(1)} %get-tuple-element.78), channel_id=1, source_target_pairs={{0,3},{1,4},{2,5},{3,6},{4,7},{5,0},{6,1},{7,2},{8,11},{9,12},{10,... | collective-permute-start | bytes 589832 | tf_op jit(solution)/shard_map/ppermute | solution.py:656
  10.1 21.1 %collective-permute-start.3 = (bf16[48,2048]{1,0:T(8,128)(2,1)S(1)}, bf16[48,2048]{1,0:T(8,128)(2,1)S(1)}, u32[]{:S(2)}, u32[]{:S(2)}) collective-permute-start(bf16[48,2048]{1,0:T(8,128)(2,1)S(1)} %get-tuple-element.79), channel_id=1, source_target_pairs={{0,4},{1,5},{2,6},{3,7},{4,0},{5,1},{6,2},{7,3},{8,12},{9,13},{10,... | collective-permute-start | bytes 589832 | tf_op jit(solution)/shard_map/ppermute | solution.py:656
  11.3 19.8 %collective-permute-start.4 = (bf16[48,2048]{1,0:T(8,128)(2,1)S(1)}, bf16[48,2048]{1,0:T(8,128)(2,1)S(1)}, u32[]{:S(2)}, u32[]{:S(2)}) collective-permute-start(bf16[48,2048]{1,0:T(8,128)(2,1)S(1)} %get-tuple-element.80), channel_id=1, source_target_pairs={{0,5},{1,6},{2,7},{3,0},{4,1},{5,2},{6,3},{7,4},{8,13},{9,14},{10,... | collective-permute-start | bytes 589832 | tf_op jit(solution)/shard_map/ppermute | solution.py:656
  15.0 16.2 %collective-permute-start.5 = (bf16[48,2048]{1,0:T(8,128)(2,1)S(1)}, bf16[48,2048]{1,0:T(8,128)(2,1)S(1)}, u32[]{:S(2)}, u32[]{:S(2)}) collective-permute-start(bf16[48,2048]{1,0:T(8,128)(2,1)S(1)} %get-tuple-element.81), channel_id=1, source_target_pairs={{0,6},{1,7},{2,0},{3,1},{4,2},{5,3},{6,4},{7,5},{8,14},{9,15},{10,... | collective-permute-start | bytes 589832 | tf_op jit(solution)/shard_map/ppermute | solution.py:656
  16.8 15.8 %collective-permute-start.6 = (bf16[48,2048]{1,0:T(8,128)(2,1)S(1)}, bf16[48,2048]{1,0:T(8,128)(2,1)S(1)}, u32[]{:S(2)}, u32[]{:S(2)}) collective-permute-start(bf16[48,2048]{1,0:T(8,128)(2,1)S(1)} %get-tuple-element.82), channel_id=1, source_target_pairs={{0,7},{1,0},{2,1},{3,2},{4,3},{5,4},{6,5},{7,6},{8,15},{9,8},{10,9... | collective-permute-start | bytes 589832 | tf_op jit(solution)/shard_map/ppermute | solution.py:656
  38.7 51.2 %all-to-all-start = ((bf16[8,48,2048]{2,1,0:T(8,128)(2,1)}), bf16[8,48,2048]{2,1,0:T(8,128)(2,1)S(1)}, u32[]{:S(2)}, u32[]{:S(2)}) async-start(bf16[8,48,2048]{2,1,0:T(8,128)(2,1)} %bitcast.17), calls=%async_computation | async-start | bytes 3145728 | tf_op jit(solution)/shard_map/all_to_all | solution.py:651
  53.7 26.2 %collective-permute-start.7 = (bf16[512,1024]{1,0:T(8,128)(2,1)S(1)}, bf16[512,1024]{1,0:T(8,128)(2,1)}, u32[]{:S(2)}, u32[]{:S(2)}) collective-permute-start(bf16[512,1024]{1,0:T(8,128)(2,1)S(1)} %get-tuple-element.89), channel_id=1, source_target_pairs={{0,16},{8,24},{16,0},{24,8},{1,17},{9,25},{17,1},{25,9},{2,18},{10... | collective-permute-start | bytes 3145736 | tf_op jit(solution)/shard_map/ppermute | solution.py:664
  55.2 43.8 %collective-permute-start.8 = (bf16[512,768]{1,0:T(8,128)(2,1)}, bf16[512,768]{1,0:T(8,128)(2,1)S(1)}, u32[]{:S(2)}, u32[]{:S(2)}) collective-permute-start(bf16[512,768]{1,0:T(8,128)(2,1)} %get-tuple-element.96.refs_9_), channel_id=1, source_target_pairs={{0,16},{8,24},{16,0},{24,8},{1,17},{9,25},{17,1},{25,9},{2,18},{10... | collective-permute-start | bytes 2359304 | tf_op jit(solution)/shard_map/ppermute | solution.py:664
  95.4 22.3 %collective-permute-start.11 = (bf16[48,2048]{1,0:T(8,128)(2,1)S(1)}, bf16[48,2048]{1,0:T(8,128)(2,1)S(1)}, u32[]{:S(2)}, u32[]{:S(2)}) collective-permute-start(bf16[48,2048]{1,0:T(8,128)(2,1)S(1)} %get-tuple-element.108), channel_id=1, source_target_pairs={{0,2},{1,3},{2,4},{3,5},{4,6},{5,7},{6,0},{7,1},{8,10},{9,11},{10,... | collective-permute-start | bytes 589832 | tf_op jit(solution)/shard_map/ppermute | solution.py:656
  96.0 21.8 %collective-permute-start.12 = (bf16[48,2048]{1,0:T(8,128)(2,1)S(1)}, bf16[48,2048]{1,0:T(8,128)(2,1)S(1)}, u32[]{:S(2)}, u32[]{:S(2)}) collective-permute-start(bf16[48,2048]{1,0:T(8,128)(2,1)S(1)} %get-tuple-element.109), channel_id=1, source_target_pairs={{0,3},{1,4},{2,5},{3,6},{4,7},{5,0},{6,1},{7,2},{8,11},{9,12},{10,... | collective-permute-start | bytes 589832 | tf_op jit(solution)/shard_map/ppermute | solution.py:656
  96.0 24.8 %collective-permute-start.13 = (bf16[48,2048]{1,0:T(8,128)(2,1)S(1)}, bf16[48,2048]{1,0:T(8,128)(2,1)S(1)}, u32[]{:S(2)}, u32[]{:S(2)}) collective-permute-start(bf16[48,2048]{1,0:T(8,128)(2,1)S(1)} %get-tuple-element.110), channel_id=1, source_target_pairs={{0,4},{1,5},{2,6},{3,7},{4,0},{5,1},{6,2},{7,3},{8,12},{9,13},{10,... | collective-permute-start | bytes 589832 | tf_op jit(solution)/shard_map/ppermute | solution.py:656
  99.0 23.3 %collective-permute-start.14 = (bf16[48,2048]{1,0:T(8,128)(2,1)S(1)}, bf16[48,2048]{1,0:T(8,128)(2,1)S(1)}, u32[]{:S(2)}, u32[]{:S(2)}) collective-permute-start(bf16[48,2048]{1,0:T(8,128)(2,1)S(1)} %get-tuple-element.111), channel_id=1, source_target_pairs={{0,5},{1,6},{2,7},{3,0},{4,1},{5,2},{6,3},{7,4},{8,13},{9,14},{10,... | collective-permute-start | bytes 589832 | tf_op jit(solution)/shard_map/ppermute | solution.py:656
  108.5 16.4 %collective-permute-start.10 = (bf16[48,2048]{1,0:T(8,128)(2,1)S(1)}, bf16[48,2048]{1,0:T(8,128)(2,1)S(1)}, u32[]{:S(2)}, u32[]{:S(2)}) collective-permute-start(bf16[48,2048]{1,0:T(8,128)(2,1)S(1)} %get-tuple-element.107), channel_id=1, source_target_pairs={{0,1},{1,2},{2,3},{3,4},{4,5},{5,6},{6,7},{7,0},{8,9},{9,10},{10,1... | collective-permute-start | bytes 589832 | tf_op jit(solution)/shard_map/ppermute | solution.py:656
  117.7 36.8 %collective-permute-start.19 = (bf16[512,2048]{1,0:T(8,128)(2,1)}, bf16[512,2048]{1,0:T(8,128)(2,1)}, u32[]{:S(2)}, u32[]{:S(2)}) collective-permute-start(bf16[512,2048]{1,0:T(8,128)(2,1)} %get-tuple-element.133.refs_0_), channel_id=1, source_target_pairs={{0,8},{8,0},{16,24},{24,16},{1,9},{9,1},{17,25},{25,17},{2,10},{10... | collective-permute-start | bytes 6291464 | tf_op jit(solution)/shard_map/ppermute | solution.py:677
  120.8 15.3 %collective-permute-start.16 = (bf16[128,2560]{1,0:T(8,128)(2,1)S(1)}, bf16[128,2560]{1,0:T(8,128)(2,1)S(1)}, u32[]{:S(2)}, u32[]{:S(2)}) collective-permute-start(bf16[128,2560]{1,0:T(8,128)(2,1)S(1)} %get-tuple-element.130), channel_id=1, source_target_pairs={{0,16},{8,24},{16,0},{24,8},{1,17},{9,25},{17,1},{25,9},{2,18},{10... | collective-permute-start | bytes 1966088 | tf_op jit(solution)/shard_map/ppermute | solution.py:664
  133.6 22.9 %collective-permute-start.23 = (bf16[384,2048]{1,0:T(8,128)(2,1)}, bf16[384,2048]{1,0:T(8,128)(2,1)}, u32[]{:S(2)}, u32[]{:S(2)}) collective-permute-start(bf16[384,2048]{1,0:T(8,128)(2,1)} %get-tuple-element.135.refs_8_), channel_id=1, source_target_pairs={{0,8},{8,0},{16,24},{24,16},{1,9},{9,1},{17,25},{25,17},{2,10},{10... | collective-permute-start | bytes 4718600 | tf_op jit(solution)/shard_map/ppermute | solution.py:677
  136.1 17.9 %collective-permute-start.17 = (bf16[384,1024]{1,0:T(8,128)(2,1)}, bf16[384,1024]{1,0:T(8,128)(2,1)}, u32[]{:S(2)}, u32[]{:S(2)}) collective-permute-start(bf16[384,1024]{1,0:T(8,128)(2,1)} %cut.1), channel_id=1, source_target_pairs={{0,16},{8,24},{16,0},{24,8},{1,17},{9,25},{17,1},{25,9},{2,18},{10... | collective-permute-start | bytes 2359304 | tf_op jit(solution)/shard_map/ppermute | solution.py:664
  137.6 16.4 %collective-permute-start.24 = (bf16[512,768]{1,0:T(8,128)(2,1)}, bf16[512,768]{1,0:T(8,128)(2,1)}, u32[]{:S(2)}, u32[]{:S(2)}) collective-permute-start(bf16[512,768]{1,0:T(8,128)(2,1)} %get-tuple-element.96.refs_9_), channel_id=1, source_target_pairs={{0,8},{8,0},{16,24},{24,16},{1,9},{9,1},{17,25},{25,17},{2,10},{10... | collective-permute-start | bytes 2359304 | tf_op jit(solution)/shard_map/ppermute | solution.py:677
  137.6 45.7 %all-to-all-start.1 = ((bf16[8,48,2048]{2,1,0:T(8,128)(2,1)}), bf16[8,48,2048]{2,1,0:T(8,128)(2,1)S(1)}, u32[]{:S(2)}, u32[]{:S(2)}) async-start(bf16[8,48,2048]{2,1,0:T(8,128)(2,1)} %bitcast.16), calls=%async_computation.1 | async-start | bytes 3145728 | tf_op jit(solution)/shard_map/all_to_all | solution.py:651
  154.5 15.3 %collective-permute-start.18 = (bf16[384,768]{1,0:T(8,128)(2,1)S(1)}, bf16[384,768]{1,0:T(8,128)(2,1)S(1)}, u32[]{:S(2)}, u32[]{:S(2)}) collective-permute-start(bf16[384,768]{1,0:T(8,128)(2,1)S(1)} %copy-done.8), channel_id=1, source_target_pairs={{0,16},{8,24},{16,0},{24,8},{1,17},{9,25},{17,1},{25,9},{2,18},{10... | collective-permute-start | bytes 1769480 | tf_op jit(solution)/shard_map/ppermute | solution.py:664
  156.0 15.4 %collective-permute-start.26 = (bf16[512,1024]{1,0:T(8,128)(2,1)}, bf16[512,1024]{1,0:T(8,128)(2,1)S(1)}, u32[]{:S(2)}, u32[]{:S(2)}) collective-permute-start(bf16[512,1024]{1,0:T(8,128)(2,1)} %collective-permute-done.7.refs_0_), channel_id=1, source_target_pairs={{0,8},{8,0},{16,24},{24,16},{1,9},{9,1},{17,25},{25,17},{2,10},{10... | collective-permute-start | bytes 3145736 | tf_op jit(solution)/shard_map/ppermute | solution.py:677
  156.5 14.9 %collective-permute-start.28 = (bf16[128,2560]{1,0:T(8,128)(2,1)S(1)}, bf16[128,2560]{1,0:T(8,128)(2,1)S(1)}, u32[]{:S(2)}, u32[]{:S(2)}) collective-permute-start(bf16[128,2560]{1,0:T(8,128)(2,1)S(1)} %collective-permute-done.16.refs_2_), channel_id=1, source_target_pairs={{0,8},{8,0},{16,24},{24,16},{1,9},{9,1},{17,25},{25,17},{2,10},{10... | collective-permute-start | bytes 1966088 | tf_op jit(solution)/shard_map/ppermute | solution.py:677
  156.8 14.6 %collective-permute-start.29 = (bf16[384,1024]{1,0:T(8,128)(2,1)}, bf16[384,1024]{1,0:T(8,128)(2,1)S(1)}, u32[]{:S(2)}, u32[]{:S(2)}) collective-permute-start(bf16[384,1024]{1,0:T(8,128)(2,1)} %collective-permute-done.17.refs_6_), channel_id=1, source_target_pairs={{0,8},{8,0},{16,24},{24,16},{1,9},{9,1},{17,25},{25,17},{2,10},{10... | collective-permute-start | bytes 2359304 | tf_op jit(solution)/shard_map/ppermute | solution.py:677
  169.8 16.0 %collective-permute-start.25 = (bf16[384,768]{1,0:T(8,128)(2,1)}, bf16[384,768]{1,0:T(8,128)(2,1)S(1)}, u32[]{:S(2)}, u32[]{:S(2)}) collective-permute-start(bf16[384,768]{1,0:T(8,128)(2,1)} %get-tuple-element.136.refs_6_), channel_id=1, source_target_pairs={{0,16},{8,24},{16,0},{24,8},{1,17},{9,25},{17,1},{25,9},{2,18},{10... | collective-permute-start | bytes 1769480 | tf_op jit(solution)/shard_map/ppermute | solution.py:664
  (24 other events, 180.8 us)
